TPU v7x, 32 devices: a whole 2x2x4 slice. The times are simulated.
32 devices in a mesh: dp: 1, ctx: 32 (over z, y, x, core), tp: 1.
Axes of the slice: x: 2, y: 2, z: 4, core: 2. Of those that a mesh axis runs over, the one named last changes fastest.
Arguments:
- queries: bfloat16 [1, 8192, 2048], P('dp', 'ctx', 'tp'), may hold values from -6 to 6
- key_rows: bfloat16 [1, 8192, 2048], P('dp', 'ctx', 'tp'), may hold values from -0.5390625 to 0.5390625
- value_rows: bfloat16 [1, 8192, 2048], P('dp', 'ctx', 'tp'), may hold values from -6 to 6
- out_grad: bfloat16 [1, 8192, 2048], P('dp', 'ctx', 'tp'), may hold values from -24 to 24
- norm_gain: float32 [16, 128], P('tp'), may hold values from 0.1 to 1.9
- doc_ids: int32 [1, 64], P('dp', 'ctx'), may hold values from 0 to 3, never falling along the last dimension, each value on 1 to 32 neighbouring positions
Outputs:
- query_grad: bfloat16 [1, 8192, 2048], P('dp', 'ctx', 'tp')
- key_grad: bfloat16 [1, 8192, 2048], P('dp', 'ctx', 'tp')
- value_grad: bfloat16 [1, 8192, 2048], P('dp', 'ctx', 'tp')
- gain_grad: float32 [16, 128], P('tp', 'dp')
Inputs may be any that keep to these rules, and one draw needn't show every extreme that they name: `doc_ids`: ids never fall along a sequence; each id covers at most 32 consecutive blocks.
All inputs are finite; a program needn't handle non-finite values.
Results may differ from a plain program's by a relative error of at most 0.0062.
Values sent between devices are 32-bit elements; how exact they have to be, the bound alone decides.
No kernel may reach another device: no remote copies, remote signals or barrier semaphores. Data moves between devices by JAX's collectives and lax.ppermute only.
A program may use at most 128 MiB of HBM per device.

v0:
```python
import jax
import jax.numpy as jnp
from jax import lax
from jax.sharding import PartitionSpec as P

STRETCH = 256
BLK = 128


EPSILON = 1e-06


def prefix(value, axis, join, neutral, backward):
    count, mine = (lax.axis_size(axis), lax.axis_index(axis))
    pieces = jax.tree.map(lambda part: lax.all_gather(part, axis), value)
    if backward:
        pieces = jax.tree.map(lambda part: part[::-1], pieces)
        mine = count - 1 - mine
    running = jax.tree.map(
        lambda part, zero: jnp.full_like(part, 0) + jnp.asarray(zero, part.dtype), value, neutral
    )

    def step(position, running):
        longer = join(running, jax.tree.map(lambda part: part[position], pieces))
        return jax.tree.map(lambda new, old: jnp.where(position < mine, new, old), longer, running)

    return lax.fori_loop(0, count - 1, step, running)


def merge_pair(former, latter):
    latter_empty = latter[1] < 0.0
    matches = (latter[1] == former[1]).astype(jnp.float32)
    joined = latter[0] + matches * former[0]
    return (
        jnp.where(latter_empty, former[0], joined),
        jnp.where(latter_empty, former[1], latter[1]),
    )


def causal_mask(docs):
    length = docs.shape[-1]
    positions = jnp.arange(length)
    lower = positions[:, None] >= positions[None, :]
    return lower[None] & (docs[:, :, None] == docs[:, None, :])


def forward_chain(own_state, empty):
    return prefix(own_state, "ctx", merge_pair, empty, False)


def backward_chain(own_back, empty):
    return prefix(own_back, "ctx", merge_pair, empty, True)


def heads_pass(queries, key_rows, value_rows, out_grad, norm_gain, docs):
    stretches = queries.shape[0]
    heads = queries.shape[2]
    width = queries.shape[3]
    empty = (jnp.zeros((heads, width, width), jnp.float32), jnp.float32(-1.0))
    last_ids = docs[:, -1]
    last_weight = (docs == last_ids[:, None]).astype(jnp.bfloat16)
    elements = jnp.einsum(
        "nshd,nshe->nhde",
        key_rows * last_weight[:, :, None, None],
        value_rows,
        preferred_element_type=jnp.float32,
    )
    own_state = (elements[0], last_ids[0])
    carried = forward_chain(own_state, empty)
    incoming = [carried[0]]
    prior_ids = [carried[1]]
    states_in = jnp.stack(incoming).astype(jnp.bfloat16)
    ids_in = jnp.stack(prior_ids)
    mask = causal_mask(docs)[:, None]
    enter_weight = (docs == ids_in[:, None]).astype(jnp.bfloat16)[:, :, None, None]
    inter = jnp.einsum(
        "nthd,nhde->nthe", queries * enter_weight, states_in, preferred_element_type=jnp.float32
    )
    scores = jnp.einsum("nthd,nshd->nhts", queries, key_rows, preferred_element_type=jnp.float32)
    scores = jnp.where(mask, scores, 0.0).astype(jnp.bfloat16)
    attended = inter + jnp.einsum(
        "nhts,nshe->nthe", scores, value_rows, preferred_element_type=jnp.float32
    )
    inv_rms = lax.rsqrt(jnp.mean(attended * attended, -1, keepdims=True) + EPSILON)
    grad_full = out_grad.astype(jnp.float32)
    scaled = grad_full * norm_gain
    gain_term = jnp.sum(grad_full * attended * inv_rms, axis=(0, 1))
    attn_grad = inv_rms * scaled - inv_rms**3 * attended * jnp.mean(
        scaled * attended, -1, keepdims=True
    )
    attn_grad = attn_grad.astype(jnp.bfloat16)
    first_ids = docs[:, 0]
    first_weight = (docs == first_ids[:, None]).astype(jnp.bfloat16)
    backs = jnp.einsum(
        "nthd,nthe->nhde",
        queries * first_weight[:, :, None, None],
        attn_grad,
        preferred_element_type=jnp.float32,
    )
    own_back = (backs[stretches - 1], first_ids[stretches - 1])
    carried = backward_chain(own_back, empty)
    outgoing = [None] * stretches
    next_ids = [None] * stretches
    outgoing[0] = carried[0]
    next_ids[0] = carried[1]
    states_out = jnp.stack(outgoing).astype(jnp.bfloat16)
    ids_out = jnp.stack(next_ids)
    leave_weight = (docs == ids_out[:, None]).astype(jnp.bfloat16)[:, :, None, None]
    pair_grad = jnp.einsum(
        "nthe,nshe->nhts", attn_grad, value_rows, preferred_element_type=jnp.float32
    )
    pair_grad = jnp.where(mask, pair_grad, 0.0).astype(jnp.bfloat16)
    query_grad = jnp.einsum(
        "nthe,nhde->nthd", attn_grad * enter_weight, states_in, preferred_element_type=jnp.float32
    )
    query_grad = query_grad + jnp.einsum(
        "nhts,nshd->nthd", pair_grad, key_rows, preferred_element_type=jnp.float32
    )
    key_grad = jnp.einsum("nhts,nthd->nshd", pair_grad, queries, preferred_element_type=jnp.float32)
    key_grad = key_grad + jnp.einsum(
        "nshe,nhde->nshd", value_rows * leave_weight, states_out, preferred_element_type=jnp.float32
    )
    value_grad = jnp.einsum(
        "nhts,nthe->nshe", scores, attn_grad, preferred_element_type=jnp.float32
    )
    value_grad = value_grad + jnp.einsum(
        "nshd,nhde->nshe", key_rows * leave_weight, states_out, preferred_element_type=jnp.float32
    )
    return (
        query_grad.astype(jnp.bfloat16),
        key_grad.astype(jnp.bfloat16),
        value_grad.astype(jnp.bfloat16),
        gain_term,
    )


def local(queries, key_rows, value_rows, out_grad, norm_gain, doc_ids):
    tokens = queries.shape[1]
    heads = norm_gain.shape[0]
    width = norm_gain.shape[1]
    stretches = tokens // STRETCH
    stretch_shape = (stretches, STRETCH, heads, width)
    docs = jnp.repeat(doc_ids[0], BLK).astype(jnp.float32).reshape(stretches, STRETCH)
    arrays = [array.reshape(stretch_shape) for array in (queries, key_rows, value_rows, out_grad)]
    pieces = [array for array in arrays]
    results = [heads_pass(pieces[0], pieces[1], pieces[2], pieces[3], norm_gain, docs)]
    flat_shape = (1, tokens, heads * width)
    query_grad = jnp.concatenate([result[0] for result in results], 2).reshape(flat_shape)
    key_grad = jnp.concatenate([result[1] for result in results], 2).reshape(flat_shape)
    value_grad = jnp.concatenate([result[2] for result in results], 2).reshape(flat_shape)
    gain_term = jnp.concatenate([result[3] for result in results], 0)
    whole = lax.psum(gain_term, "ctx")
    gain_grad = lax.psum_scatter(whole, "dp", scatter_dimension=1, tiled=True)
    return (query_grad, key_grad, value_grad, gain_grad)


def solution(mesh):
    in_specs = (
        P("dp", "ctx", "tp"),
        P("dp", "ctx", "tp"),
        P("dp", "ctx", "tp"),
        P("dp", "ctx", "tp"),
        P("tp", None),
        P("dp", "ctx"),
    )
    out_specs = (P("dp", "ctx", "tp"), P("dp", "ctx", "tp"), P("dp", "ctx", "tp"), P("tp", "dp"))
    return jax.shard_map(local, mesh=mesh, in_specs=in_specs, out_specs=out_specs, check_vma=False)
```

profile of v0, /device:TPU:1, one launch (start us, length us, event | category | flops | bytes accessed | tf_op | source)
XLA Modules:
  0.0 731.0 jit_solution(1686602883841603519)
XLA Ops:
  15.1 42.9 %all-reduce = f32[32]{0:T(128)S(1)} all-reduce(f32[32]{0:T(128)S(1)} %bitcast_dynamic-update-slice_fusion.1), channel_id=2, replica_groups=mesh['dp'=1,'ctx'=32,'tp'=1] {'ctx'}, use_global_device_ids=true, to_apply=%add | all-reduce | flops 32 | bytes 256 | tf_op jit(solution)/shard_map/all_gather | solution.py:15
  60.8 2.5 copy.43
  63.4 3.7 select_convert_fusion.1
  67.1 145.8 %all-gather.7.cloned.1.call-done = f32[512,128,128]{2,1,0:T(8,128)} async-done(((f32[16,128,128]{2,1,0:T(8,128)}), f32[512,128,128]{2,1,0:T(8,128)}) %all-gather.7.cloned.1.call-update) | async-done | bytes 33554448 | tf_op jit(solution)/shard_map/all_gather | solution.py:15
  212.9 138.7 %while.32 = (s32[]{:T(128)}, f32[16,128,128]{2,1,0:T(8,128)S(1)}, f32[]{:T(128)}, s32[]{:T(128)}, f32[32]{0:T(128)S(1)}, /*index=5*/f32[32,16,128,128]{3,2,1,0:T(8,128)}, s32[]{:T(128)}, s32[]{:T(128)}, f32[]{:T(128)}) while((s32[]{:T(128)}, f32[16,128,128]{2,1,0:T(8,128)S(1)}, f32[]{:T(128)}, s32[]{:T(128)}, f32[32]{0:T(128)S(1)}, ...), condition=%wide.region_1.2_spmd.clone, body=%wide.region_0.1_spmd.clone.sunk | while | flops 1310729 | bytes 3145911 | solution.py:27
  214.8 1.9 select_select_fusion.4
  223.7 1.9 select_select_fusion.4
  232.7 1.9 select_select_fusion.4
  241.6 1.9 select_select_fusion.4
  246.1 1.9 select_select_fusion.4
  250.6 1.9 select_select_fusion.4
  255.0 1.9 select_select_fusion.4
  259.5 1.9 select_select_fusion.4
  264.0 1.9 select_select_fusion.4
  268.5 1.9 select_select_fusion.4
  272.9 1.9 select_select_fusion.4
  277.4 1.9 select_select_fusion.4
  281.9 1.9 select_select_fusion.4
  286.4 1.9 select_select_fusion.4
  290.8 1.9 select_select_fusion.4
  299.8 1.9 select_select_fusion.4
  308.7 1.9 select_select_fusion.4
  317.7 1.9 select_select_fusion.4
  326.6 1.9 select_select_fusion.4
  331.1 1.9 select_select_fusion.4
  335.6 1.9 select_select_fusion.4
  340.0 1.9 select_select_fusion.4
  344.5 1.9 select_select_fusion.4
  349.0 1.9 select_select_fusion.4
  352.3 1.9 fusion.21
  359.9 39.9 %all-reduce.2 = (f32[32]{0:T(128)S(1)}, f32[16,128]{1,0:T(8,128)}) all-reduce(f32[32]{0:T(128)S(1)} %bitcast_dynamic-update-slice_fusion, f32[16,128]{1,0:T(8,128)S(1)} %get-tuple-element.278), channel_id=4, replica_groups=mesh['dp'=1,'ctx'=32,'tp'=1] {'ctx'}, use_global_device_ids=true, to_apply=%add.1 | all-reduce | flops 2080 | bytes 16640
  404.9 2.4 copy.49
  407.3 3.4 fusion.9
  410.6 143.0 %all-gather.9.cloned.1.call-done = f32[512,128,128]{2,1,0:T(8,128)} async-done(((f32[16,128,128]{2,1,0:T(8,128)}), f32[512,128,128]{2,1,0:T(8,128)}) %all-gather.9.cloned.1.call-update) | async-done | bytes 33554448 | tf_op jit(solution)/shard_map/all_gather | solution.py:15
  553.6 23.0 %rev.7 = f32[32,16,128,128]{3,2,1,0:T(8,128)} reverse(f32[32,16,128,128]{3,2,1,0:T(8,128)} %bitcast.116), dimensions={0} | reverse | bytes 67108864 | tf_op jit(solution)/shard_map/rev | solution.py:17
  576.6 138.7 %while.33 = (s32[]{:T(128)}, f32[16,128,128]{2,1,0:T(8,128)S(1)}, f32[]{:T(128)}, s32[]{:T(128)}, f32[32]{0:T(128)S(1)}, /*index=5*/f32[32,16,128,128]{3,2,1,0:T(8,128)}, s32[]{:T(128)}, s32[]{:T(128)}, f32[]{:T(128)}) while((s32[]{:T(128)}, f32[16,128,128]{2,1,0:T(8,128)S(1)}, f32[]{:T(128)}, s32[]{:T(128)}, f32[32]{0:T(128)S(1)}, ...), condition=%wide.region_5.6_spmd.clone, body=%wide.region_4.5_spmd.clone.sunk | while | flops 1310729 | bytes 3145911 | solution.py:27
  578.5 1.9 select_select_fusion.5
  583.0 1.9 select_select_fusion.5
  591.9 1.9 select_select_fusion.5
  596.4 1.9 select_select_fusion.5
  600.9 1.9 select_select_fusion.5
  605.3 1.9 select_select_fusion.5
  614.3 1.9 select_select_fusion.5
  618.8 1.9 select_select_fusion.5
  623.2 1.9 select_select_fusion.5
  627.7 1.9 select_select_fusion.5
  715.4 1.9 fusion.17
  720.1 2.7 fusion
  (163 shorter events, 116.2 us)
Async XLA Ops:
  7.2 205.7 %all-gather.7.cloned.1.call-start = ((), (), s32[]{:S(2)}) async-start(), calls=%async_computation | async-start | bytes 34603008 | tf_op jit(solution)/shard_map/all_gather | solution.py:15
  9.2 2.4 copy-start.15
  10.8 1.1 copy-start.6
  11.6 2.8 copy-start.10
  11.9 1.1 copy-start
  12.9 45.1 %copy-start.16 = (bf16[1,256,2048]{2,1,0:T(8,128)(2,1)S(1)}, bf16[1,256,2048]{2,1,0:T(8,128)(2,1)}, u32[]{:S(2)}) copy-start(bf16[1,256,2048]{2,1,0:T(8,128)(2,1)} %param.10) | copy-start | bytes 3145732
  14.4 539.2 %all-gather.9.cloned.1.call-start = ((), (), s32[]{:S(2)}) async-start(), calls=%async_computation.1 | async-start | bytes 34603008 | tf_op jit(solution)/shard_map/all_gather | solution.py:15
  352.3 1.9 copy-start.1
  352.3 2.2 copy-start.13
  354.5 0.9 copy-start.17
  356.2 1.6 copy-start.8
  356.8 1.0 copy-start.3
  399.9 1.9 copy-start.2
  399.9 2.0 copy-start.4
  401.9 1.2 copy-start.11
  403.1 1.8 copy-start.12
  404.9 2.4 copy-start.5
  715.3 1.9 copy-start.7
  715.3 2.7 copy-start.14
  718.7 1.4 copy-start.9
Sparse Core Ops, SparseCore 0:
  14.5 198.3 all-gather.6
  359.3 194.2 all-gather.8
where the time goes:
time: 736 us; the launch traced here: 731 us
  waiting for transfers between devices  289 us (39%)
  loops' own time  123 us (17%)
  other arithmetic  122 us (17%)
  blocking collectives  82.7 us (11%)
  local copies, waits for them, and re-layouts  78.1 us (11%)
  matrix products  22.4 us (3%)
  between operations  14.3 us (2%)
    all_gather x2, waiting for transfers between devices, prefix(): pieces = jax.tree.map(lambda part: lax.all_gather(part, axis), value)  289 us
    another operation x2, loops' own time, prefix(): return lax.fori_loop(0, count - 1, step, running)  123 us
    select_n x62, other arithmetic, step(): jnp.where(position < mine, new, old)  118 us
    all_gather x1, blocking collectives, prefix(): pieces = jax.tree.map(lambda part: lax.all_gather(part, axis), value)  42.9 us
    unnamed x1, blocking collectives  39.9 us
    dynamic_slice x62, local copies, waits for them, and re-layouts, step(): longer = join(running, jax.tree.map(lambda part: part[position], pieces))  36.3 us
    rev x2, local copies, waits for them, and re-layouts, prefix(): pieces = jax.tree.map(lambda part: part[::-1], pieces)  23.1 us
  transfers between devices with their start and end apart: 2, of which 2 were waited for; matrix products, arithmetic and copies ran while one was open for 3% of the time, Pallas kernels for 0%

commit v1 on v0

v1 whole, which is shorter than its diff:
```python
import functools

import jax
import jax.numpy as jnp
from jax import lax
from jax.experimental import pallas as pl
from jax.experimental.pallas import tpu as pltpu
from jax.sharding import PartitionSpec as P

BLK = 128
EPSILON = 1e-06
CHIPS = 4
GROUP = 2 * CHIPS
IDS = 8
FIRST, LAST = 0, 1
F32, BF16 = jnp.float32, jnp.bfloat16


def dot(left, right, left_dim, right_dim):
    return lax.dot_general(
        left, right, (((left_dim,), (right_dim,)), ((), ())), preferred_element_type=F32
    )


def my_core():
    return lax.axis_index("ctx") % 2


def my_chip():
    return (lax.axis_index("ctx") // 2) % CHIPS


def turned(turn):
    return (0, 1 + my_core(), 2 - my_core(), 3)[turn]


def one_doc(docs):
    return jnp.where(docs[0, 0] == docs[0, 1], 1.0, 0.0)


def column(docs, first_block, dtype):
    rows = lax.broadcasted_iota(jnp.int32, (2 * BLK, 1), 0)
    own = (rows < BLK) if first_block else (rows >= BLK)
    return jnp.where(own, 1.0, one_doc(docs)).astype(dtype)


def lower(table, both):
    rows = lax.broadcasted_iota(jnp.int32, (BLK, BLK), 0)
    cols = lax.broadcasted_iota(jnp.int32, (BLK, BLK), 1)
    keep = rows >= cols
    upper = jnp.where(keep, table[:BLK, :BLK], 0.0).astype(BF16)
    below = (table[BLK:, :BLK] * both).astype(BF16)
    right = jnp.where(keep, table[BLK:, BLK:], 0.0).astype(BF16)
    return upper, jnp.concatenate([below, right], 1)


def higher(table, both):
    rows = lax.broadcasted_iota(jnp.int32, (BLK, BLK), 0)
    cols = lax.broadcasted_iota(jnp.int32, (BLK, BLK), 1)
    keep = rows <= cols
    left = jnp.where(keep, table[:BLK, :BLK], 0.0).astype(BF16)
    above = (table[:BLK, BLK:] * both).astype(BF16)
    below = jnp.where(keep, table[BLK:, BLK:], 0.0).astype(BF16)
    return jnp.concatenate([left, above], 1), below


def times_lower(masked, values):
    upper, below = masked
    return jnp.concatenate([dot(upper, values[:BLK], 1, 0), dot(below, values, 1, 0)], 0)


def times_higher(masked, values):
    above, lower_right = masked
    return jnp.concatenate([dot(above, values, 1, 0), dot(lower_right, values[BLK:], 1, 0)], 0)


def write_ids(docs, out, rows, backward):
    first, last = docs[0, 0].astype(F32), docs[0, 1].astype(F32)
    if backward:
        first, last = -last, -first
    out[pl.ds(rows, IDS), :] = jnp.zeros((IDS, 128), F32)
    out[pl.ds(rows + FIRST, 1), :] = jnp.full((1, 128), first, F32)
    out[pl.ds(rows + LAST, 1), :] = jnp.full((1, 128), last, F32)


def wide(base, head):
    return pl.ds(pl.multiple_of((base + head) * 128, 128), 128)


def element_kernel(docs, key, value, out, *, half, other):
    base = (1 - my_core() if other else my_core()) * half
    weight = column(docs, False, BF16)
    write_ids(docs, out, half * 128, False)
    for head in range(half):
        at = wide(base, head)
        out[pl.ds(head * 128, 128), :] = dot(key[:, at] * weight, value[:, at], 0, 0)


def intra_kernel(docs, query, key, value, grad, own, message, *, half):
    both = one_doc(docs)
    tokens = query.shape[0]
    for other in (True, False):
        base = (1 - my_core() if other else my_core()) * half
        for head in range(half):
            full, cols = wide(base, head), pl.ds(head * 128, 128)
            q = query[:, full]
            scores = lower(dot(q, key[:, full], 1, 1), both)
            part = times_lower(scores, value[:, full])
            if other:
                message[pl.ds(0, tokens), cols] = q.astype(F32)
                message[pl.ds(tokens, tokens), cols] = grad[:, full].astype(F32)
                message[pl.ds(2 * tokens, tokens), cols] = part
            else:
                own[:, cols] = part


def attend(q, g, intra, state, gain, joined):
    inter = dot(q, state, 1, 0)
    attended = intra + jnp.concatenate([inter[:BLK], inter[BLK:] * joined], 0)
    inv_rms = lax.rsqrt(jnp.mean(attended * attended, -1, keepdims=True) + EPSILON)
    scaled = g * gain
    normed = attended * inv_rms
    terms = jnp.sum(g * normed, 0, keepdims=True)
    mean = jnp.mean(scaled * normed, -1, keepdims=True)
    attn = (inv_rms * (scaled - normed * mean)).astype(BF16)
    back = dot(q[:BLK], attn[:BLK], 0, 0) + dot(q[BLK:], attn[BLK:], 0, 0) * joined
    return attn, back, terms


def middle_kernel(
    docs, own, other, c0, c1, c2, c3, query, grad, intra, message, gain,
    up0, up1, up2, up3, back_own, back_other, attn_own, reply, state_own, *, half, size,
):
    rows, tokens, chunk = half * 128, query.shape[0], size // 128
    base = my_core() * half
    is_first = my_core() == 0
    own_first, own_last = row(own, rows, FIRST), row(own, rows, LAST)
    other_first, other_last = row(other, rows, FIRST), row(other, rows, LAST)
    keep_coming, keep_other, send_coming, send_own = spread_weights(
        is_first, own_first, own_last, other_first, other_last
    )
    own_joined, other_joined = match(own_first, own_last), match(other_first, other_last)
    for back, first, last in ((back_own, own_first, own_last), (back_other, other_first, other_last)):
        back[pl.ds(rows, IDS), :] = jnp.zeros((IDS, 128), F32)
        back[pl.ds(rows + FIRST, 1), :] = -last
        back[pl.ds(rows + LAST, 1), :] = -first
    first = jnp.minimum(own_first, other_first)
    last = jnp.maximum(own_last, other_last)
    own_weight, other_weight = match(own_first, first), match(other_first, first)
    ups = (up0, up1, up2, up3)
    for up in ups:
        up[pl.ds(size, 2 * IDS), :] = jnp.zeros((2 * IDS, 128), F32)
        up[pl.ds(size + FIRST, 1), :] = -last
        up[pl.ds(size + LAST, 1), :] = -first
    for turn, chip in enumerate((c0, c1, c2, c3)):
        for step in range(chunk):
            head = lax.bitwise_xor(my_chip(), turned(turn)) * chunk + step
            cols, full = wide(0, head), wide(base, head)
            coming = chip[pl.ds(step * 128, 128), :]
            state = (coming * keep_coming + other[cols, :] * keep_other).astype(BF16)
            state_own[cols, :] = state
            state_other = coming * send_coming + own[cols, :] * send_own
            reply[pl.ds(tokens, 128), cols] = state_other
            weights = gain[pl.ds(base + head, 1), :]
            attn, back, terms = attend(
                query[:, full], grad[:, full].astype(F32), intra[:, cols], state, weights, own_joined
            )
            attn_own[:, cols] = attn
            back_own[cols, :] = back
            attn, back_far, terms_far = attend(
                message[pl.ds(0, tokens), cols].astype(BF16),
                message[pl.ds(tokens, tokens), cols],
                message[pl.ds(2 * tokens, tokens), cols],
                state_other.astype(BF16),
                weights,
                other_joined,
            )
            reply[pl.ds(0, tokens), cols] = attn.astype(F32)
            back_other[cols, :] = back_far
            ups[turn][pl.ds(step * 128, 128), :] = back * own_weight + back_far * other_weight
            for up in ups:
                up[pl.ds(size + IDS + head, 1), :] = terms + terms_far


def within_kernel(docs, query, key, value, *refs, half, other):
    query_grad, key_part, value_part, held, sems = refs[-5:]
    tokens = query.shape[0]
    both = one_doc(docs)
    enter32 = column(docs, True, F32)
    base = (1 - my_core() if other else my_core()) * half
    copies = []
    for head in range(half):
        cols = pl.ds(head * 128, 128)
        full = wide(base, head)
        q, k, v = query[:, full], key[:, full], value[:, full]
        if other:
            a = refs[0][pl.ds(0, tokens), cols].astype(BF16)
            state = refs[0][pl.ds(tokens, 128), cols].astype(BF16)
        else:
            a, state = refs[0][:, cols], refs[1][cols, :]
        pair = lower(dot(a, v, 1, 1), both)
        cross = enter32 * dot(a, state, 1, 1)
        held[:, cols] = (cross + times_lower(pair, k)).astype(BF16)
        key_part[:, cols] = times_higher(higher(dot(v, a, 1, 1), both), q)
        value_part[:, cols] = times_higher(higher(dot(k, q, 1, 1), both), a)
        copies.append(pltpu.make_async_copy(held.at[:, cols], query_grad.at[:, full], sems.at[head]))
        copies[-1].start()
    for copy in copies:
        copy.wait()


def finish_kernel(docs, key, value, key_part, value_part, state, *refs, half, other):
    refs, (key_held, value_held, sems) = refs[:-3], refs[-3:]
    if other:
        refs, gain_grad = refs[:-1], refs[-1]
        for head in range(half):
            gain_grad[pl.ds(my_core() * half + head, 1), :] = refs[0][pl.ds(head, 1), :]
            gain_grad[pl.ds((1 - my_core()) * half + head, 1), :] = state[pl.ds(half * 128 + head, 1), :]
    key_grad, value_grad = refs[-2:]
    leave = column(docs, False, F32)
    base = (1 - my_core() if other else my_core()) * half
    copies = []
    for head in range(half):
        cols = pl.ds(head * 128, 128)
        full = wide(base, head)
        g = state[cols, :].astype(BF16)
        key_held[:, cols] = (key_part[:, cols] + leave * dot(value[:, full], g, 1, 1)).astype(BF16)
        value_held[:, cols] = (value_part[:, cols] + leave * dot(key[:, full], g, 1, 0)).astype(BF16)
        copies.append(pltpu.make_async_copy(key_held.at[:, cols], key_grad.at[:, full], sems.at[0, head]))
        copies.append(pltpu.make_async_copy(value_held.at[:, cols], value_grad.at[:, full], sems.at[1, head]))
        copies[-2].start()
        copies[-1].start()
    for copy in copies:
        copy.wait()


def row(ref, rows, which):
    return ref[pl.ds(rows + which, 1), :]


def match(left, right):
    return jnp.where(left == right, 1.0, 0.0)


def pair_kernel(docs, own, other, *outs, half, size):
    rows = half * 128
    first = jnp.minimum(row(own, rows, FIRST), row(other, rows, FIRST))
    last = jnp.maximum(row(own, rows, LAST), row(other, rows, LAST))
    own_weight = match(row(own, rows, LAST), last)
    other_weight = match(row(other, rows, LAST), last)
    for turn, out in enumerate(outs):
        owner = lax.bitwise_xor(my_chip(), turned(turn))
        part = pl.ds(pl.multiple_of(owner * size, size), size)
        out[pl.ds(0, size), :] = own[part, :] * own_weight + other[part, :] * other_weight
        out[pl.ds(size, IDS), :] = jnp.zeros((IDS, 128), F32)
        out[pl.ds(size + FIRST, 1), :] = first
        out[pl.ds(size + LAST, 1), :] = last


def plane_kernel(docs, c0, c1, c2, c3, out, *gain, size):
    chips = (c0, c1, c2, c3)
    last = functools.reduce(jnp.maximum, [row(c, size, LAST) for c in chips])
    out[pl.ds(0, size), :] = sum(
        c[pl.ds(0, size), :] * match(row(c, size, LAST), last) for c in chips
    )
    out[pl.ds(size, IDS), :] = jnp.zeros((IDS, 128), F32)
    out[pl.ds(size + LAST, 1), :] = last
    if gain:
        gain[0][...] = sum(c[pl.ds(size + IDS, IDS), :] for c in chips)
        out[pl.ds(size + IDS, IDS), :] = gain[0][...]


def chain_kernel(docs, c0, c1, c2, c3, *refs, size, distances, planes):
    chips = (c0, c1, c2, c3)
    backward = distances[0] < 0
    others, outs = refs[: len(distances)], refs[-CHIPS:]
    place = [lax.bitwise_xor(my_chip(), turned(turn)) for turn in range(CHIPS)]
    my_plane = lax.axis_index("ctx") // GROUP
    first = functools.reduce(jnp.minimum, [row(c, size, FIRST) for c in chips])
    coming = jnp.zeros((size, 128), F32)
    for distance, other in zip(distances, others):
        source = my_plane - distance
        inside = (source >= 0) & (source < planes)
        weight = match(row(other, size, LAST), first) * jnp.where(inside, 1.0, 0.0)
        coming = coming + other[pl.ds(0, size), :] * weight
    if backward:
        gain, sums, outs = refs[len(distances)], refs[-1], refs[-1 - CHIPS : -1]
        sums[...] = gain[...] + sum(p[pl.ds(size + IDS, IDS), :] for p in others)
    for turn, out in enumerate(outs):
        mine = row(chips[turn], size, FIRST)
        total = coming * match(mine, first)
        for other in range(CHIPS):
            if other == turn:
                continue
            ahead = place[other] > place[turn] if backward else place[other] < place[turn]
            weight = match(row(chips[other], size, LAST), mine) * jnp.where(ahead, 1.0, 0.0)
            total = total + chips[other][pl.ds(0, size), :] * weight
        out[...] = total


def spread_weights(is_first, own_first, own_last, other_first, other_last):
    ones = jnp.ones((1, 128), F32)
    joins = match(own_first, other_first)
    return (
        jnp.where(is_first, ones, joins),
        jnp.where(is_first, 0.0 * ones, match(other_last, own_first)),
        jnp.where(is_first, joins, ones),
        jnp.where(is_first, match(own_last, other_first), 0.0 * ones),
    )


def spread_kernel(docs, own, other, c0, c1, c2, c3, sums, sums_near, send, keep, total, *, half, size):
    rows = half * 128
    keep_coming, keep_other, send_coming, send_own = spread_weights(
        my_core() == 1,
        row(own, rows, FIRST),
        row(own, rows, LAST),
        row(other, rows, FIRST),
        row(other, rows, LAST),
    )
    for turn, chip in enumerate((c0, c1, c2, c3)):
        owner = lax.bitwise_xor(my_chip(), turned(turn))
        part = pl.ds(pl.multiple_of(owner * size, size), size)
        coming = chip[pl.ds(0, size), :]
        send[part, :] = coming * send_coming + own[part, :] * send_own
        keep[part, :] = (coming * keep_coming + other[part, :] * keep_other).astype(BF16)
    total[...] = sums[...] + sums_near[...]
    send[pl.ds(rows, IDS), :] = total[...]


def shape(rows, cols, dtype):
    return jax.ShapeDtypeStruct((rows, cols), dtype)


def call(kernel, docs, args, outs, flops=0, in_specs=None, out_specs=None, aliases=None, scratch=()):
    whole = pl.BlockSpec(memory_space=pltpu.VMEM)
    in_specs = in_specs or [None] * len(args)
    out_specs = out_specs or [None] * len(outs)
    moved = sum(a.size * a.dtype.itemsize for a in list(args) + list(outs))
    return pl.pallas_call(
        kernel,
        out_shape=outs,
        grid_spec=pltpu.PrefetchScalarGridSpec(
            num_scalar_prefetch=1,
            grid=(1,),
            in_specs=[spec or whole for spec in in_specs],
            out_specs=[spec or whole for spec in out_specs],
            scratch_shapes=scratch,
        ),
        input_output_aliases=aliases or {},
        cost_estimate=pl.CostEstimate(flops=flops, bytes_accessed=moved, transcendentals=0),
        compiler_params=pltpu.CompilerParams(vmem_limit_bytes=32 * 1024 * 1024),
    )(docs, *args)


def tie(value, *after):
    return lax.optimization_barrier((value, after))[0]


def local(queries, key_rows, value_rows, out_grad, norm_gain, doc_ids, *, shards, dp):
    tokens = queries.shape[1]
    heads, width = norm_gain.shape
    half = heads // 2
    rows, cols = half * width, heads * width
    size = rows // CHIPS
    query, key, value, grad = (
        a.reshape(tokens, cols) for a in (queries, key_rows, value_rows, out_grad)
    )
    planes = shards // GROUP
    any_place = pl.BlockSpec(memory_space=pl.ANY)

    def swap(value):
        return lax.ppermute(value, "ctx", [(i, i ^ 1) for i in range(shards)])

    def to_chips(values):
        return [values[0]] + [
            lax.ppermute(values[turn], "ctx", [(i, i ^ (2 * odd if i % 2 else 2 * even)) for i in range(shards)])
            for turn, even, odd in ((1, 1, 2), (2, 2, 1), (3, 3, 3))
        ]

    def around(value, distance):
        pairs = [(i, (i + distance * GROUP) % shards) for i in range(shards)]
        return lax.ppermute(value, "ctx", pairs)

    payload = shape(rows + IDS, width, F32)

    def chain(sent, backward, beside_up, beside_planes, beside_down):
        chunks = tie(to_chips(sent), beside_up(sent))
        plane, *gain = call(
            functools.partial(plane_kernel, size=size),
            doc_ids,
            chunks,
            [shape(size + (2 * IDS if backward else IDS), width, F32)]
            + ([shape(IDS, width, F32)] if backward else []),
        )
        distances = (-1, -2) if backward else (1, 2)
        others = [around(plane, distance) for distance in distances]
        others = tie(others, beside_planes(plane, others, *gain))
        sent = call(
            functools.partial(chain_kernel, size=size, distances=distances, planes=planes),
            doc_ids,
            [*chunks, *others, *gain],
            [shape(size, width, F32)] * CHIPS + ([shape(IDS, width, F32)] if backward else []),
        )
        return tie(to_chips(sent[:CHIPS]), beside_down(sent))

    def element(other):
        return call(
            functools.partial(element_kernel, half=half, other=other),
            doc_ids,
            [key, value],
            [payload],
            flops=2 * half * tokens * width * width,
        )[0]

    def within(other, sources, into):
        spare = [] if into is None else [into]
        at = 3 + len(sources)
        return call(
            functools.partial(within_kernel, half=half, other=other),
            doc_ids,
            [query, key, value, *sources, *spare],
            [shape(tokens, cols, BF16), shape(tokens, rows, F32), shape(tokens, rows, F32)],
            flops=2 * half * tokens * width * (6 * tokens + width),
            in_specs=[None] * at + [any_place] * len(spare),
            out_specs=[any_place] + [None] * 2,
            aliases={1 + at: 0} if spare else None,
            scratch=[pltpu.VMEM((tokens, rows), BF16), pltpu.SemaphoreType.DMA((half,))],
        )

    def finish(other, parts, state, sums, into):
        return call(
            functools.partial(finish_kernel, half=half, other=other),
            doc_ids,
            [key, value, *parts, state, *sums, *into],
            [shape(tokens, cols, BF16)] * 2 + [shape(heads, width, F32)] * len(sums),
            flops=2 * half * tokens * width * 2 * width,
            in_specs=[None] * (5 + len(sums)) + [any_place] * len(into),
            out_specs=[any_place] * 2 + [None] * len(sums),
            aliases={7: 0, 8: 1} if into else None,
            scratch=[
                pltpu.VMEM((tokens, rows), BF16),
                pltpu.VMEM((tokens, rows), BF16),
                pltpu.SemaphoreType.DMA((2, half)),
            ],
        )

    received = swap(element(True))
    own = element(False)
    sent = call(
        functools.partial(pair_kernel, half=half, size=size),
        doc_ids,
        [own, received],
        [shape(size + IDS, width, F32)] * CHIPS,
    )

    kept = {}

    def intra(sent):
        kept["inside"], kept["message"] = call(
            functools.partial(intra_kernel, half=half),
            doc_ids,
            [tie(query, sent), key, value, grad],
            [shape(tokens, rows, F32), shape(3 * tokens, rows, F32)],
            flops=2 * heads * tokens * width * 2 * tokens,
        )
        return kept["inside"]

    def forward_message(plane, others):
        kept["message"] = swap(tie(kept["message"], plane))
        return []

    coming = chain(sent, False, intra, forward_message, lambda sent: [])
    *sent, back, back_other, attn, reply, state = call(
        functools.partial(middle_kernel, half=half, size=size),
        doc_ids,
        [own, received, *coming, query, grad, kept["inside"], kept["message"], norm_gain],
        [shape(size + 2 * IDS, width, F32)] * CHIPS
        + [payload, payload]
        + [shape(tokens, rows, BF16), shape(tokens + width, rows, F32), shape(rows, width, BF16)],
        flops=2 * heads * tokens * width * 2 * width,
    )

    def beside_up(sent):
        kept["first"] = within(False, [tie(attn, sent), state], None)
        return kept["first"]

    def beside_planes(plane, others, gain):
        kept["reply"] = swap(tie(reply, plane))
        kept["near"] = around(tie(gain, others[1]), 1)
        return []

    def beside_down(sent):
        kept["sums"] = [sent[-1], kept["near"]]
        kept["second"] = within(True, [tie(kept["reply"], sent)], kept["first"][0])
        return kept["second"]

    coming = chain(sent, True, beside_up, beside_planes, beside_down)
    send, out_state, total = call(
        functools.partial(spread_kernel, half=half, size=size),
        doc_ids,
        [back, back_other, *coming, *kept["sums"]],
        [shape(rows + IDS, width, F32), shape(rows, width, BF16), shape(IDS, width, F32)],
    )
    out_received = swap(send)
    grads = finish(False, kept["first"][1:], out_state, [], [])
    out_received, grads = lax.optimization_barrier((out_received, grads))
    query_grad, *parts = kept["second"]
    key_grad, value_grad, gain_grad = finish(True, parts, out_received, [total], grads)
    if dp > 1:
        gain_grad = lax.psum_scatter(gain_grad, "dp", scatter_dimension=1, tiled=True)
    flat = (1, tokens, cols)
    return (query_grad.reshape(flat), key_grad.reshape(flat), value_grad.reshape(flat), gain_grad)


def solution(mesh):
    in_specs = (
        P("dp", "ctx", "tp"),
        P("dp", "ctx", "tp"),
        P("dp", "ctx", "tp"),
        P("dp", "ctx", "tp"),
        P("tp", None),
        P("dp", "ctx"),
    )
    out_specs = (P("dp", "ctx", "tp"), P("dp", "ctx", "tp"), P("dp", "ctx", "tp"), P("tp", "dp"))
    body = functools.partial(local, shards=mesh.shape["ctx"], dp=mesh.shape["dp"])
    return jax.shard_map(body, mesh=mesh, in_specs=in_specs, out_specs=out_specs, check_vma=False)
```

time: 736 us -> 82.7 us (0.11)
  waiting for transfers between devices: 289 us -> 28.6 us
  loops' own time: 123 us -> 0 us
  other arithmetic: 122 us -> 0 us
  blocking collectives: 82.7 us -> 0 us
  local copies, waits for them, and re-layouts: 78.1 us -> 3.12 us
  starting transfers between devices: 0.08 us -> 26.3 us
  Pallas kernels: 0 us -> 23.3 us
  matrix products: 22.4 us -> 0 us
  between operations: 14.3 us -> 0.97 us
    all_gather x2 -> x0, waiting for transfers between devices: 289 us -> none  [prefix(): pieces = jax.tree.map(lambda part: lax.all_gather(part, axis), value)]
    another operation x2 -> x0, loops' own time: 123 us -> none  [prefix(): return lax.fori_loop(0, count - 1, step, running)]
    select_n x62 -> x0, other arithmetic: 118 us -> none  [step(): jnp.where(position < mine, new, old)]
    all_gather x1 -> x0, blocking collectives: 42.9 us -> none  [prefix(): pieces = jax.tree.map(lambda part: lax.all_gather(part, axis), value)]
    unnamed x1 -> x0, blocking collectives: 39.9 us -> none
    dynamic_slice x62 -> x0, local copies, waits for them, and re-layouts: 36.3 us -> none  [step(): longer = join(running, jax.tree.map(lambda part: part[position], pieces))]
    ppermute x0 -> x21, waiting for transfers between devices: none -> 28.6 us  [the longest x5 15.7 us: around(): return lax.ppermute(value, 'ctx', pairs)]
    ppermute x0 -> x21, starting transfers between devices: none -> 26.3 us  [the longest x12 11.9 us: to_chips(): lax.ppermute(values[turn], 'ctx', [(i, i ^ (2 * odd if i % 2 else 2 * eve...]
  transfers between devices with their start and end apart: 2 -> 21, of which waited for: 2 -> 10; matrix products, arithmetic and copies ran while one was open for 3% -> 0% of each run, Pallas kernels for 0% -> 17%
where the time goes in v1:
time: 82.7 us; the launch traced here: 82.3 us
  waiting for transfers between devices  28.6 us (35%)
  starting transfers between devices  26.3 us (32%)
  Pallas kernels  23.3 us (28%)
  local copies, waits for them, and re-layouts  3.12 us (4%)
  between operations  0.97 us (1%)
    pallas_call x14, Pallas kernels, call(): pl.pallas_call(kernel, out_shape=outs, grid_spec=pltpu.PrefetchScalarGrid...  23.3 us
    ppermute x5, waiting for transfers between devices, around(): return lax.ppermute(value, 'ctx', pairs)  15.7 us
    ppermute x12, waiting for transfers between devices, to_chips(): lax.ppermute(values[turn], 'ctx', [(i, i ^ (2 * odd if i % 2 else 2 * eve...  12 us
    ppermute x12, starting transfers between devices, to_chips(): lax.ppermute(values[turn], 'ctx', [(i, i ^ (2 * odd if i % 2 else 2 * eve...  11.9 us
    ppermute x5, starting transfers between devices, around(): return lax.ppermute(value, 'ctx', pairs)  9.27 us
    ppermute x4, starting transfers between devices, swap(): return lax.ppermute(value, 'ctx', [(i, i ^ 1) for i in range(shards)])  5.13 us
    unnamed x16, local copies, waits for them, and re-layouts  3.12 us
  transfers between devices with their start and end apart: 21, of which 10 were waited for; matrix products, arithmetic and copies ran while one was open for 0% of the time, Pallas kernels for 17%

profile of v1, /device:TPU:1, one launch (start us, length us, event | category | flops | bytes accessed | tf_op | source)
XLA Modules:
  0.0 82.3 jit_solution(16764386518194841111)
XLA Ops:
  0.6 1.2 %copy-done = bf16[1,256,2048]{2,1,0:T(8,128)(2,1)S(1)} copy-done((bf16[1,256,2048]{2,1,0:T(8,128)(2,1)S(1)}, bf16[1,256,2048]{2,1,0:T(8,128)(2,1)}, u32[]{:S(2)}) %copy-start) | copy-done | bytes 1048600
  1.9 1.2 %copy-done.2 = bf16[1,256,2048]{2,1,0:T(8,128)(2,1)S(1)} copy-done((bf16[1,256,2048]{2,1,0:T(8,128)(2,1)S(1)}, bf16[1,256,2048]{2,1,0:T(8,128)(2,1)}, u32[]{:S(2)}) %copy-start.2) | copy-done | bytes 1048600
  3.1 0.7 copy-done.6
  3.8 1.0 %shard_map.94 = f32[1032,128]{1,0:T(8,128)S(1)} custom-call(s32[1,2]{1,0:T(1,128)S(1)} %copy-done.6, bf16[256,2048]{1,0:T(8,128)(2,1)S(1)} %bitcast.7, bf16[256,2048]{1,0:T(8,128)(2,1)S(1)} %bitcast.14), custom_call_target="tpu_custom_call" | custom-call | flops 67108864 | bytes 2625536 | tf_op jit(solution)/shard_map/pallas_call | solution.py:340
  4.8 0.1 collective-permute-start
  4.9 1.0 %shard_map.93.own = f32[1032,128]{1,0:T(8,128)S(1)} custom-call(s32[1,2]{1,0:T(1,128)S(1)} %copy-done.6, bf16[256,2048]{1,0:T(8,128)(2,1)S(1)} %bitcast.8, bf16[256,2048]{1,0:T(8,128)(2,1)S(1)} %bitcast.15), custom_call_target="tpu_custom_call" | custom-call | flops 67108864 | bytes 2625536 | tf_op jit(solution)/shard_map/pallas_call | solution.py:340
  6.0 0.8 collective-permute-done.other
  6.8 0.6 shard_map.95
  7.4 2.4 %collective-permute-start.1 = (f32[264,128]{1,0:T(8,128)S(1)}, f32[264,128]{1,0:T(8,128)S(1)}, u32[]{:S(2)}, u32[]{:S(2)}) collective-permute-start(f32[264,128]{1,0:T(8,128)S(1)} %get-tuple-element.74), channel_id=1, source_target_pairs={{0,2},{1,5},{2,0},{3,7},{4,6},{5,1},{6,4},{7,3},{8,10},{9,13},{10,... | collective-permute-start | bytes 405512 | tf_op jit(solution)/shard_map/ppermute | solution.py:377
  9.8 1.2 %collective-permute-start.2 = (f32[264,128]{1,0:T(8,128)S(1)}, f32[264,128]{1,0:T(8,128)S(1)}, u32[]{:S(2)}, u32[]{:S(2)}) collective-permute-start(f32[264,128]{1,0:T(8,128)S(1)} %get-tuple-element.75), channel_id=1, source_target_pairs={{0,4},{1,3},{2,6},{3,1},{4,0},{5,7},{6,2},{7,5},{8,12},{9,11},{10,... | collective-permute-start | bytes 405512 | tf_op jit(solution)/shard_map/ppermute | solution.py:377
  11.1 0.0 collective-permute-start.3
  11.1 3.6 %shard_map.96 = (f32[256,1024]{1,0:T(8,128)S(1)}, f32[768,1024]{1,0:T(8,128)S(1)}) custom-call(s32[1,2]{1,0:T(1,128)S(1)} %copy-done.6, bf16[256,2048]{1,0:T(8,128)(2,1)S(1)} %bitcast.21, bf16[256,2048]{1,0:T(8,128)(2,1)S(1)} %bitcast.9, bf16[256,2048]{1,0:T(8,128)(2,1)S(1)} %bitcast.16, bf16[256,2048]{1,0:T(8,128)(2,1)S(1)} %bitcast.25), custom_call_target="tpu_custom_call" | custom-call | flops 536870912 | bytes 8388608 | tf_op jit(solution)/shard_map/pallas_call | solution.py:340
  14.7 2.6 %collective-permute-done.3.c3 = f32[264,128]{1,0:T(8,128)S(1)} collective-permute-done((f32[264,128]{1,0:T(8,128)S(1)}, f32[264,128]{1,0:T(8,128)S(1)}, u32[]{:S(2)}, u32[]{:S(2)}) %collective-permute-start.3) | collective-permute-done | bytes 135200 | tf_op jit(solution)/shard_map/ppermute | solution.py:377
  17.3 0.6 shard_map.97
  17.8 1.3 %collective-permute-start.9 = (f32[768,1024]{1,0:T(8,128)S(1)}, f32[768,1024]{1,0:T(8,128)S(1)}, u32[]{:S(2)}, u32[]{:S(2)}) collective-permute-start(f32[768,1024]{1,0:T(8,128)S(1)} %get-tuple-element.94), channel_id=1, source_target_pairs={{0,1},{1,0},{2,3},{3,2},{4,5},{5,4},{6,7},{7,6},{8,9},{9,8},{10,11... | collective-permute-start | bytes 9437192 | tf_op jit(solution)/shard_map/ppermute | solution.py:373
  19.2 2.5 %collective-permute-start.5 = (f32[264,128]{1,0:T(8,128)S(1)}, f32[264,128]{1,0:T(8,128)S(1)}, u32[]{:S(2)}, u32[]{:S(2)}) collective-permute-start(f32[264,128]{1,0:T(8,128)S(1)} %shard_map.97), channel_id=1, source_target_pairs={{0,16},{1,17},{2,18},{3,19},{4,20},{5,21},{6,22},{7,23},{8,24},{9,... | collective-permute-start | bytes 405512 | tf_op jit(solution)/shard_map/ppermute | solution.py:383
  21.7 1.3 %collective-permute-start.4 = (f32[264,128]{1,0:T(8,128)S(1)}, f32[264,128]{1,0:T(8,128)S(1)}, u32[]{:S(2)}, u32[]{:S(2)}) collective-permute-start(f32[264,128]{1,0:T(8,128)S(1)} %shard_map.97), channel_id=1, source_target_pairs={{0,8},{1,9},{2,10},{3,11},{4,12},{5,13},{6,14},{7,15},{8,16},{9,17... | collective-permute-start | bytes 405512 | tf_op jit(solution)/shard_map/ppermute | solution.py:383
  23.0 8.3 %collective-permute-done.5.refs_1_ = f32[264,128]{1,0:T(8,128)S(1)} collective-permute-done((f32[264,128]{1,0:T(8,128)S(1)}, f32[264,128]{1,0:T(8,128)S(1)}, u32[]{:S(2)}, u32[]{:S(2)}) %collective-permute-start.5) | collective-permute-done | bytes 135200 | tf_op jit(solution)/shard_map/ppermute | solution.py:383
  31.2 0.7 shard_map.98
  32.0 1.0 %collective-permute-start.6 = (f32[256,128]{1,0:T(8,128)S(1)}, f32[256,128]{1,0:T(8,128)S(1)}, u32[]{:S(2)}, u32[]{:S(2)}) collective-permute-start(f32[256,128]{1,0:T(8,128)S(1)} %get-tuple-element.86), channel_id=1, source_target_pairs={{0,2},{1,5},{2,0},{3,7},{4,6},{5,1},{6,4},{7,3},{8,10},{9,13},{10,... | collective-permute-start | bytes 393224 | tf_op jit(solution)/shard_map/ppermute | solution.py:377
  33.0 0.6 collective-permute-start.7
  33.6 1.1 %collective-permute-start.8 = (f32[256,128]{1,0:T(8,128)S(1)}, f32[256,128]{1,0:T(8,128)S(1)}, u32[]{:S(2)}, u32[]{:S(2)}) collective-permute-start(f32[256,128]{1,0:T(8,128)S(1)} %get-tuple-element.88), channel_id=1, source_target_pairs={{0,6},{1,7},{2,4},{3,5},{4,2},{5,3},{6,0},{7,1},{8,14},{9,15},{10,... | collective-permute-start | bytes 393224 | tf_op jit(solution)/shard_map/ppermute | solution.py:377
  34.7 1.5 %collective-permute-done.6.c1 = f32[256,128]{1,0:T(8,128)S(1)} collective-permute-done((f32[256,128]{1,0:T(8,128)S(1)}, f32[256,128]{1,0:T(8,128)S(1)}, u32[]{:S(2)}, u32[]{:S(2)}) %collective-permute-start.6) | collective-permute-done | bytes 131104 | tf_op jit(solution)/shard_map/ppermute | solution.py:377
  36.1 2.0 %collective-permute-done.7.c2 = f32[256,128]{1,0:T(8,128)S(1)} collective-permute-done((f32[256,128]{1,0:T(8,128)S(1)}, f32[256,128]{1,0:T(8,128)S(1)}, u32[]{:S(2)}, u32[]{:S(2)}) %collective-permute-start.7) | collective-permute-done | bytes 131104 | tf_op jit(solution)/shard_map/ppermute | solution.py:377
  38.2 2.7 %collective-permute-done.8.c3 = f32[256,128]{1,0:T(8,128)S(1)} collective-permute-done((f32[256,128]{1,0:T(8,128)S(1)}, f32[256,128]{1,0:T(8,128)S(1)}, u32[]{:S(2)}, u32[]{:S(2)}) %collective-permute-start.8) | collective-permute-done | bytes 131104 | tf_op jit(solution)/shard_map/ppermute | solution.py:377
  40.8 3.3 %shard_map.99 = (f32[272,128]{1,0:T(8,128)S(1)}, f32[272,128]{1,0:T(8,128)S(1)}, f32[272,128]{1,0:T(8,128)S(1)}, f32[272,128]{1,0:T(8,128)S(1)}, f32[1032,128]{1...) custom-call(s32[1,2]{1,0:T(1,128)S(1)} %copy-done.6, ...), custom_call_target="tpu_custom_call" | custom-call | flops 268435456 | bytes 11853824 | tf_op jit(solution)/shard_map/pallas_call | solution.py:340
  44.1 1.1 %collective-permute-start.10 = (f32[272,128]{1,0:T(8,128)S(1)}, f32[272,128]{1,0:T(8,128)S(1)}, u32[]{:S(2)}, u32[]{:S(2)}) collective-permute-start(f32[272,128]{1,0:T(8,128)S(1)} %get-tuple-element.97), channel_id=1, source_target_pairs={{0,2},{1,5},{2,0},{3,7},{4,6},{5,1},{6,4},{7,3},{8,10},{9,13},{10,... | collective-permute-start | bytes 417800 | tf_op jit(solution)/shard_map/ppermute | solution.py:377
  45.2 0.6 collective-permute-start.11
  45.8 1.1 %collective-permute-start.12 = (f32[272,128]{1,0:T(8,128)S(1)}, f32[272,128]{1,0:T(8,128)S(1)}, u32[]{:S(2)}, u32[]{:S(2)}) collective-permute-start(f32[272,128]{1,0:T(8,128)S(1)} %get-tuple-element.99), channel_id=1, source_target_pairs={{0,6},{1,7},{2,4},{3,5},{4,2},{5,3},{6,0},{7,1},{8,14},{9,15},{10,... | collective-permute-start | bytes 417800 | tf_op jit(solution)/shard_map/ppermute | solution.py:377
  46.9 3.1 %shard_map.100 = (bf16[256,2048]{1,0:T(8,128)(2,1)}, f32[256,1024]{1,0:T(8,128)S(1)}, f32[256,1024]{1,0:T(8,128)S(1)}) custom-call(s32[1,2]{1,0:T(1,128)S(1)} %copy-done.6, bf16[256,2048]{1,0:T(8,128)(2,1)S(1)} %bitcast.23, bf16[256,2048]{1,0:T(8,128)(2,1)S(1)} %bitcast.10, bf16[256,2048]{1,0:T(8,128)(2,1)S(1)} %bitcast.17, ...), custom_call_target="tpu_custom_call" | custom-call | flops 872415232 | bytes 7077888 | tf_op jit(solution)/shard_map/pallas_call | solution.py:340
  50.0 0.3 collective-permute-done.11.c2
  50.3 3.0 %collective-permute-done.12.c3 = f32[272,128]{1,0:T(8,128)S(1)} collective-permute-done((f32[272,128]{1,0:T(8,128)S(1)}, f32[272,128]{1,0:T(8,128)S(1)}, u32[]{:S(2)}, u32[]{:S(2)}) %collective-permute-start.12) | collective-permute-done | bytes 139296 | tf_op jit(solution)/shard_map/ppermute | solution.py:377
  53.3 0.6 shard_map.101
  53.9 1.6 %collective-permute-start.13 = (f32[384,1024]{1,0:T(8,128)S(1)}, f32[384,1024]{1,0:T(8,128)S(1)}, u32[]{:S(2)}, u32[]{:S(2)}) collective-permute-start(f32[384,1024]{1,0:T(8,128)S(1)} %get-tuple-element.111), channel_id=1, source_target_pairs={{0,1},{1,0},{2,3},{3,2},{4,5},{5,4},{6,7},{7,6},{8,9},{9,8},{10,11... | collective-permute-start | bytes 4718600 | tf_op jit(solution)/shard_map/ppermute | solution.py:373
  55.5 2.7 %collective-permute-start.15 = (f32[272,128]{1,0:T(8,128)S(1)}, f32[272,128]{1,0:T(8,128)S(1)}, u32[]{:S(2)}, u32[]{:S(2)}) collective-permute-start(f32[272,128]{1,0:T(8,128)S(1)} %get-tuple-element.110), channel_id=1, source_target_pairs={{0,16},{1,17},{2,18},{3,19},{4,20},{5,21},{6,22},{7,23},{8,24},{9,... | collective-permute-start | bytes 417800 | tf_op jit(solution)/shard_map/ppermute | solution.py:383
  58.2 0.2 collective-permute-start.14
  58.3 6.8 %collective-permute-done.15.refs_1_ = f32[272,128]{1,0:T(8,128)S(1)} collective-permute-done((f32[272,128]{1,0:T(8,128)S(1)}, f32[272,128]{1,0:T(8,128)S(1)}, u32[]{:S(2)}, u32[]{:S(2)}) %collective-permute-start.15) | collective-permute-done | bytes 139296 | tf_op jit(solution)/shard_map/ppermute | solution.py:383
  65.2 0.6 collective-permute-done.14.refs_0_
  65.8 0.7 shard_map.102
  66.6 1.0 %collective-permute-start.16 = (f32[256,128]{1,0:T(8,128)S(1)}, f32[256,128]{1,0:T(8,128)S(1)}, u32[]{:S(2)}, u32[]{:S(2)}) collective-permute-start(f32[256,128]{1,0:T(8,128)S(1)} %get-tuple-element.116), channel_id=1, source_target_pairs={{0,2},{1,5},{2,0},{3,7},{4,6},{5,1},{6,4},{7,3},{8,10},{9,13},{10,... | collective-permute-start | bytes 393224 | tf_op jit(solution)/shard_map/ppermute | solution.py:377
  67.6 0.7 collective-permute-start.17
  68.3 1.0 %collective-permute-start.18 = (f32[256,128]{1,0:T(8,128)S(1)}, f32[256,128]{1,0:T(8,128)S(1)}, u32[]{:S(2)}, u32[]{:S(2)}) collective-permute-start(f32[256,128]{1,0:T(8,128)S(1)} %get-tuple-element.118), channel_id=1, source_target_pairs={{0,6},{1,7},{2,4},{3,5},{4,2},{5,3},{6,0},{7,1},{8,14},{9,15},{10,... | collective-permute-start | bytes 393224 | tf_op jit(solution)/shard_map/ppermute | solution.py:377
  69.3 2.6 %collective-permute-start.19 = (f32[8,128]{1,0:T(8,128)S(1)}, f32[8,128]{1,0:T(8,128)S(1)}, u32[]{:S(2)}, u32[]{:S(2)}) collective-permute-start(f32[8,128]{1,0:T(8,128)S(1)} %get-tuple-element.130.refs_2_), channel_id=1, source_target_pairs={{0,8},{1,9},{2,10},{3,11},{4,12},{5,13},{6,14},{7,15},{8,16},{9,17... | collective-permute-start | bytes 12296 | tf_op jit(solution)/shard_map/ppermute | solution.py:383
  71.9 3.1 %shard_map.103 = (bf16[256,2048]{1,0:T(8,128)(2,1)}, f32[256,1024]{1,0:T(8,128)S(1)}, f32[256,1024]{1,0:T(8,128)S(1)}) custom-call(s32[1,2]{1,0:T(1,128)S(1)} %copy-done.6, bf16[256,2048]{1,0:T(8,128)(2,1)S(1)} %bitcast.24, bf16[256,2048]{1,0:T(8,128)(2,1)S(1)} %bitcast.11, bf16[256,2048]{1,0:T(8,128)(2,1)S(1)} %bitcast.18, ...), custom_call_target="tpu_custom_call", output_to_operand_aliasing={{0}: (5, {})} | custom-call | flops 872415232 | bytes 8912896 | tf_op jit(solution)/shard_map/pallas_call | solution.py:340
  75.0 0.7 shard_map.104
  75.8 2.1 %collective-permute-start.20 = (f32[1032,128]{1,0:T(8,128)S(1)}, f32[1032,128]{1,0:T(8,128)S(1)}, u32[]{:S(2)}, u32[]{:S(2)}) collective-permute-start(f32[1032,128]{1,0:T(8,128)S(1)} %get-tuple-element.131), channel_id=1, source_target_pairs={{0,1},{1,0},{2,3},{3,2},{4,5},{5,4},{6,7},{7,6},{8,9},{9,8},{10,11... | collective-permute-start | bytes 1585160 | tf_op jit(solution)/shard_map/ppermute | solution.py:373
  77.8 1.9 %shard_map.105 = (bf16[256,2048]{1,0:T(8,128)(2,1)}, bf16[256,2048]{1,0:T(8,128)(2,1)}) custom-call(s32[1,2]{1,0:T(1,128)S(1)} %copy-done.6, bf16[256,2048]{1,0:T(8,128)(2,1)S(1)} %bitcast.12, bf16[256,2048]{1,0:T(8,128)(2,1)S(1)} %bitcast.19, f32[256,1024]{1,0:T(8,128)S(1)} %get-tuple-element.104.key_part, f32[256,1024]{1,0:T(8,128)S(1)} %get-tuple-element.105.value_part, ...), custom_call_target="tpu_custom_call" | custom-call | flops 134217728 | bytes 6553600 | tf_op jit(solution)/shard_map/pallas_call | solution.py:340
  79.7 2.5 %shard_map.106 = (bf16[256,2048]{1,0:T(8,128)(2,1)}, bf16[256,2048]{1,0:T(8,128)(2,1)}, f32[16,128]{1,0:T(8,128)}) custom-call(s32[1,2]{1,0:T(1,128)S(1)} %copy-done.6, bf16[256,2048]{1,0:T(8,128)(2,1)S(1)} %bitcast.13, bf16[256,2048]{1,0:T(8,128)(2,1)S(1)} %bitcast.20, ...), custom_call_target="tpu_custom_call", output_to_operand_aliasing={{0}: (7, {}), {1}: (8, {})} | custom-call | flops 134217728 | bytes 8929280 | tf_op jit(solution)/shard_map/pallas_call | solution.py:340
  (24 shorter events, 0.1 us)
Async XLA Ops:
  0.6 1.2 %copy-start = (bf16[1,256,2048]{2,1,0:T(8,128)(2,1)S(1)}, bf16[1,256,2048]{2,1,0:T(8,128)(2,1)}, u32[]{:S(2)}) copy-start(bf16[1,256,2048]{2,1,0:T(8,128)(2,1)} %param.7) | copy-start | bytes 3145732
  1.9 1.2 %copy-start.2 = (bf16[1,256,2048]{2,1,0:T(8,128)(2,1)S(1)}, bf16[1,256,2048]{2,1,0:T(8,128)(2,1)}, u32[]{:S(2)}) copy-start(bf16[1,256,2048]{2,1,0:T(8,128)(2,1)} %param.8) | copy-start | bytes 3145732
  3.1 0.7 copy-start.6
  3.7 7.4 %copy-start.1 = (bf16[1,256,2048]{2,1,0:T(8,128)(2,1)S(1)}, bf16[1,256,2048]{2,1,0:T(8,128)(2,1)}, u32[]{:S(2)}) copy-start(bf16[1,256,2048]{2,1,0:T(8,128)(2,1)} %param.7) | copy-start | bytes 3145732
  3.7 7.4 %copy-start.3 = (bf16[1,256,2048]{2,1,0:T(8,128)(2,1)S(1)}, bf16[1,256,2048]{2,1,0:T(8,128)(2,1)}, u32[]{:S(2)}) copy-start(bf16[1,256,2048]{2,1,0:T(8,128)(2,1)} %param.8) | copy-start | bytes 3145732
  3.7 7.4 %copy-start.4 = (bf16[1,256,2048]{2,1,0:T(8,128)(2,1)S(1)}, bf16[1,256,2048]{2,1,0:T(8,128)(2,1)}, u32[]{:S(2)}) copy-start(bf16[1,256,2048]{2,1,0:T(8,128)(2,1)} %param.6) | copy-start | bytes 3145732
  3.7 7.4 %copy-start.5 = (bf16[1,256,2048]{2,1,0:T(8,128)(2,1)S(1)}, bf16[1,256,2048]{2,1,0:T(8,128)(2,1)}, u32[]{:S(2)}) copy-start(bf16[1,256,2048]{2,1,0:T(8,128)(2,1)} %param.9) | copy-start | bytes 3145732
  4.8 2.0 %collective-permute-start = (f32[1032,128]{1,0:T(8,128)S(1)}, f32[1032,128]{1,0:T(8,128)S(1)}, u32[]{:S(2)}, u32[]{:S(2)}) collective-permute-start(f32[1032,128]{1,0:T(8,128)S(1)} %shard_map.94), channel_id=1, source_target_pairs={{0,1},{1,0},{2,3},{3,2},{4,5},{5,4},{6,7},{7,6},{8,9},{9,8},{10,11... | collective-permute-start | bytes 1585160 | tf_op jit(solution)/shard_map/ppermute | solution.py:373
  5.9 34.9 %copy-start.7 = (f32[16,128]{1,0:T(8,128)S(1)}, f32[16,128]{1,0:T(8,128)}, u32[]{:S(2)}) copy-start(f32[16,128]{1,0:T(8,128)} %gain.1) | copy-start | bytes 24580
  7.4 7.3 %collective-permute-start.1 = (f32[264,128]{1,0:T(8,128)S(1)}, f32[264,128]{1,0:T(8,128)S(1)}, u32[]{:S(2)}, u32[]{:S(2)}) collective-permute-start(f32[264,128]{1,0:T(8,128)S(1)} %get-tuple-element.74), channel_id=1, source_target_pairs={{0,2},{1,5},{2,0},{3,7},{4,6},{5,1},{6,4},{7,3},{8,10},{9,13},{10,... | collective-permute-start | bytes 405512 | tf_op jit(solution)/shard_map/ppermute | solution.py:377
  9.8 4.8 %collective-permute-start.2 = (f32[264,128]{1,0:T(8,128)S(1)}, f32[264,128]{1,0:T(8,128)S(1)}, u32[]{:S(2)}, u32[]{:S(2)}) collective-permute-start(f32[264,128]{1,0:T(8,128)S(1)} %get-tuple-element.75), channel_id=1, source_target_pairs={{0,4},{1,3},{2,6},{3,1},{4,0},{5,7},{6,2},{7,5},{8,12},{9,11},{10,... | collective-permute-start | bytes 405512 | tf_op jit(solution)/shard_map/ppermute | solution.py:377
  11.1 6.2 %collective-permute-start.3 = (f32[264,128]{1,0:T(8,128)S(1)}, f32[264,128]{1,0:T(8,128)S(1)}, u32[]{:S(2)}, u32[]{:S(2)}) collective-permute-start(f32[264,128]{1,0:T(8,128)S(1)} %get-tuple-element.76), channel_id=1, source_target_pairs={{0,6},{1,7},{2,4},{3,5},{4,2},{5,3},{6,0},{7,1},{8,14},{9,15},{10,... | collective-permute-start | bytes 405512 | tf_op jit(solution)/shard_map/ppermute | solution.py:377
  17.8 23.0 %collective-permute-start.9 = (f32[768,1024]{1,0:T(8,128)S(1)}, f32[768,1024]{1,0:T(8,128)S(1)}, u32[]{:S(2)}, u32[]{:S(2)}) collective-permute-start(f32[768,1024]{1,0:T(8,128)S(1)} %get-tuple-element.94), channel_id=1, source_target_pairs={{0,1},{1,0},{2,3},{3,2},{4,5},{5,4},{6,7},{7,6},{8,9},{9,8},{10,11... | collective-permute-start | bytes 9437192 | tf_op jit(solution)/shard_map/ppermute | solution.py:373
  19.2 12.0 %collective-permute-start.5 = (f32[264,128]{1,0:T(8,128)S(1)}, f32[264,128]{1,0:T(8,128)S(1)}, u32[]{:S(2)}, u32[]{:S(2)}) collective-permute-start(f32[264,128]{1,0:T(8,128)S(1)} %shard_map.97), channel_id=1, source_target_pairs={{0,16},{1,17},{2,18},{3,19},{4,20},{5,21},{6,22},{7,23},{8,24},{9,... | collective-permute-start | bytes 405512 | tf_op jit(solution)/shard_map/ppermute | solution.py:383
  21.7 9.6 %collective-permute-start.4 = (f32[264,128]{1,0:T(8,128)S(1)}, f32[264,128]{1,0:T(8,128)S(1)}, u32[]{:S(2)}, u32[]{:S(2)}) collective-permute-start(f32[264,128]{1,0:T(8,128)S(1)} %shard_map.97), channel_id=1, source_target_pairs={{0,8},{1,9},{2,10},{3,11},{4,12},{5,13},{6,14},{7,15},{8,16},{9,17... | collective-permute-start | bytes 405512 | tf_op jit(solution)/shard_map/ppermute | solution.py:383
  32.0 4.2 %collective-permute-start.6 = (f32[256,128]{1,0:T(8,128)S(1)}, f32[256,128]{1,0:T(8,128)S(1)}, u32[]{:S(2)}, u32[]{:S(2)}) collective-permute-start(f32[256,128]{1,0:T(8,128)S(1)} %get-tuple-element.86), channel_id=1, source_target_pairs={{0,2},{1,5},{2,0},{3,7},{4,6},{5,1},{6,4},{7,3},{8,10},{9,13},{10,... | collective-permute-start | bytes 393224 | tf_op jit(solution)/shard_map/ppermute | solution.py:377
  33.0 5.2 %collective-permute-start.7 = (f32[256,128]{1,0:T(8,128)S(1)}, f32[256,128]{1,0:T(8,128)S(1)}, u32[]{:S(2)}, u32[]{:S(2)}) collective-permute-start(f32[256,128]{1,0:T(8,128)S(1)} %get-tuple-element.87), channel_id=1, source_target_pairs={{0,4},{1,3},{2,6},{3,1},{4,0},{5,7},{6,2},{7,5},{8,12},{9,11},{10,... | collective-permute-start | bytes 393224 | tf_op jit(solution)/shard_map/ppermute | solution.py:377
  33.6 7.2 %collective-permute-start.8 = (f32[256,128]{1,0:T(8,128)S(1)}, f32[256,128]{1,0:T(8,128)S(1)}, u32[]{:S(2)}, u32[]{:S(2)}) collective-permute-start(f32[256,128]{1,0:T(8,128)S(1)} %get-tuple-element.88), channel_id=1, source_target_pairs={{0,6},{1,7},{2,4},{3,5},{4,2},{5,3},{6,0},{7,1},{8,14},{9,15},{10,... | collective-permute-start | bytes 393224 | tf_op jit(solution)/shard_map/ppermute | solution.py:377
  44.1 5.9 %collective-permute-start.10 = (f32[272,128]{1,0:T(8,128)S(1)}, f32[272,128]{1,0:T(8,128)S(1)}, u32[]{:S(2)}, u32[]{:S(2)}) collective-permute-start(f32[272,128]{1,0:T(8,128)S(1)} %get-tuple-element.97), channel_id=1, source_target_pairs={{0,2},{1,5},{2,0},{3,7},{4,6},{5,1},{6,4},{7,3},{8,10},{9,13},{10,... | collective-permute-start | bytes 417800 | tf_op jit(solution)/shard_map/ppermute | solution.py:377
  45.2 5.0 %collective-permute-start.11 = (f32[272,128]{1,0:T(8,128)S(1)}, f32[272,128]{1,0:T(8,128)S(1)}, u32[]{:S(2)}, u32[]{:S(2)}) collective-permute-start(f32[272,128]{1,0:T(8,128)S(1)} %get-tuple-element.98), channel_id=1, source_target_pairs={{0,4},{1,3},{2,6},{3,1},{4,0},{5,7},{6,2},{7,5},{8,12},{9,11},{10,... | collective-permute-start | bytes 417800 | tf_op jit(solution)/shard_map/ppermute | solution.py:377
  45.8 7.5 %collective-permute-start.12 = (f32[272,128]{1,0:T(8,128)S(1)}, f32[272,128]{1,0:T(8,128)S(1)}, u32[]{:S(2)}, u32[]{:S(2)}) collective-permute-start(f32[272,128]{1,0:T(8,128)S(1)} %get-tuple-element.99), channel_id=1, source_target_pairs={{0,6},{1,7},{2,4},{3,5},{4,2},{5,3},{6,0},{7,1},{8,14},{9,15},{10,... | collective-permute-start | bytes 417800 | tf_op jit(solution)/shard_map/ppermute | solution.py:377
  53.9 18.0 %collective-permute-start.13 = (f32[384,1024]{1,0:T(8,128)S(1)}, f32[384,1024]{1,0:T(8,128)S(1)}, u32[]{:S(2)}, u32[]{:S(2)}) collective-permute-start(f32[384,1024]{1,0:T(8,128)S(1)} %get-tuple-element.111), channel_id=1, source_target_pairs={{0,1},{1,0},{2,3},{3,2},{4,5},{5,4},{6,7},{7,6},{8,9},{9,8},{10,11... | collective-permute-start | bytes 4718600 | tf_op jit(solution)/shard_map/ppermute | solution.py:373
  55.5 9.7 %collective-permute-start.15 = (f32[272,128]{1,0:T(8,128)S(1)}, f32[272,128]{1,0:T(8,128)S(1)}, u32[]{:S(2)}, u32[]{:S(2)}) collective-permute-start(f32[272,128]{1,0:T(8,128)S(1)} %get-tuple-element.110), channel_id=1, source_target_pairs={{0,16},{1,17},{2,18},{3,19},{4,20},{5,21},{6,22},{7,23},{8,24},{9,... | collective-permute-start | bytes 417800 | tf_op jit(solution)/shard_map/ppermute | solution.py:383
  58.2 7.6 %collective-permute-start.14 = (f32[272,128]{1,0:T(8,128)S(1)}, f32[272,128]{1,0:T(8,128)S(1)}, u32[]{:S(2)}, u32[]{:S(2)}) collective-permute-start(f32[272,128]{1,0:T(8,128)S(1)} %get-tuple-element.110), channel_id=1, source_target_pairs={{0,24},{1,25},{2,26},{3,27},{4,28},{5,29},{6,30},{7,31},{8,0},{9,1... | collective-permute-start | bytes 417800 | tf_op jit(solution)/shard_map/ppermute | solution.py:383
  66.6 8.4 %collective-permute-start.16 = (f32[256,128]{1,0:T(8,128)S(1)}, f32[256,128]{1,0:T(8,128)S(1)}, u32[]{:S(2)}, u32[]{:S(2)}) collective-permute-start(f32[256,128]{1,0:T(8,128)S(1)} %get-tuple-element.116), channel_id=1, source_target_pairs={{0,2},{1,5},{2,0},{3,7},{4,6},{5,1},{6,4},{7,3},{8,10},{9,13},{10,... | collective-permute-start | bytes 393224 | tf_op jit(solution)/shard_map/ppermute | solution.py:377
  67.6 7.4 %collective-permute-start.17 = (f32[256,128]{1,0:T(8,128)S(1)}, f32[256,128]{1,0:T(8,128)S(1)}, u32[]{:S(2)}, u32[]{:S(2)}) collective-permute-start(f32[256,128]{1,0:T(8,128)S(1)} %get-tuple-element.117), channel_id=1, source_target_pairs={{0,4},{1,3},{2,6},{3,1},{4,0},{5,7},{6,2},{7,5},{8,12},{9,11},{10,... | collective-permute-start | bytes 393224 | tf_op jit(solution)/shard_map/ppermute | solution.py:377
  68.3 6.7 %collective-permute-start.18 = (f32[256,128]{1,0:T(8,128)S(1)}, f32[256,128]{1,0:T(8,128)S(1)}, u32[]{:S(2)}, u32[]{:S(2)}) collective-permute-start(f32[256,128]{1,0:T(8,128)S(1)} %get-tuple-element.118), channel_id=1, source_target_pairs={{0,6},{1,7},{2,4},{3,5},{4,2},{5,3},{6,0},{7,1},{8,14},{9,15},{10,... | collective-permute-start | bytes 393224 | tf_op jit(solution)/shard_map/ppermute | solution.py:377
  69.3 5.7 %collective-permute-start.19 = (f32[8,128]{1,0:T(8,128)S(1)}, f32[8,128]{1,0:T(8,128)S(1)}, u32[]{:S(2)}, u32[]{:S(2)}) collective-permute-start(f32[8,128]{1,0:T(8,128)S(1)} %get-tuple-element.130.refs_2_), channel_id=1, source_target_pairs={{0,8},{1,9},{2,10},{3,11},{4,12},{5,13},{6,14},{7,15},{8,16},{9,17... | collective-permute-start | bytes 12296 | tf_op jit(solution)/shard_map/ppermute | solution.py:383
  75.8 3.9 %collective-permute-start.20 = (f32[1032,128]{1,0:T(8,128)S(1)}, f32[1032,128]{1,0:T(8,128)S(1)}, u32[]{:S(2)}, u32[]{:S(2)}) collective-permute-start(f32[1032,128]{1,0:T(8,128)S(1)} %get-tuple-element.131), channel_id=1, source_target_pairs={{0,1},{1,0},{2,3},{3,2},{4,5},{5,4},{6,7},{7,6},{8,9},{9,8},{10,11... | collective-permute-start | bytes 1585160 | tf_op jit(solution)/shard_map/ppermute | solution.py:373

commit v2 on v1

--- a/solution.py
+++ b/solution.py
@@ -28,10 +28,6 @@
 
 def my_chip():
     return (lax.axis_index("ctx") // 2) % CHIPS
-
-
-def turned(turn):
-    return (0, 1 + my_core(), 2 - my_core(), 3)[turn]
 
 
 def one_doc(docs):
@@ -87,13 +83,36 @@
     return pl.ds(pl.multiple_of((base + head) * 128, 128), 128)
 
 
-def element_kernel(docs, key, value, out, *, half, other):
-    base = (1 - my_core() if other else my_core()) * half
+def element(docs, key, value, out, first_col, half):
     weight = column(docs, False, BF16)
     write_ids(docs, out, half * 128, False)
     for head in range(half):
-        at = wide(base, head)
+        at = wide(first_col, head)
         out[pl.ds(head * 128, 128), :] = dot(key[:, at] * weight, value[:, at], 0, 0)
+
+
+def first_kernel(docs, key, value, out, key_own, value_own, docs_held, key_held, value_held, sems, *, half):
+    core, rows = my_core(), half * 128
+    far = pl.ds(pl.multiple_of((1 - core) * rows, rows), rows)
+    own = pl.ds(pl.multiple_of(core * rows, rows), rows)
+    copies = [
+        pltpu.make_async_copy(docs, docs_held, sems.at[0]),
+        pltpu.make_async_copy(key.at[:, far], key_held, sems.at[1]),
+        pltpu.make_async_copy(value.at[:, far], value_held, sems.at[2]),
+        pltpu.make_async_copy(key.at[:, own], key_own, sems.at[3]),
+        pltpu.make_async_copy(value.at[:, own], value_own, sems.at[4]),
+    ]
+    for copy in copies:
+        copy.start()
+    for copy in copies[:3]:
+        copy.wait()
+    element(docs_held, key_held, value_held, out, 0, half)
+    for copy in copies[3:]:
+        copy.wait()
+
+
+def second_kernel(docs, key, value, out, *, half):
+    element(docs, key, value, out, 0, half)
 
 
 def intra_kernel(docs, query, key, value, grad, own, message, *, half):
@@ -114,14 +133,20 @@
                 own[:, cols] = part
 
 
+def channel_mean(table):
+    high = table.astype(BF16)
+    low = (table - high.astype(F32)).astype(BF16)
+    return dot(jnp.concatenate([high, low], 1), jnp.full((256, 128), 1.0 / 128, BF16), 1, 0)
+
+
 def attend(q, g, intra, state, gain, joined):
     inter = dot(q, state, 1, 0)
     attended = intra + jnp.concatenate([inter[:BLK], inter[BLK:] * joined], 0)
-    inv_rms = lax.rsqrt(jnp.mean(attended * attended, -1, keepdims=True) + EPSILON)
+    inv_rms = lax.rsqrt(channel_mean(attended * attended) + EPSILON)
     scaled = g * gain
     normed = attended * inv_rms
     terms = jnp.sum(g * normed, 0, keepdims=True)
-    mean = jnp.mean(scaled * normed, -1, keepdims=True)
+    mean = channel_mean(scaled * normed)
     attn = (inv_rms * (scaled - normed * mean)).astype(BF16)
     back = dot(q[:BLK], attn[:BLK], 0, 0) + dot(q[BLK:], attn[BLK:], 0, 0) * joined
     return attn, back, terms
@@ -154,7 +179,7 @@
         up[pl.ds(size + LAST, 1), :] = -first
     for turn, chip in enumerate((c0, c1, c2, c3)):
         for step in range(chunk):
-            head = lax.bitwise_xor(my_chip(), turned(turn)) * chunk + step
+            head = lax.bitwise_xor(my_chip(), turn) * chunk + step
             cols, full = wide(0, head), wide(base, head)
             coming = chip[pl.ds(step * 128, 128), :]
             state = (coming * keep_coming + other[cols, :] * keep_other).astype(BF16)
@@ -249,7 +274,7 @@
     own_weight = match(row(own, rows, LAST), last)
     other_weight = match(row(other, rows, LAST), last)
     for turn, out in enumerate(outs):
-        owner = lax.bitwise_xor(my_chip(), turned(turn))
+        owner = lax.bitwise_xor(my_chip(), turn)
         part = pl.ds(pl.multiple_of(owner * size, size), size)
         out[pl.ds(0, size), :] = own[part, :] * own_weight + other[part, :] * other_weight
         out[pl.ds(size, IDS), :] = jnp.zeros((IDS, 128), F32)
@@ -274,7 +299,7 @@
     chips = (c0, c1, c2, c3)
     backward = distances[0] < 0
     others, outs = refs[: len(distances)], refs[-CHIPS:]
-    place = [lax.bitwise_xor(my_chip(), turned(turn)) for turn in range(CHIPS)]
+    place = [lax.bitwise_xor(my_chip(), turn) for turn in range(CHIPS)]
     my_plane = lax.axis_index("ctx") // GROUP
     first = functools.reduce(jnp.minimum, [row(c, size, FIRST) for c in chips])
     coming = jnp.zeros((size, 128), F32)
@@ -319,7 +344,7 @@
         row(other, rows, LAST),
     )
     for turn, chip in enumerate((c0, c1, c2, c3)):
-        owner = lax.bitwise_xor(my_chip(), turned(turn))
+        owner = lax.bitwise_xor(my_chip(), turn)
         part = pl.ds(pl.multiple_of(owner * size, size), size)
         coming = chip[pl.ds(0, size), :]
         send[part, :] = coming * send_coming + own[part, :] * send_own
@@ -374,8 +399,8 @@
 
     def to_chips(values):
         return [values[0]] + [
-            lax.ppermute(values[turn], "ctx", [(i, i ^ (2 * odd if i % 2 else 2 * even)) for i in range(shards)])
-            for turn, even, odd in ((1, 1, 2), (2, 2, 1), (3, 3, 3))
+            lax.ppermute(values[turn], "ctx", [(i, i ^ (2 * turn)) for i in range(shards)])
+            for turn in (1, 2, 3)
         ]
 
     def around(value, distance):
@@ -395,23 +420,14 @@
         )
         distances = (-1, -2) if backward else (1, 2)
         others = [around(plane, distance) for distance in distances]
-        others = tie(others, beside_planes(plane, others, *gain))
+        others = tie(others, beside_planes(plane))
         sent = call(
             functools.partial(chain_kernel, size=size, distances=distances, planes=planes),
             doc_ids,
             [*chunks, *others, *gain],
             [shape(size, width, F32)] * CHIPS + ([shape(IDS, width, F32)] if backward else []),
         )
-        return tie(to_chips(sent[:CHIPS]), beside_down(sent))
-
-    def element(other):
-        return call(
-            functools.partial(element_kernel, half=half, other=other),
-            doc_ids,
-            [key, value],
-            [payload],
-            flops=2 * half * tokens * width * width,
-        )[0]
+        return tie(to_chips(sent[:CHIPS]), beside_down(sent, *gain))
 
     def within(other, sources, into):
         spare = [] if into is None else [into]
@@ -445,8 +461,34 @@
             ],
         )
 
-    received = swap(element(True))
-    own = element(False)
+    hbm = pl.BlockSpec(memory_space=pltpu.HBM)
+    vmem = pl.BlockSpec(memory_space=pltpu.VMEM)
+    half_shape = shape(tokens, rows, BF16)
+    states, key_own, value_own = pl.pallas_call(
+        functools.partial(first_kernel, half=half),
+        out_shape=[payload, half_shape, half_shape],
+        in_specs=[hbm] * 3,
+        out_specs=[vmem] * 3,
+        scratch_shapes=[
+            pltpu.SMEM(doc_ids.shape, jnp.int32),
+            pltpu.VMEM(half_shape.shape, BF16),
+            pltpu.VMEM(half_shape.shape, BF16),
+            pltpu.SemaphoreType.DMA((5,)),
+        ],
+        cost_estimate=pl.CostEstimate(
+            flops=2 * half * tokens * width * width, bytes_accessed=4 * tokens * rows * 2, transcendentals=0
+        ),
+        compiler_params=pltpu.CompilerParams(vmem_limit_bytes=32 * 1024 * 1024),
+    )(*(pltpu.with_memory_space_constraint(x, pltpu.HBM) for x in (doc_ids, key, value)))
+    received = swap(states)
+    query, key, value, grad, doc_ids = tie((query, key, value, grad, doc_ids), states)
+    (own,) = call(
+        functools.partial(second_kernel, half=half),
+        doc_ids,
+        [key_own, value_own],
+        [payload],
+        flops=2 * half * tokens * width * width,
+    )
     sent = call(
         functools.partial(pair_kernel, half=half, size=size),
         doc_ids,
@@ -466,7 +508,7 @@
         )
         return kept["inside"]
 
-    def forward_message(plane, others):
+    def forward_message(plane):
         kept["message"] = swap(tie(kept["message"], plane))
         return []
 
@@ -485,13 +527,12 @@
         kept["first"] = within(False, [tie(attn, sent), state], None)
         return kept["first"]
 
-    def beside_planes(plane, others, gain):
+    def beside_planes(plane):
         kept["reply"] = swap(tie(reply, plane))
-        kept["near"] = around(tie(gain, others[1]), 1)
         return []
 
-    def beside_down(sent):
-        kept["sums"] = [sent[-1], kept["near"]]
+    def beside_down(sent, gain):
+        kept["sums"] = [sent[-1], around(tie(gain, sent), 1)]
         kept["second"] = within(True, [tie(kept["reply"], sent)], kept["first"][0])
         return kept["second"]
 

time: 82.7 us -> 82.1 us (level)
  Pallas kernels: 23.3 us -> 27.2 us
  waiting for transfers between devices: 28.6 us -> 25.6 us
  local copies, waits for them, and re-layouts: 3.12 us -> 0.68 us
  starting transfers between devices: 26.3 us -> 27.5 us
    ppermute x12, waiting for transfers between devices: 12 us -> 9.55 us  [to_chips(): lax.ppermute(values[turn], 'ctx', [(i, i ^ 2 * turn) for i in range(shard...]
    unnamed x16 -> x12, local copies, waits for them, and re-layouts: 3.12 us -> 0.68 us
    pallas_call x14 -> x13, Pallas kernels: 23.3 us -> 25.5 us  [call(): pl.pallas_call(kernel, out_shape=outs, grid_spec=pltpu.PrefetchScalarGrid...]
    pallas_call x0 -> x1, Pallas kernels: none -> 1.77 us  [local(): pl.pallas_call(functools.partial(first_kernel, half=half), out_shape=[pay...]
    ppermute x4, starting transfers between devices: 5.13 us -> 6.35 us  [swap(): return lax.ppermute(value, 'ctx', [(i, i ^ 1) for i in range(shards)])]
  transfers between devices with their start and end apart: 21 -> 21, of which waited for: 10 -> 9; matrix products, arithmetic and copies ran while one was open for 0% -> 0% of each run, Pallas kernels for 17% -> 17%
where the time goes in v2:
time: 82.1 us; the launch traced here: 82 us
  starting transfers between devices  27.5 us (33%)
  Pallas kernels  27.2 us (33%)
  waiting for transfers between devices  25.6 us (31%)
  between operations  1 us (1%)
    pallas_call x13, Pallas kernels, call(): pl.pallas_call(kernel, out_shape=outs, grid_spec=pltpu.PrefetchScalarGrid...  25.5 us
    ppermute x5, waiting for transfers between devices, around(): return lax.ppermute(value, 'ctx', pairs)  15.7 us
    ppermute x12, starting transfers between devices, to_chips(): lax.ppermute(values[turn], 'ctx', [(i, i ^ 2 * turn) for i in range(shard...  11.8 us
    ppermute x12, waiting for transfers between devices, to_chips(): lax.ppermute(values[turn], 'ctx', [(i, i ^ 2 * turn) for i in range(shard...  9.55 us
    ppermute x5, starting transfers between devices, around(): return lax.ppermute(value, 'ctx', pairs)  9.31 us
    ppermute x4, starting transfers between devices, swap(): return lax.ppermute(value, 'ctx', [(i, i ^ 1) for i in range(shards)])  6.35 us
    pallas_call x1, Pallas kernels, local(): pl.pallas_call(functools.partial(first_kernel, half=half), out_shape=[pay...  1.77 us
  transfers between devices with their start and end apart: 21, of which 9 were waited for; matrix products, arithmetic and copies ran while one was open for 0% of the time, Pallas kernels for 17%

profile of v2, /device:TPU:1, one launch (start us, length us, event | category | flops | bytes accessed | tf_op | source)
XLA Modules:
  0.0 82.0 jit_solution(12576755269136212780)
XLA Ops:
  0.7 1.8 %shard_map.93 = (f32[1032,128]{1,0:T(8,128)S(1)}, bf16[256,1024]{1,0:T(8,128)(2,1)S(1)}, bf16[256,1024]{1,0:T(8,128)(2,1)S(1)}) custom-call(s32[1,2]{1,0:T(1,128)} %docs.14, bf16[256,2048]{1,0:T(8,128)(2,1)} %bitcast.7, bf16[256,2048]{1,0:T(8,128)(2,1)} %bitcast.13), custom_call_target="tpu_custom_call" | custom-call | flops 67108864 | bytes 2097152 | tf_op jit(solution)/shard_map/pallas_call | solution.py:467
  2.5 0.1 collective-permute-start
  2.6 0.7 copy-done.4
  3.2 0.9 %shard_map.94.own = f32[1032,128]{1,0:T(8,128)S(1)} custom-call(s32[1,2]{1,0:T(1,128)S(1)} %copy-done.4, bf16[256,1024]{1,0:T(8,128)(2,1)S(1)} %get-tuple-element.86.key, bf16[256,1024]{1,0:T(8,128)(2,1)S(1)} %get-tuple-element.87.value), custom_call_target="tpu_custom_call" | custom-call | flops 67108864 | bytes 1576960 | tf_op jit(solution)/shard_map/pallas_call | solution.py:365
  4.1 0.0 copy-start.5
  4.1 0.3 collective-permute-done.other
  4.4 0.6 shard_map.95
  5.1 2.4 %collective-permute-start.1 = (f32[264,128]{1,0:T(8,128)S(1)}, f32[264,128]{1,0:T(8,128)S(1)}, u32[]{:S(2)}, u32[]{:S(2)}) collective-permute-start(f32[264,128]{1,0:T(8,128)S(1)} %get-tuple-element.89), channel_id=1, source_target_pairs={{0,2},{1,3},{2,0},{3,1},{4,6},{5,7},{6,4},{7,5},{8,10},{9,11},{10,... | collective-permute-start | bytes 405512 | tf_op jit(solution)/shard_map/ppermute | solution.py:402
  7.5 1.2 %collective-permute-start.2 = (f32[264,128]{1,0:T(8,128)S(1)}, f32[264,128]{1,0:T(8,128)S(1)}, u32[]{:S(2)}, u32[]{:S(2)}) collective-permute-start(f32[264,128]{1,0:T(8,128)S(1)} %get-tuple-element.90), channel_id=1, source_target_pairs={{0,4},{1,5},{2,6},{3,7},{4,0},{5,1},{6,2},{7,3},{8,12},{9,13},{10,... | collective-permute-start | bytes 405512 | tf_op jit(solution)/shard_map/ppermute | solution.py:402
  8.8 0.0 collective-permute-start.3
  8.8 3.6 %shard_map.96 = (f32[256,1024]{1,0:T(8,128)S(1)}, f32[768,1024]{1,0:T(8,128)S(1)}) custom-call(s32[1,2]{1,0:T(1,128)S(1)} %copy-done.4, bf16[256,2048]{1,0:T(8,128)(2,1)S(1)} %bitcast.19, bf16[256,2048]{1,0:T(8,128)(2,1)S(1)} %bitcast.8, bf16[256,2048]{1,0:T(8,128)(2,1)S(1)} %bitcast.14, bf16[256,2048]{1,0:T(8,128)(2,1)S(1)} %bitcast.23), custom_call_target="tpu_custom_call" | custom-call | flops 536870912 | bytes 8388608 | tf_op jit(solution)/shard_map/pallas_call | solution.py:365
  12.4 0.0 collective-permute-done.2.c2
  12.4 2.5 %collective-permute-done.3.c3 = f32[264,128]{1,0:T(8,128)S(1)} collective-permute-done((f32[264,128]{1,0:T(8,128)S(1)}, f32[264,128]{1,0:T(8,128)S(1)}, u32[]{:S(2)}, u32[]{:S(2)}) %collective-permute-start.3) | collective-permute-done | bytes 135200 | tf_op jit(solution)/shard_map/ppermute | solution.py:402
  14.9 0.6 shard_map.97
  15.5 1.6 %collective-permute-start.9 = (f32[768,1024]{1,0:T(8,128)S(1)}, f32[768,1024]{1,0:T(8,128)S(1)}, u32[]{:S(2)}, u32[]{:S(2)}) collective-permute-start(f32[768,1024]{1,0:T(8,128)S(1)} %get-tuple-element.110), channel_id=1, source_target_pairs={{0,1},{1,0},{2,3},{3,2},{4,5},{5,4},{6,7},{7,6},{8,9},{9,8},{10,11... | collective-permute-start | bytes 9437192 | tf_op jit(solution)/shard_map/ppermute | solution.py:398
  17.1 2.3 %collective-permute-start.5 = (f32[264,128]{1,0:T(8,128)S(1)}, f32[264,128]{1,0:T(8,128)S(1)}, u32[]{:S(2)}, u32[]{:S(2)}) collective-permute-start(f32[264,128]{1,0:T(8,128)S(1)} %shard_map.97), channel_id=1, source_target_pairs={{0,16},{1,17},{2,18},{3,19},{4,20},{5,21},{6,22},{7,23},{8,24},{9,... | collective-permute-start | bytes 405512 | tf_op jit(solution)/shard_map/ppermute | solution.py:408
  19.4 1.3 %collective-permute-start.4 = (f32[264,128]{1,0:T(8,128)S(1)}, f32[264,128]{1,0:T(8,128)S(1)}, u32[]{:S(2)}, u32[]{:S(2)}) collective-permute-start(f32[264,128]{1,0:T(8,128)S(1)} %shard_map.97), channel_id=1, source_target_pairs={{0,8},{1,9},{2,10},{3,11},{4,12},{5,13},{6,14},{7,15},{8,16},{9,17... | collective-permute-start | bytes 405512 | tf_op jit(solution)/shard_map/ppermute | solution.py:408
  20.7 8.2 %collective-permute-done.5.refs_1_ = f32[264,128]{1,0:T(8,128)S(1)} collective-permute-done((f32[264,128]{1,0:T(8,128)S(1)}, f32[264,128]{1,0:T(8,128)S(1)}, u32[]{:S(2)}, u32[]{:S(2)}) %collective-permute-start.5) | collective-permute-done | bytes 135200 | tf_op jit(solution)/shard_map/ppermute | solution.py:408
  28.9 0.7 shard_map.98
  29.7 1.0 %collective-permute-start.6 = (f32[256,128]{1,0:T(8,128)S(1)}, f32[256,128]{1,0:T(8,128)S(1)}, u32[]{:S(2)}, u32[]{:S(2)}) collective-permute-start(f32[256,128]{1,0:T(8,128)S(1)} %get-tuple-element.102), channel_id=1, source_target_pairs={{0,2},{1,3},{2,0},{3,1},{4,6},{5,7},{6,4},{7,5},{8,10},{9,11},{10,... | collective-permute-start | bytes 393224 | tf_op jit(solution)/shard_map/ppermute | solution.py:402
  30.7 0.5 collective-permute-start.7
  31.2 1.2 %collective-permute-start.8 = (f32[256,128]{1,0:T(8,128)S(1)}, f32[256,128]{1,0:T(8,128)S(1)}, u32[]{:S(2)}, u32[]{:S(2)}) collective-permute-start(f32[256,128]{1,0:T(8,128)S(1)} %get-tuple-element.104), channel_id=1, source_target_pairs={{0,6},{1,7},{2,4},{3,5},{4,2},{5,3},{6,0},{7,1},{8,14},{9,15},{10,... | collective-permute-start | bytes 393224 | tf_op jit(solution)/shard_map/ppermute | solution.py:402
  32.4 1.5 %collective-permute-done.6.c1 = f32[256,128]{1,0:T(8,128)S(1)} collective-permute-done((f32[256,128]{1,0:T(8,128)S(1)}, f32[256,128]{1,0:T(8,128)S(1)}, u32[]{:S(2)}, u32[]{:S(2)}) %collective-permute-start.6) | collective-permute-done | bytes 131104 | tf_op jit(solution)/shard_map/ppermute | solution.py:402
  33.9 0.9 %collective-permute-done.7.c2 = f32[256,128]{1,0:T(8,128)S(1)} collective-permute-done((f32[256,128]{1,0:T(8,128)S(1)}, f32[256,128]{1,0:T(8,128)S(1)}, u32[]{:S(2)}, u32[]{:S(2)}) %collective-permute-start.7) | collective-permute-done | bytes 131104 | tf_op jit(solution)/shard_map/ppermute | solution.py:402
  34.8 2.9 %collective-permute-done.8.c3 = f32[256,128]{1,0:T(8,128)S(1)} collective-permute-done((f32[256,128]{1,0:T(8,128)S(1)}, f32[256,128]{1,0:T(8,128)S(1)}, u32[]{:S(2)}, u32[]{:S(2)}) %collective-permute-start.8) | collective-permute-done | bytes 131104 | tf_op jit(solution)/shard_map/ppermute | solution.py:402
  37.7 6.6 %shard_map.99 = (f32[272,128]{1,0:T(8,128)S(1)}, f32[272,128]{1,0:T(8,128)S(1)}, f32[272,128]{1,0:T(8,128)S(1)}, f32[272,128]{1,0:T(8,128)S(1)}, f32[1032,128]{1...) custom-call(s32[1,2]{1,0:T(1,128)S(1)} %copy-done.4, ...), custom_call_target="tpu_custom_call" | custom-call | flops 268435456 | bytes 11853824 | tf_op jit(solution)/shard_map/pallas_call | solution.py:365
  44.2 0.1 collective-permute-start.10
  44.3 1.4 %collective-permute-start.11 = (f32[272,128]{1,0:T(8,128)S(1)}, f32[272,128]{1,0:T(8,128)S(1)}, u32[]{:S(2)}, u32[]{:S(2)}) collective-permute-start(f32[272,128]{1,0:T(8,128)S(1)} %get-tuple-element.114), channel_id=1, source_target_pairs={{0,4},{1,5},{2,6},{3,7},{4,0},{5,1},{6,2},{7,3},{8,12},{9,13},{10,... | collective-permute-start | bytes 417800 | tf_op jit(solution)/shard_map/ppermute | solution.py:402
  45.7 1.2 %collective-permute-start.12 = (f32[272,128]{1,0:T(8,128)S(1)}, f32[272,128]{1,0:T(8,128)S(1)}, u32[]{:S(2)}, u32[]{:S(2)}) collective-permute-start(f32[272,128]{1,0:T(8,128)S(1)} %get-tuple-element.115), channel_id=1, source_target_pairs={{0,6},{1,7},{2,4},{3,5},{4,2},{5,3},{6,0},{7,1},{8,14},{9,15},{10,... | collective-permute-start | bytes 417800 | tf_op jit(solution)/shard_map/ppermute | solution.py:402
  47.0 3.1 %shard_map.100 = (bf16[256,2048]{1,0:T(8,128)(2,1)}, f32[256,1024]{1,0:T(8,128)S(1)}, f32[256,1024]{1,0:T(8,128)S(1)}) custom-call(s32[1,2]{1,0:T(1,128)S(1)} %copy-done.4, bf16[256,2048]{1,0:T(8,128)(2,1)S(1)} %bitcast.21, bf16[256,2048]{1,0:T(8,128)(2,1)S(1)} %bitcast.9, bf16[256,2048]{1,0:T(8,128)(2,1)S(1)} %bitcast.15, ...), custom_call_target="tpu_custom_call" | custom-call | flops 872415232 | bytes 7077888 | tf_op jit(solution)/shard_map/pallas_call | solution.py:365
  50.0 1.7 %collective-permute-done.12.c3 = f32[272,128]{1,0:T(8,128)S(1)} collective-permute-done((f32[272,128]{1,0:T(8,128)S(1)}, f32[272,128]{1,0:T(8,128)S(1)}, u32[]{:S(2)}, u32[]{:S(2)}) %collective-permute-start.12) | collective-permute-done | bytes 139296 | tf_op jit(solution)/shard_map/ppermute | solution.py:402
  51.8 0.6 shard_map.101
  52.4 2.8 %collective-permute-start.13 = (f32[384,1024]{1,0:T(8,128)S(1)}, f32[384,1024]{1,0:T(8,128)S(1)}, u32[]{:S(2)}, u32[]{:S(2)}) collective-permute-start(f32[384,1024]{1,0:T(8,128)S(1)} %get-tuple-element.127), channel_id=1, source_target_pairs={{0,1},{1,0},{2,3},{3,2},{4,5},{5,4},{6,7},{7,6},{8,9},{9,8},{10,11... | collective-permute-start | bytes 4718600 | tf_op jit(solution)/shard_map/ppermute | solution.py:398
  55.2 2.9 %collective-permute-start.15 = (f32[272,128]{1,0:T(8,128)S(1)}, f32[272,128]{1,0:T(8,128)S(1)}, u32[]{:S(2)}, u32[]{:S(2)}) collective-permute-start(f32[272,128]{1,0:T(8,128)S(1)} %get-tuple-element.126), channel_id=1, source_target_pairs={{0,16},{1,17},{2,18},{3,19},{4,20},{5,21},{6,22},{7,23},{8,24},{9,... | collective-permute-start | bytes 417800 | tf_op jit(solution)/shard_map/ppermute | solution.py:408
  58.1 0.2 collective-permute-start.14
  58.2 6.8 %collective-permute-done.15.refs_1_ = f32[272,128]{1,0:T(8,128)S(1)} collective-permute-done((f32[272,128]{1,0:T(8,128)S(1)}, f32[272,128]{1,0:T(8,128)S(1)}, u32[]{:S(2)}, u32[]{:S(2)}) %collective-permute-start.15) | collective-permute-done | bytes 139296 | tf_op jit(solution)/shard_map/ppermute | solution.py:408
  65.1 0.6 collective-permute-done.14.refs_0_
  65.7 0.7 shard_map.102
  66.4 0.7 collective-permute-start.16
  67.1 0.9 %collective-permute-start.17 = (f32[256,128]{1,0:T(8,128)S(1)}, f32[256,128]{1,0:T(8,128)S(1)}, u32[]{:S(2)}, u32[]{:S(2)}) collective-permute-start(f32[256,128]{1,0:T(8,128)S(1)} %get-tuple-element.133), channel_id=1, source_target_pairs={{0,4},{1,5},{2,6},{3,7},{4,0},{5,1},{6,2},{7,3},{8,12},{9,13},{10,... | collective-permute-start | bytes 393224 | tf_op jit(solution)/shard_map/ppermute | solution.py:402
  68.1 1.1 %collective-permute-start.18 = (f32[256,128]{1,0:T(8,128)S(1)}, f32[256,128]{1,0:T(8,128)S(1)}, u32[]{:S(2)}, u32[]{:S(2)}) collective-permute-start(f32[256,128]{1,0:T(8,128)S(1)} %get-tuple-element.134), channel_id=1, source_target_pairs={{0,6},{1,7},{2,4},{3,5},{4,2},{5,3},{6,0},{7,1},{8,14},{9,15},{10,... | collective-permute-start | bytes 393224 | tf_op jit(solution)/shard_map/ppermute | solution.py:402
  69.2 2.6 %collective-permute-start.19 = (f32[8,128]{1,0:T(8,128)S(1)}, f32[8,128]{1,0:T(8,128)S(1)}, u32[]{:S(2)}, u32[]{:S(2)}) collective-permute-start(f32[8,128]{1,0:T(8,128)S(1)} %get-tuple-element.146.refs_2_), channel_id=1, source_target_pairs={{0,8},{1,9},{2,10},{3,11},{4,12},{5,13},{6,14},{7,15},{8,16},{9,17... | collective-permute-start | bytes 12296 | tf_op jit(solution)/shard_map/ppermute | solution.py:408
  71.8 3.1 %shard_map.103 = (bf16[256,2048]{1,0:T(8,128)(2,1)}, f32[256,1024]{1,0:T(8,128)S(1)}, f32[256,1024]{1,0:T(8,128)S(1)}) custom-call(s32[1,2]{1,0:T(1,128)S(1)} %copy-done.4, bf16[256,2048]{1,0:T(8,128)(2,1)S(1)} %bitcast.22, bf16[256,2048]{1,0:T(8,128)(2,1)S(1)} %bitcast.10, bf16[256,2048]{1,0:T(8,128)(2,1)S(1)} %bitcast.16, ...), custom_call_target="tpu_custom_call", output_to_operand_aliasing={{0}: (5, {})} | custom-call | flops 872415232 | bytes 8912896 | tf_op jit(solution)/shard_map/pallas_call | solution.py:365
  74.9 0.0 collective-permute-done.16.c1
  74.9 0.7 shard_map.104
  75.6 1.8 %collective-permute-start.20 = (f32[1032,128]{1,0:T(8,128)S(1)}, f32[1032,128]{1,0:T(8,128)S(1)}, u32[]{:S(2)}, u32[]{:S(2)}) collective-permute-start(f32[1032,128]{1,0:T(8,128)S(1)} %get-tuple-element.147), channel_id=1, source_target_pairs={{0,1},{1,0},{2,3},{3,2},{4,5},{5,4},{6,7},{7,6},{8,9},{9,8},{10,11... | collective-permute-start | bytes 1585160 | tf_op jit(solution)/shard_map/ppermute | solution.py:398
  77.5 1.9 %shard_map.105 = (bf16[256,2048]{1,0:T(8,128)(2,1)}, bf16[256,2048]{1,0:T(8,128)(2,1)}) custom-call(s32[1,2]{1,0:T(1,128)S(1)} %copy-done.4, bf16[256,2048]{1,0:T(8,128)(2,1)S(1)} %bitcast.11, bf16[256,2048]{1,0:T(8,128)(2,1)S(1)} %bitcast.17, f32[256,1024]{1,0:T(8,128)S(1)} %get-tuple-element.120.key_part, f32[256,1024]{1,0:T(8,128)S(1)} %get-tuple-element.121.value_part, ...), custom_call_target="tpu_custom_call" | custom-call | flops 134217728 | bytes 6553600 | tf_op jit(solution)/shard_map/pallas_call | solution.py:365
  79.3 2.5 %shard_map.106 = (bf16[256,2048]{1,0:T(8,128)(2,1)}, bf16[256,2048]{1,0:T(8,128)(2,1)}, f32[16,128]{1,0:T(8,128)}) custom-call(s32[1,2]{1,0:T(1,128)S(1)} %copy-done.4, bf16[256,2048]{1,0:T(8,128)(2,1)S(1)} %bitcast.12, bf16[256,2048]{1,0:T(8,128)(2,1)S(1)} %bitcast.18, ...), custom_call_target="tpu_custom_call", output_to_operand_aliasing={{0}: (7, {}), {1}: (8, {})} | custom-call | flops 134217728 | bytes 8929280 | tf_op jit(solution)/shard_map/pallas_call | solution.py:365
  (20 shorter events, 0.0 us)
Async XLA Ops:
  0.6 8.2 %copy-start.1 = (bf16[1,256,2048]{2,1,0:T(8,128)(2,1)S(1)}, bf16[1,256,2048]{2,1,0:T(8,128)(2,1)}, u32[]{:S(2)}) copy-start(bf16[1,256,2048]{2,1,0:T(8,128)(2,1)} %param.8) | copy-start | bytes 3145732
  0.6 8.1 %copy-start = (bf16[1,256,2048]{2,1,0:T(8,128)(2,1)S(1)}, bf16[1,256,2048]{2,1,0:T(8,128)(2,1)}, u32[]{:S(2)}) copy-start(bf16[1,256,2048]{2,1,0:T(8,128)(2,1)} %param.7) | copy-start | bytes 3145732
  0.7 8.1 %copy-start.3 = (bf16[1,256,2048]{2,1,0:T(8,128)(2,1)S(1)}, bf16[1,256,2048]{2,1,0:T(8,128)(2,1)}, u32[]{:S(2)}) copy-start(bf16[1,256,2048]{2,1,0:T(8,128)(2,1)} %param.9) | copy-start | bytes 3145732
  0.7 8.1 %copy-start.2 = (bf16[1,256,2048]{2,1,0:T(8,128)(2,1)S(1)}, bf16[1,256,2048]{2,1,0:T(8,128)(2,1)}, u32[]{:S(2)}) copy-start(bf16[1,256,2048]{2,1,0:T(8,128)(2,1)} %param.6) | copy-start | bytes 3145732
  2.5 2.0 %collective-permute-start = (f32[1032,128]{1,0:T(8,128)S(1)}, f32[1032,128]{1,0:T(8,128)S(1)}, u32[]{:S(2)}, u32[]{:S(2)}) collective-permute-start(f32[1032,128]{1,0:T(8,128)S(1)} %get-tuple-element.81), channel_id=1, source_target_pairs={{0,1},{1,0},{2,3},{3,2},{4,5},{5,4},{6,7},{7,6},{8,9},{9,8},{10,11... | collective-permute-start | bytes 1585160 | tf_op jit(solution)/shard_map/ppermute | solution.py:398
  2.6 0.7 copy-start.4
  4.1 33.6 %copy-start.5 = (f32[16,128]{1,0:T(8,128)S(1)}, f32[16,128]{1,0:T(8,128)}, u32[]{:S(2)}) copy-start(f32[16,128]{1,0:T(8,128)} %gain.1) | copy-start | bytes 24580
  5.1 7.3 %collective-permute-start.1 = (f32[264,128]{1,0:T(8,128)S(1)}, f32[264,128]{1,0:T(8,128)S(1)}, u32[]{:S(2)}, u32[]{:S(2)}) collective-permute-start(f32[264,128]{1,0:T(8,128)S(1)} %get-tuple-element.89), channel_id=1, source_target_pairs={{0,2},{1,3},{2,0},{3,1},{4,6},{5,7},{6,4},{7,5},{8,10},{9,11},{10,... | collective-permute-start | bytes 405512 | tf_op jit(solution)/shard_map/ppermute | solution.py:402
  7.5 4.8 %collective-permute-start.2 = (f32[264,128]{1,0:T(8,128)S(1)}, f32[264,128]{1,0:T(8,128)S(1)}, u32[]{:S(2)}, u32[]{:S(2)}) collective-permute-start(f32[264,128]{1,0:T(8,128)S(1)} %get-tuple-element.90), channel_id=1, source_target_pairs={{0,4},{1,5},{2,6},{3,7},{4,0},{5,1},{6,2},{7,3},{8,12},{9,13},{10,... | collective-permute-start | bytes 405512 | tf_op jit(solution)/shard_map/ppermute | solution.py:402
  8.8 6.1 %collective-permute-start.3 = (f32[264,128]{1,0:T(8,128)S(1)}, f32[264,128]{1,0:T(8,128)S(1)}, u32[]{:S(2)}, u32[]{:S(2)}) collective-permute-start(f32[264,128]{1,0:T(8,128)S(1)} %get-tuple-element.91), channel_id=1, source_target_pairs={{0,6},{1,7},{2,4},{3,5},{4,2},{5,3},{6,0},{7,1},{8,14},{9,15},{10,... | collective-permute-start | bytes 405512 | tf_op jit(solution)/shard_map/ppermute | solution.py:402
  15.5 22.2 %collective-permute-start.9 = (f32[768,1024]{1,0:T(8,128)S(1)}, f32[768,1024]{1,0:T(8,128)S(1)}, u32[]{:S(2)}, u32[]{:S(2)}) collective-permute-start(f32[768,1024]{1,0:T(8,128)S(1)} %get-tuple-element.110), channel_id=1, source_target_pairs={{0,1},{1,0},{2,3},{3,2},{4,5},{5,4},{6,7},{7,6},{8,9},{9,8},{10,11... | collective-permute-start | bytes 9437192 | tf_op jit(solution)/shard_map/ppermute | solution.py:398
  17.1 11.9 %collective-permute-start.5 = (f32[264,128]{1,0:T(8,128)S(1)}, f32[264,128]{1,0:T(8,128)S(1)}, u32[]{:S(2)}, u32[]{:S(2)}) collective-permute-start(f32[264,128]{1,0:T(8,128)S(1)} %shard_map.97), channel_id=1, source_target_pairs={{0,16},{1,17},{2,18},{3,19},{4,20},{5,21},{6,22},{7,23},{8,24},{9,... | collective-permute-start | bytes 405512 | tf_op jit(solution)/shard_map/ppermute | solution.py:408
  19.4 9.5 %collective-permute-start.4 = (f32[264,128]{1,0:T(8,128)S(1)}, f32[264,128]{1,0:T(8,128)S(1)}, u32[]{:S(2)}, u32[]{:S(2)}) collective-permute-start(f32[264,128]{1,0:T(8,128)S(1)} %shard_map.97), channel_id=1, source_target_pairs={{0,8},{1,9},{2,10},{3,11},{4,12},{5,13},{6,14},{7,15},{8,16},{9,17... | collective-permute-start | bytes 405512 | tf_op jit(solution)/shard_map/ppermute | solution.py:408
  29.7 4.2 %collective-permute-start.6 = (f32[256,128]{1,0:T(8,128)S(1)}, f32[256,128]{1,0:T(8,128)S(1)}, u32[]{:S(2)}, u32[]{:S(2)}) collective-permute-start(f32[256,128]{1,0:T(8,128)S(1)} %get-tuple-element.102), channel_id=1, source_target_pairs={{0,2},{1,3},{2,0},{3,1},{4,6},{5,7},{6,4},{7,5},{8,10},{9,11},{10,... | collective-permute-start | bytes 393224 | tf_op jit(solution)/shard_map/ppermute | solution.py:402
  30.7 4.1 %collective-permute-start.7 = (f32[256,128]{1,0:T(8,128)S(1)}, f32[256,128]{1,0:T(8,128)S(1)}, u32[]{:S(2)}, u32[]{:S(2)}) collective-permute-start(f32[256,128]{1,0:T(8,128)S(1)} %get-tuple-element.103), channel_id=1, source_target_pairs={{0,4},{1,5},{2,6},{3,7},{4,0},{5,1},{6,2},{7,3},{8,12},{9,13},{10,... | collective-permute-start | bytes 393224 | tf_op jit(solution)/shard_map/ppermute | solution.py:402
  31.2 6.4 %collective-permute-start.8 = (f32[256,128]{1,0:T(8,128)S(1)}, f32[256,128]{1,0:T(8,128)S(1)}, u32[]{:S(2)}, u32[]{:S(2)}) collective-permute-start(f32[256,128]{1,0:T(8,128)S(1)} %get-tuple-element.104), channel_id=1, source_target_pairs={{0,6},{1,7},{2,4},{3,5},{4,2},{5,3},{6,0},{7,1},{8,14},{9,15},{10,... | collective-permute-start | bytes 393224 | tf_op jit(solution)/shard_map/ppermute | solution.py:402
  44.2 5.8 %collective-permute-start.10 = (f32[272,128]{1,0:T(8,128)S(1)}, f32[272,128]{1,0:T(8,128)S(1)}, u32[]{:S(2)}, u32[]{:S(2)}) collective-permute-start(f32[272,128]{1,0:T(8,128)S(1)} %get-tuple-element.113), channel_id=1, source_target_pairs={{0,2},{1,3},{2,0},{3,1},{4,6},{5,7},{6,4},{7,5},{8,10},{9,11},{10,... | collective-permute-start | bytes 417800 | tf_op jit(solution)/shard_map/ppermute | solution.py:402
  44.3 5.7 %collective-permute-start.11 = (f32[272,128]{1,0:T(8,128)S(1)}, f32[272,128]{1,0:T(8,128)S(1)}, u32[]{:S(2)}, u32[]{:S(2)}) collective-permute-start(f32[272,128]{1,0:T(8,128)S(1)} %get-tuple-element.114), channel_id=1, source_target_pairs={{0,4},{1,5},{2,6},{3,7},{4,0},{5,1},{6,2},{7,3},{8,12},{9,13},{10,... | collective-permute-start | bytes 417800 | tf_op jit(solution)/shard_map/ppermute | solution.py:402
  45.7 6.0 %collective-permute-start.12 = (f32[272,128]{1,0:T(8,128)S(1)}, f32[272,128]{1,0:T(8,128)S(1)}, u32[]{:S(2)}, u32[]{:S(2)}) collective-permute-start(f32[272,128]{1,0:T(8,128)S(1)} %get-tuple-element.115), channel_id=1, source_target_pairs={{0,6},{1,7},{2,4},{3,5},{4,2},{5,3},{6,0},{7,1},{8,14},{9,15},{10,... | collective-permute-start | bytes 417800 | tf_op jit(solution)/shard_map/ppermute | solution.py:402
  52.4 19.4 %collective-permute-start.13 = (f32[384,1024]{1,0:T(8,128)S(1)}, f32[384,1024]{1,0:T(8,128)S(1)}, u32[]{:S(2)}, u32[]{:S(2)}) collective-permute-start(f32[384,1024]{1,0:T(8,128)S(1)} %get-tuple-element.127), channel_id=1, source_target_pairs={{0,1},{1,0},{2,3},{3,2},{4,5},{5,4},{6,7},{7,6},{8,9},{9,8},{10,11... | collective-permute-start | bytes 4718600 | tf_op jit(solution)/shard_map/ppermute | solution.py:398
  55.2 9.9 %collective-permute-start.15 = (f32[272,128]{1,0:T(8,128)S(1)}, f32[272,128]{1,0:T(8,128)S(1)}, u32[]{:S(2)}, u32[]{:S(2)}) collective-permute-start(f32[272,128]{1,0:T(8,128)S(1)} %get-tuple-element.126), channel_id=1, source_target_pairs={{0,16},{1,17},{2,18},{3,19},{4,20},{5,21},{6,22},{7,23},{8,24},{9,... | collective-permute-start | bytes 417800 | tf_op jit(solution)/shard_map/ppermute | solution.py:408
  58.1 7.6 %collective-permute-start.14 = (f32[272,128]{1,0:T(8,128)S(1)}, f32[272,128]{1,0:T(8,128)S(1)}, u32[]{:S(2)}, u32[]{:S(2)}) collective-permute-start(f32[272,128]{1,0:T(8,128)S(1)} %get-tuple-element.126), channel_id=1, source_target_pairs={{0,24},{1,25},{2,26},{3,27},{4,28},{5,29},{6,30},{7,31},{8,0},{9,1... | collective-permute-start | bytes 417800 | tf_op jit(solution)/shard_map/ppermute | solution.py:408
  66.4 8.4 %collective-permute-start.16 = (f32[256,128]{1,0:T(8,128)S(1)}, f32[256,128]{1,0:T(8,128)S(1)}, u32[]{:S(2)}, u32[]{:S(2)}) collective-permute-start(f32[256,128]{1,0:T(8,128)S(1)} %get-tuple-element.132), channel_id=1, source_target_pairs={{0,2},{1,3},{2,0},{3,1},{4,6},{5,7},{6,4},{7,5},{8,10},{9,11},{10,... | collective-permute-start | bytes 393224 | tf_op jit(solution)/shard_map/ppermute | solution.py:402
  67.1 7.7 %collective-permute-start.17 = (f32[256,128]{1,0:T(8,128)S(1)}, f32[256,128]{1,0:T(8,128)S(1)}, u32[]{:S(2)}, u32[]{:S(2)}) collective-permute-start(f32[256,128]{1,0:T(8,128)S(1)} %get-tuple-element.133), channel_id=1, source_target_pairs={{0,4},{1,5},{2,6},{3,7},{4,0},{5,1},{6,2},{7,3},{8,12},{9,13},{10,... | collective-permute-start | bytes 393224 | tf_op jit(solution)/shard_map/ppermute | solution.py:402
  68.1 6.8 %collective-permute-start.18 = (f32[256,128]{1,0:T(8,128)S(1)}, f32[256,128]{1,0:T(8,128)S(1)}, u32[]{:S(2)}, u32[]{:S(2)}) collective-permute-start(f32[256,128]{1,0:T(8,128)S(1)} %get-tuple-element.134), channel_id=1, source_target_pairs={{0,6},{1,7},{2,4},{3,5},{4,2},{5,3},{6,0},{7,1},{8,14},{9,15},{10,... | collective-permute-start | bytes 393224 | tf_op jit(solution)/shard_map/ppermute | solution.py:402
  69.2 5.7 %collective-permute-start.19 = (f32[8,128]{1,0:T(8,128)S(1)}, f32[8,128]{1,0:T(8,128)S(1)}, u32[]{:S(2)}, u32[]{:S(2)}) collective-permute-start(f32[8,128]{1,0:T(8,128)S(1)} %get-tuple-element.146.refs_2_), channel_id=1, source_target_pairs={{0,8},{1,9},{2,10},{3,11},{4,12},{5,13},{6,14},{7,15},{8,16},{9,17... | collective-permute-start | bytes 12296 | tf_op jit(solution)/shard_map/ppermute | solution.py:408
  75.6 3.7 %collective-permute-start.20 = (f32[1032,128]{1,0:T(8,128)S(1)}, f32[1032,128]{1,0:T(8,128)S(1)}, u32[]{:S(2)}, u32[]{:S(2)}) collective-permute-start(f32[1032,128]{1,0:T(8,128)S(1)} %get-tuple-element.147), channel_id=1, source_target_pairs={{0,1},{1,0},{2,3},{3,2},{4,5},{5,4},{6,7},{7,6},{8,9},{9,8},{10,11... | collective-permute-start | bytes 1585160 | tf_op jit(solution)/shard_map/ppermute | solution.py:398

commit v3 on v2

--- a/solution.py
+++ b/solution.py
@@ -83,12 +83,19 @@
     return pl.ds(pl.multiple_of((base + head) * 128, 128), 128)
 
 
+def batches(total, most):
+    most = most if total % most == 0 else 1
+    return [range(start, start + most) for start in range(0, total, most)]
+
+
 def element(docs, key, value, out, first_col, half):
     weight = column(docs, False, BF16)
     write_ids(docs, out, half * 128, False)
-    for head in range(half):
-        at = wide(first_col, head)
-        out[pl.ds(head * 128, 128), :] = dot(key[:, at] * weight, value[:, at], 0, 0)
+    for heads in batches(half, 4):
+        columns = [wide(first_col, head) for head in heads]
+        states = [dot(key[:, at] * weight, value[:, at], 0, 0) for at in columns]
+        for head, state in zip(heads, states):
+            out[pl.ds(head * 128, 128), :] = state
 
 
 def first_kernel(docs, key, value, out, key_own, value_own, docs_held, key_held, value_held, sems, *, half):
@@ -120,33 +127,31 @@
     tokens = query.shape[0]
     for other in (True, False):
         base = (1 - my_core() if other else my_core()) * half
-        for head in range(half):
-            full, cols = wide(base, head), pl.ds(head * 128, 128)
-            q = query[:, full]
-            scores = lower(dot(q, key[:, full], 1, 1), both)
-            part = times_lower(scores, value[:, full])
-            if other:
-                message[pl.ds(0, tokens), cols] = q.astype(F32)
-                message[pl.ds(tokens, tokens), cols] = grad[:, full].astype(F32)
-                message[pl.ds(2 * tokens, tokens), cols] = part
-            else:
-                own[:, cols] = part
-
-
-def channel_mean(table):
-    high = table.astype(BF16)
-    low = (table - high.astype(F32)).astype(BF16)
-    return dot(jnp.concatenate([high, low], 1), jnp.full((256, 128), 1.0 / 128, BF16), 1, 0)
+        for heads in batches(half, 2):
+            results = []
+            for head in heads:
+                full = wide(base, head)
+                q = query[:, full]
+                scores = lower(dot(q, key[:, full], 1, 1), both)
+                part = times_lower(scores, value[:, full])
+                results.append((q.astype(F32), grad[:, full].astype(F32), part) if other else (part,))
+            for head, parts in zip(heads, results):
+                cols = pl.ds(head * 128, 128)
+                if other:
+                    for at, part in enumerate(parts):
+                        message[pl.ds(at * tokens, tokens), cols] = part
+                else:
+                    own[:, cols] = parts[0]
 
 
 def attend(q, g, intra, state, gain, joined):
     inter = dot(q, state, 1, 0)
     attended = intra + jnp.concatenate([inter[:BLK], inter[BLK:] * joined], 0)
-    inv_rms = lax.rsqrt(channel_mean(attended * attended) + EPSILON)
+    inv_rms = lax.rsqrt(jnp.mean(attended * attended, -1, keepdims=True) + EPSILON)
     scaled = g * gain
     normed = attended * inv_rms
     terms = jnp.sum(g * normed, 0, keepdims=True)
-    mean = channel_mean(scaled * normed)
+    mean = jnp.mean(scaled * normed, -1, keepdims=True)
     attn = (inv_rms * (scaled - normed * mean)).astype(BF16)
     back = dot(q[:BLK], attn[:BLK], 0, 0) + dot(q[BLK:], attn[BLK:], 0, 0) * joined
     return attn, back, terms
@@ -178,21 +183,18 @@
         up[pl.ds(size + FIRST, 1), :] = -last
         up[pl.ds(size + LAST, 1), :] = -first
     for turn, chip in enumerate((c0, c1, c2, c3)):
+        results = []
         for step in range(chunk):
             head = lax.bitwise_xor(my_chip(), turn) * chunk + step
             cols, full = wide(0, head), wide(base, head)
             coming = chip[pl.ds(step * 128, 128), :]
             state = (coming * keep_coming + other[cols, :] * keep_other).astype(BF16)
-            state_own[cols, :] = state
             state_other = coming * send_coming + own[cols, :] * send_own
-            reply[pl.ds(tokens, 128), cols] = state_other
             weights = gain[pl.ds(base + head, 1), :]
-            attn, back, terms = attend(
+            near = attend(
                 query[:, full], grad[:, full].astype(F32), intra[:, cols], state, weights, own_joined
             )
-            attn_own[:, cols] = attn
-            back_own[cols, :] = back
-            attn, back_far, terms_far = attend(
+            far = attend(
                 message[pl.ds(0, tokens), cols].astype(BF16),
                 message[pl.ds(tokens, tokens), cols],
                 message[pl.ds(2 * tokens, tokens), cols],
@@ -200,7 +202,15 @@
                 weights,
                 other_joined,
             )
-            reply[pl.ds(0, tokens), cols] = attn.astype(F32)
+            results.append((head, cols, state, state_other, near, far))
+        for step, (head, cols, state, state_other, near, far) in enumerate(results):
+            attn, back, terms = near
+            attn_far, back_far, terms_far = far
+            state_own[cols, :] = state
+            reply[pl.ds(tokens, 128), cols] = state_other
+            attn_own[:, cols] = attn
+            back_own[cols, :] = back
+            reply[pl.ds(0, tokens), cols] = attn_far.astype(F32)
             back_other[cols, :] = back_far
             ups[turn][pl.ds(step * 128, 128), :] = back * own_weight + back_far * other_weight
             for up in ups:
@@ -214,22 +224,32 @@
     enter32 = column(docs, True, F32)
     base = (1 - my_core() if other else my_core()) * half
     copies = []
-    for head in range(half):
-        cols = pl.ds(head * 128, 128)
-        full = wide(base, head)
-        q, k, v = query[:, full], key[:, full], value[:, full]
-        if other:
-            a = refs[0][pl.ds(0, tokens), cols].astype(BF16)
-            state = refs[0][pl.ds(tokens, 128), cols].astype(BF16)
-        else:
-            a, state = refs[0][:, cols], refs[1][cols, :]
-        pair = lower(dot(a, v, 1, 1), both)
-        cross = enter32 * dot(a, state, 1, 1)
-        held[:, cols] = (cross + times_lower(pair, k)).astype(BF16)
-        key_part[:, cols] = times_higher(higher(dot(v, a, 1, 1), both), q)
-        value_part[:, cols] = times_higher(higher(dot(k, q, 1, 1), both), a)
-        copies.append(pltpu.make_async_copy(held.at[:, cols], query_grad.at[:, full], sems.at[head]))
-        copies[-1].start()
+    for heads in batches(half, 2):
+        results = []
+        for head in heads:
+            cols, full = pl.ds(head * 128, 128), wide(base, head)
+            q, k, v = query[:, full], key[:, full], value[:, full]
+            if other:
+                a = refs[0][pl.ds(0, tokens), cols].astype(BF16)
+                state = refs[0][pl.ds(tokens, 128), cols].astype(BF16)
+            else:
+                a, state = refs[0][:, cols], refs[1][cols, :]
+            pair = lower(dot(a, v, 1, 1), both)
+            cross = enter32 * dot(a, state, 1, 1)
+            results.append(
+                (
+                    (cross + times_lower(pair, k)).astype(BF16),
+                    times_higher(higher(dot(v, a, 1, 1), both), q),
+                    times_higher(higher(dot(k, q, 1, 1), both), a),
+                )
+            )
+        for head, (query_part, key_term, value_term) in zip(heads, results):
+            cols, full = pl.ds(head * 128, 128), wide(base, head)
+            held[:, cols] = query_part
+            copies.append(pltpu.make_async_copy(held.at[:, cols], query_grad.at[:, full], sems.at[head]))
+            copies[-1].start()
+            key_part[:, cols] = key_term
+            value_part[:, cols] = value_term
     for copy in copies:
         copy.wait()
 
@@ -245,16 +265,25 @@
     leave = column(docs, False, F32)
     base = (1 - my_core() if other else my_core()) * half
     copies = []
-    for head in range(half):
-        cols = pl.ds(head * 128, 128)
-        full = wide(base, head)
-        g = state[cols, :].astype(BF16)
-        key_held[:, cols] = (key_part[:, cols] + leave * dot(value[:, full], g, 1, 1)).astype(BF16)
-        value_held[:, cols] = (value_part[:, cols] + leave * dot(key[:, full], g, 1, 0)).astype(BF16)
-        copies.append(pltpu.make_async_copy(key_held.at[:, cols], key_grad.at[:, full], sems.at[0, head]))
-        copies.append(pltpu.make_async_copy(value_held.at[:, cols], value_grad.at[:, full], sems.at[1, head]))
-        copies[-2].start()
-        copies[-1].start()
+    for heads in batches(half, 4):
+        results = []
+        for head in heads:
+            cols, full = pl.ds(head * 128, 128), wide(base, head)
+            g = state[cols, :].astype(BF16)
+            results.append(
+                (
+                    (key_part[:, cols] + leave * dot(value[:, full], g, 1, 1)).astype(BF16),
+                    (value_part[:, cols] + leave * dot(key[:, full], g, 1, 0)).astype(BF16),
+                )
+            )
+        for head, (key_sum, value_sum) in zip(heads, results):
+            cols, full = pl.ds(head * 128, 128), wide(base, head)
+            key_held[:, cols] = key_sum
+            value_held[:, cols] = value_sum
+            copies.append(pltpu.make_async_copy(key_held.at[:, cols], key_grad.at[:, full], sems.at[0, head]))
+            copies.append(pltpu.make_async_copy(value_held.at[:, cols], value_grad.at[:, full], sems.at[1, head]))
+            copies[-2].start()
+            copies[-1].start()
     for copy in copies:
         copy.wait()
 

time: 82.1 us -> 78.9 us (0.961)
  Pallas kernels: 27.2 us -> 24 us
    pallas_call x13, Pallas kernels: 25.5 us -> 22.2 us  [call(): pl.pallas_call(kernel, out_shape=outs, grid_spec=pltpu.PrefetchScalarGrid...]
  transfers between devices with their start and end apart: 21 -> 21, of which waited for: 9 -> 9; matrix products, arithmetic and copies ran while one was open for 0% -> 0% of each run, Pallas kernels for 17% -> 18%
where the time goes in v3:
time: 78.9 us; the launch traced here: 78.7 us
  starting transfers between devices  27.6 us (35%)
  waiting for transfers between devices  25.5 us (32%)
  Pallas kernels  24 us (30%)
  between operations  1.01 us (1%)
    pallas_call x13, Pallas kernels, call(): pl.pallas_call(kernel, out_shape=outs, grid_spec=pltpu.PrefetchScalarGrid...  22.2 us
    ppermute x5, waiting for transfers between devices, around(): return lax.ppermute(value, 'ctx', pairs)  15.7 us
    ppermute x12, starting transfers between devices, to_chips(): lax.ppermute(values[turn], 'ctx', [(i, i ^ 2 * turn) for i in range(shard...  11.8 us
    ppermute x12, waiting for transfers between devices, to_chips(): lax.ppermute(values[turn], 'ctx', [(i, i ^ 2 * turn) for i in range(shard...  9.45 us
    ppermute x5, starting transfers between devices, around(): return lax.ppermute(value, 'ctx', pairs)  9.35 us
    ppermute x4, starting transfers between devices, swap(): return lax.ppermute(value, 'ctx', [(i, i ^ 1) for i in range(shards)])  6.4 us
    pallas_call x1, Pallas kernels, local(): pl.pallas_call(functools.partial(first_kernel, half=half), out_shape=[pay...  1.77 us
  transfers between devices with their start and end apart: 21, of which 9 were waited for; matrix products, arithmetic and copies ran while one was open for 0% of the time, Pallas kernels for 18%

profile of v3, /device:TPU:1, one launch (start us, length us, event | category | flops | bytes accessed | tf_op | source)
XLA Modules:
  0.0 78.7 jit_solution(7364804734203615527)
XLA Ops:
  0.7 1.8 %shard_map.93 = (f32[1032,128]{1,0:T(8,128)S(1)}, bf16[256,1024]{1,0:T(8,128)(2,1)S(1)}, bf16[256,1024]{1,0:T(8,128)(2,1)S(1)}) custom-call(s32[1,2]{1,0:T(1,128)} %docs.14, bf16[256,2048]{1,0:T(8,128)(2,1)} %bitcast.7, bf16[256,2048]{1,0:T(8,128)(2,1)} %bitcast.13), custom_call_target="tpu_custom_call" | custom-call | flops 67108864 | bytes 2097152 | tf_op jit(solution)/shard_map/pallas_call | solution.py:496
  2.5 0.1 collective-permute-start
  2.6 0.7 copy-done.4
  3.2 0.9 %shard_map.94.own = f32[1032,128]{1,0:T(8,128)S(1)} custom-call(s32[1,2]{1,0:T(1,128)S(1)} %copy-done.4, bf16[256,1024]{1,0:T(8,128)(2,1)S(1)} %get-tuple-element.86.key, bf16[256,1024]{1,0:T(8,128)(2,1)S(1)} %get-tuple-element.87.value), custom_call_target="tpu_custom_call" | custom-call | flops 67108864 | bytes 1576960 | tf_op jit(solution)/shard_map/pallas_call | solution.py:394
  4.1 0.0 copy-start.5
  4.1 0.3 collective-permute-done.other
  4.4 0.6 shard_map.95
  5.1 2.4 %collective-permute-start.1 = (f32[264,128]{1,0:T(8,128)S(1)}, f32[264,128]{1,0:T(8,128)S(1)}, u32[]{:S(2)}, u32[]{:S(2)}) collective-permute-start(f32[264,128]{1,0:T(8,128)S(1)} %get-tuple-element.89), channel_id=1, source_target_pairs={{0,2},{1,3},{2,0},{3,1},{4,6},{5,7},{6,4},{7,5},{8,10},{9,11},{10,... | collective-permute-start | bytes 405512 | tf_op jit(solution)/shard_map/ppermute | solution.py:431
  7.5 1.2 %collective-permute-start.2 = (f32[264,128]{1,0:T(8,128)S(1)}, f32[264,128]{1,0:T(8,128)S(1)}, u32[]{:S(2)}, u32[]{:S(2)}) collective-permute-start(f32[264,128]{1,0:T(8,128)S(1)} %get-tuple-element.90), channel_id=1, source_target_pairs={{0,4},{1,5},{2,6},{3,7},{4,0},{5,1},{6,2},{7,3},{8,12},{9,13},{10,... | collective-permute-start | bytes 405512 | tf_op jit(solution)/shard_map/ppermute | solution.py:431
  8.8 0.0 collective-permute-start.3
  8.8 3.6 %shard_map.96 = (f32[256,1024]{1,0:T(8,128)S(1)}, f32[768,1024]{1,0:T(8,128)S(1)}) custom-call(s32[1,2]{1,0:T(1,128)S(1)} %copy-done.4, bf16[256,2048]{1,0:T(8,128)(2,1)S(1)} %bitcast.19, bf16[256,2048]{1,0:T(8,128)(2,1)S(1)} %bitcast.8, bf16[256,2048]{1,0:T(8,128)(2,1)S(1)} %bitcast.14, bf16[256,2048]{1,0:T(8,128)(2,1)S(1)} %bitcast.23), custom_call_target="tpu_custom_call" | custom-call | flops 536870912 | bytes 8388608 | tf_op jit(solution)/shard_map/pallas_call | solution.py:394
  12.4 0.0 collective-permute-done.1.c1
  12.4 0.0 collective-permute-done.2.c2
  12.4 2.5 %collective-permute-done.3.c3 = f32[264,128]{1,0:T(8,128)S(1)} collective-permute-done((f32[264,128]{1,0:T(8,128)S(1)}, f32[264,128]{1,0:T(8,128)S(1)}, u32[]{:S(2)}, u32[]{:S(2)}) %collective-permute-start.3) | collective-permute-done | bytes 135200 | tf_op jit(solution)/shard_map/ppermute | solution.py:431
  14.9 0.6 shard_map.97
  15.5 1.6 %collective-permute-start.9 = (f32[768,1024]{1,0:T(8,128)S(1)}, f32[768,1024]{1,0:T(8,128)S(1)}, u32[]{:S(2)}, u32[]{:S(2)}) collective-permute-start(f32[768,1024]{1,0:T(8,128)S(1)} %get-tuple-element.110), channel_id=1, source_target_pairs={{0,1},{1,0},{2,3},{3,2},{4,5},{5,4},{6,7},{7,6},{8,9},{9,8},{10,11... | collective-permute-start | bytes 9437192 | tf_op jit(solution)/shard_map/ppermute | solution.py:427
  17.1 2.3 %collective-permute-start.5 = (f32[264,128]{1,0:T(8,128)S(1)}, f32[264,128]{1,0:T(8,128)S(1)}, u32[]{:S(2)}, u32[]{:S(2)}) collective-permute-start(f32[264,128]{1,0:T(8,128)S(1)} %shard_map.97), channel_id=1, source_target_pairs={{0,16},{1,17},{2,18},{3,19},{4,20},{5,21},{6,22},{7,23},{8,24},{9,... | collective-permute-start | bytes 405512 | tf_op jit(solution)/shard_map/ppermute | solution.py:437
  19.4 1.3 %collective-permute-start.4 = (f32[264,128]{1,0:T(8,128)S(1)}, f32[264,128]{1,0:T(8,128)S(1)}, u32[]{:S(2)}, u32[]{:S(2)}) collective-permute-start(f32[264,128]{1,0:T(8,128)S(1)} %shard_map.97), channel_id=1, source_target_pairs={{0,8},{1,9},{2,10},{3,11},{4,12},{5,13},{6,14},{7,15},{8,16},{9,17... | collective-permute-start | bytes 405512 | tf_op jit(solution)/shard_map/ppermute | solution.py:437
  20.7 8.2 %collective-permute-done.5.refs_1_ = f32[264,128]{1,0:T(8,128)S(1)} collective-permute-done((f32[264,128]{1,0:T(8,128)S(1)}, f32[264,128]{1,0:T(8,128)S(1)}, u32[]{:S(2)}, u32[]{:S(2)}) %collective-permute-start.5) | collective-permute-done | bytes 135200 | tf_op jit(solution)/shard_map/ppermute | solution.py:437
  28.9 0.7 shard_map.98
  29.7 1.0 %collective-permute-start.6 = (f32[256,128]{1,0:T(8,128)S(1)}, f32[256,128]{1,0:T(8,128)S(1)}, u32[]{:S(2)}, u32[]{:S(2)}) collective-permute-start(f32[256,128]{1,0:T(8,128)S(1)} %get-tuple-element.102), channel_id=1, source_target_pairs={{0,2},{1,3},{2,0},{3,1},{4,6},{5,7},{6,4},{7,5},{8,10},{9,11},{10,... | collective-permute-start | bytes 393224 | tf_op jit(solution)/shard_map/ppermute | solution.py:431
  30.7 0.5 collective-permute-start.7
  31.2 1.2 %collective-permute-start.8 = (f32[256,128]{1,0:T(8,128)S(1)}, f32[256,128]{1,0:T(8,128)S(1)}, u32[]{:S(2)}, u32[]{:S(2)}) collective-permute-start(f32[256,128]{1,0:T(8,128)S(1)} %get-tuple-element.104), channel_id=1, source_target_pairs={{0,6},{1,7},{2,4},{3,5},{4,2},{5,3},{6,0},{7,1},{8,14},{9,15},{10,... | collective-permute-start | bytes 393224 | tf_op jit(solution)/shard_map/ppermute | solution.py:431
  32.4 1.5 %collective-permute-done.6.c1 = f32[256,128]{1,0:T(8,128)S(1)} collective-permute-done((f32[256,128]{1,0:T(8,128)S(1)}, f32[256,128]{1,0:T(8,128)S(1)}, u32[]{:S(2)}, u32[]{:S(2)}) %collective-permute-start.6) | collective-permute-done | bytes 131104 | tf_op jit(solution)/shard_map/ppermute | solution.py:431
  33.9 0.9 %collective-permute-done.7.c2 = f32[256,128]{1,0:T(8,128)S(1)} collective-permute-done((f32[256,128]{1,0:T(8,128)S(1)}, f32[256,128]{1,0:T(8,128)S(1)}, u32[]{:S(2)}, u32[]{:S(2)}) %collective-permute-start.7) | collective-permute-done | bytes 131104 | tf_op jit(solution)/shard_map/ppermute | solution.py:431
  34.8 2.9 %collective-permute-done.8.c3 = f32[256,128]{1,0:T(8,128)S(1)} collective-permute-done((f32[256,128]{1,0:T(8,128)S(1)}, f32[256,128]{1,0:T(8,128)S(1)}, u32[]{:S(2)}, u32[]{:S(2)}) %collective-permute-start.8) | collective-permute-done | bytes 131104 | tf_op jit(solution)/shard_map/ppermute | solution.py:431
  37.7 3.3 %shard_map.99 = (f32[272,128]{1,0:T(8,128)S(1)}, f32[272,128]{1,0:T(8,128)S(1)}, f32[272,128]{1,0:T(8,128)S(1)}, f32[272,128]{1,0:T(8,128)S(1)}, f32[1032,128]{1...) custom-call(s32[1,2]{1,0:T(1,128)S(1)} %copy-done.4, ...), custom_call_target="tpu_custom_call" | custom-call | flops 268435456 | bytes 11853824 | tf_op jit(solution)/shard_map/pallas_call | solution.py:394
  41.0 0.1 collective-permute-start.10
  41.0 1.4 %collective-permute-start.11 = (f32[272,128]{1,0:T(8,128)S(1)}, f32[272,128]{1,0:T(8,128)S(1)}, u32[]{:S(2)}, u32[]{:S(2)}) collective-permute-start(f32[272,128]{1,0:T(8,128)S(1)} %get-tuple-element.114), channel_id=1, source_target_pairs={{0,4},{1,5},{2,6},{3,7},{4,0},{5,1},{6,2},{7,3},{8,12},{9,13},{10,... | collective-permute-start | bytes 417800 | tf_op jit(solution)/shard_map/ppermute | solution.py:431
  42.4 1.2 %collective-permute-start.12 = (f32[272,128]{1,0:T(8,128)S(1)}, f32[272,128]{1,0:T(8,128)S(1)}, u32[]{:S(2)}, u32[]{:S(2)}) collective-permute-start(f32[272,128]{1,0:T(8,128)S(1)} %get-tuple-element.115), channel_id=1, source_target_pairs={{0,6},{1,7},{2,4},{3,5},{4,2},{5,3},{6,0},{7,1},{8,14},{9,15},{10,... | collective-permute-start | bytes 417800 | tf_op jit(solution)/shard_map/ppermute | solution.py:431
  43.7 3.1 %shard_map.100 = (bf16[256,2048]{1,0:T(8,128)(2,1)}, f32[256,1024]{1,0:T(8,128)S(1)}, f32[256,1024]{1,0:T(8,128)S(1)}) custom-call(s32[1,2]{1,0:T(1,128)S(1)} %copy-done.4, bf16[256,2048]{1,0:T(8,128)(2,1)S(1)} %bitcast.21, bf16[256,2048]{1,0:T(8,128)(2,1)S(1)} %bitcast.9, bf16[256,2048]{1,0:T(8,128)(2,1)S(1)} %bitcast.15, ...), custom_call_target="tpu_custom_call" | custom-call | flops 872415232 | bytes 7077888 | tf_op jit(solution)/shard_map/pallas_call | solution.py:394
  46.8 1.6 %collective-permute-done.12.c3 = f32[272,128]{1,0:T(8,128)S(1)} collective-permute-done((f32[272,128]{1,0:T(8,128)S(1)}, f32[272,128]{1,0:T(8,128)S(1)}, u32[]{:S(2)}, u32[]{:S(2)}) %collective-permute-start.12) | collective-permute-done | bytes 139296 | tf_op jit(solution)/shard_map/ppermute | solution.py:431
  48.4 0.6 shard_map.101
  49.0 2.9 %collective-permute-start.13 = (f32[384,1024]{1,0:T(8,128)S(1)}, f32[384,1024]{1,0:T(8,128)S(1)}, u32[]{:S(2)}, u32[]{:S(2)}) collective-permute-start(f32[384,1024]{1,0:T(8,128)S(1)} %get-tuple-element.127), channel_id=1, source_target_pairs={{0,1},{1,0},{2,3},{3,2},{4,5},{5,4},{6,7},{7,6},{8,9},{9,8},{10,11... | collective-permute-start | bytes 4718600 | tf_op jit(solution)/shard_map/ppermute | solution.py:427
  51.9 2.9 %collective-permute-start.15 = (f32[272,128]{1,0:T(8,128)S(1)}, f32[272,128]{1,0:T(8,128)S(1)}, u32[]{:S(2)}, u32[]{:S(2)}) collective-permute-start(f32[272,128]{1,0:T(8,128)S(1)} %get-tuple-element.126), channel_id=1, source_target_pairs={{0,16},{1,17},{2,18},{3,19},{4,20},{5,21},{6,22},{7,23},{8,24},{9,... | collective-permute-start | bytes 417800 | tf_op jit(solution)/shard_map/ppermute | solution.py:437
  54.8 0.2 collective-permute-start.14
  54.9 6.8 %collective-permute-done.15.refs_1_ = f32[272,128]{1,0:T(8,128)S(1)} collective-permute-done((f32[272,128]{1,0:T(8,128)S(1)}, f32[272,128]{1,0:T(8,128)S(1)}, u32[]{:S(2)}, u32[]{:S(2)}) %collective-permute-start.15) | collective-permute-done | bytes 139296 | tf_op jit(solution)/shard_map/ppermute | solution.py:437
  61.8 0.6 collective-permute-done.14.refs_0_
  62.4 0.7 shard_map.102
  63.2 0.7 collective-permute-start.16
  63.9 0.9 %collective-permute-start.17 = (f32[256,128]{1,0:T(8,128)S(1)}, f32[256,128]{1,0:T(8,128)S(1)}, u32[]{:S(2)}, u32[]{:S(2)}) collective-permute-start(f32[256,128]{1,0:T(8,128)S(1)} %get-tuple-element.133), channel_id=1, source_target_pairs={{0,4},{1,5},{2,6},{3,7},{4,0},{5,1},{6,2},{7,3},{8,12},{9,13},{10,... | collective-permute-start | bytes 393224 | tf_op jit(solution)/shard_map/ppermute | solution.py:431
  64.8 1.1 %collective-permute-start.18 = (f32[256,128]{1,0:T(8,128)S(1)}, f32[256,128]{1,0:T(8,128)S(1)}, u32[]{:S(2)}, u32[]{:S(2)}) collective-permute-start(f32[256,128]{1,0:T(8,128)S(1)} %get-tuple-element.134), channel_id=1, source_target_pairs={{0,6},{1,7},{2,4},{3,5},{4,2},{5,3},{6,0},{7,1},{8,14},{9,15},{10,... | collective-permute-start | bytes 393224 | tf_op jit(solution)/shard_map/ppermute | solution.py:431
  65.9 2.6 %collective-permute-start.19 = (f32[8,128]{1,0:T(8,128)S(1)}, f32[8,128]{1,0:T(8,128)S(1)}, u32[]{:S(2)}, u32[]{:S(2)}) collective-permute-start(f32[8,128]{1,0:T(8,128)S(1)} %get-tuple-element.146.refs_2_), channel_id=1, source_target_pairs={{0,8},{1,9},{2,10},{3,11},{4,12},{5,13},{6,14},{7,15},{8,16},{9,17... | collective-permute-start | bytes 12296 | tf_op jit(solution)/shard_map/ppermute | solution.py:437
  68.5 3.1 %shard_map.103 = (bf16[256,2048]{1,0:T(8,128)(2,1)}, f32[256,1024]{1,0:T(8,128)S(1)}, f32[256,1024]{1,0:T(8,128)S(1)}) custom-call(s32[1,2]{1,0:T(1,128)S(1)} %copy-done.4, bf16[256,2048]{1,0:T(8,128)(2,1)S(1)} %bitcast.22, bf16[256,2048]{1,0:T(8,128)(2,1)S(1)} %bitcast.10, bf16[256,2048]{1,0:T(8,128)(2,1)S(1)} %bitcast.16, ...), custom_call_target="tpu_custom_call", output_to_operand_aliasing={{0}: (5, {})} | custom-call | flops 872415232 | bytes 8912896 | tf_op jit(solution)/shard_map/pallas_call | solution.py:394
  71.6 0.7 shard_map.104
  72.4 1.8 %collective-permute-start.20 = (f32[1032,128]{1,0:T(8,128)S(1)}, f32[1032,128]{1,0:T(8,128)S(1)}, u32[]{:S(2)}, u32[]{:S(2)}) collective-permute-start(f32[1032,128]{1,0:T(8,128)S(1)} %get-tuple-element.147), channel_id=1, source_target_pairs={{0,1},{1,0},{2,3},{3,2},{4,5},{5,4},{6,7},{7,6},{8,9},{9,8},{10,11... | collective-permute-start | bytes 1585160 | tf_op jit(solution)/shard_map/ppermute | solution.py:427
  74.2 1.9 %shard_map.105 = (bf16[256,2048]{1,0:T(8,128)(2,1)}, bf16[256,2048]{1,0:T(8,128)(2,1)}) custom-call(s32[1,2]{1,0:T(1,128)S(1)} %copy-done.4, bf16[256,2048]{1,0:T(8,128)(2,1)S(1)} %bitcast.11, bf16[256,2048]{1,0:T(8,128)(2,1)S(1)} %bitcast.17, f32[256,1024]{1,0:T(8,128)S(1)} %get-tuple-element.120.key_part, f32[256,1024]{1,0:T(8,128)S(1)} %get-tuple-element.121.value_part, ...), custom_call_target="tpu_custom_call" | custom-call | flops 134217728 | bytes 6553600 | tf_op jit(solution)/shard_map/pallas_call | solution.py:394
  76.1 2.5 %shard_map.106 = (bf16[256,2048]{1,0:T(8,128)(2,1)}, bf16[256,2048]{1,0:T(8,128)(2,1)}, f32[16,128]{1,0:T(8,128)}) custom-call(s32[1,2]{1,0:T(1,128)S(1)} %copy-done.4, bf16[256,2048]{1,0:T(8,128)(2,1)S(1)} %bitcast.12, bf16[256,2048]{1,0:T(8,128)(2,1)S(1)} %bitcast.18, ...), custom_call_target="tpu_custom_call", output_to_operand_aliasing={{0}: (7, {}), {1}: (8, {})} | custom-call | flops 134217728 | bytes 8929280 | tf_op jit(solution)/shard_map/pallas_call | solution.py:394
  (20 shorter events, 0.0 us)
Async XLA Ops:
  0.6 8.2 %copy-start.1 = (bf16[1,256,2048]{2,1,0:T(8,128)(2,1)S(1)}, bf16[1,256,2048]{2,1,0:T(8,128)(2,1)}, u32[]{:S(2)}) copy-start(bf16[1,256,2048]{2,1,0:T(8,128)(2,1)} %param.8) | copy-start | bytes 3145732
  0.6 8.1 %copy-start = (bf16[1,256,2048]{2,1,0:T(8,128)(2,1)S(1)}, bf16[1,256,2048]{2,1,0:T(8,128)(2,1)}, u32[]{:S(2)}) copy-start(bf16[1,256,2048]{2,1,0:T(8,128)(2,1)} %param.7) | copy-start | bytes 3145732
  0.7 8.1 %copy-start.3 = (bf16[1,256,2048]{2,1,0:T(8,128)(2,1)S(1)}, bf16[1,256,2048]{2,1,0:T(8,128)(2,1)}, u32[]{:S(2)}) copy-start(bf16[1,256,2048]{2,1,0:T(8,128)(2,1)} %param.9) | copy-start | bytes 3145732
  0.7 8.1 %copy-start.2 = (bf16[1,256,2048]{2,1,0:T(8,128)(2,1)S(1)}, bf16[1,256,2048]{2,1,0:T(8,128)(2,1)}, u32[]{:S(2)}) copy-start(bf16[1,256,2048]{2,1,0:T(8,128)(2,1)} %param.6) | copy-start | bytes 3145732
  2.5 2.0 %collective-permute-start = (f32[1032,128]{1,0:T(8,128)S(1)}, f32[1032,128]{1,0:T(8,128)S(1)}, u32[]{:S(2)}, u32[]{:S(2)}) collective-permute-start(f32[1032,128]{1,0:T(8,128)S(1)} %get-tuple-element.81), channel_id=1, source_target_pairs={{0,1},{1,0},{2,3},{3,2},{4,5},{5,4},{6,7},{7,6},{8,9},{9,8},{10,11... | collective-permute-start | bytes 1585160 | tf_op jit(solution)/shard_map/ppermute | solution.py:427
  2.6 0.7 copy-start.4
  4.1 33.6 %copy-start.5 = (f32[16,128]{1,0:T(8,128)S(1)}, f32[16,128]{1,0:T(8,128)}, u32[]{:S(2)}) copy-start(f32[16,128]{1,0:T(8,128)} %gain.1) | copy-start | bytes 24580
  5.1 7.3 %collective-permute-start.1 = (f32[264,128]{1,0:T(8,128)S(1)}, f32[264,128]{1,0:T(8,128)S(1)}, u32[]{:S(2)}, u32[]{:S(2)}) collective-permute-start(f32[264,128]{1,0:T(8,128)S(1)} %get-tuple-element.89), channel_id=1, source_target_pairs={{0,2},{1,3},{2,0},{3,1},{4,6},{5,7},{6,4},{7,5},{8,10},{9,11},{10,... | collective-permute-start | bytes 405512 | tf_op jit(solution)/shard_map/ppermute | solution.py:431
  7.5 4.8 %collective-permute-start.2 = (f32[264,128]{1,0:T(8,128)S(1)}, f32[264,128]{1,0:T(8,128)S(1)}, u32[]{:S(2)}, u32[]{:S(2)}) collective-permute-start(f32[264,128]{1,0:T(8,128)S(1)} %get-tuple-element.90), channel_id=1, source_target_pairs={{0,4},{1,5},{2,6},{3,7},{4,0},{5,1},{6,2},{7,3},{8,12},{9,13},{10,... | collective-permute-start | bytes 405512 | tf_op jit(solution)/shard_map/ppermute | solution.py:431
  8.8 6.1 %collective-permute-start.3 = (f32[264,128]{1,0:T(8,128)S(1)}, f32[264,128]{1,0:T(8,128)S(1)}, u32[]{:S(2)}, u32[]{:S(2)}) collective-permute-start(f32[264,128]{1,0:T(8,128)S(1)} %get-tuple-element.91), channel_id=1, source_target_pairs={{0,6},{1,7},{2,4},{3,5},{4,2},{5,3},{6,0},{7,1},{8,14},{9,15},{10,... | collective-permute-start | bytes 405512 | tf_op jit(solution)/shard_map/ppermute | solution.py:431
  15.5 22.2 %collective-permute-start.9 = (f32[768,1024]{1,0:T(8,128)S(1)}, f32[768,1024]{1,0:T(8,128)S(1)}, u32[]{:S(2)}, u32[]{:S(2)}) collective-permute-start(f32[768,1024]{1,0:T(8,128)S(1)} %get-tuple-element.110), channel_id=1, source_target_pairs={{0,1},{1,0},{2,3},{3,2},{4,5},{5,4},{6,7},{7,6},{8,9},{9,8},{10,11... | collective-permute-start | bytes 9437192 | tf_op jit(solution)/shard_map/ppermute | solution.py:427
  17.1 11.9 %collective-permute-start.5 = (f32[264,128]{1,0:T(8,128)S(1)}, f32[264,128]{1,0:T(8,128)S(1)}, u32[]{:S(2)}, u32[]{:S(2)}) collective-permute-start(f32[264,128]{1,0:T(8,128)S(1)} %shard_map.97), channel_id=1, source_target_pairs={{0,16},{1,17},{2,18},{3,19},{4,20},{5,21},{6,22},{7,23},{8,24},{9,... | collective-permute-start | bytes 405512 | tf_op jit(solution)/shard_map/ppermute | solution.py:437
  19.4 9.5 %collective-permute-start.4 = (f32[264,128]{1,0:T(8,128)S(1)}, f32[264,128]{1,0:T(8,128)S(1)}, u32[]{:S(2)}, u32[]{:S(2)}) collective-permute-start(f32[264,128]{1,0:T(8,128)S(1)} %shard_map.97), channel_id=1, source_target_pairs={{0,8},{1,9},{2,10},{3,11},{4,12},{5,13},{6,14},{7,15},{8,16},{9,17... | collective-permute-start | bytes 405512 | tf_op jit(solution)/shard_map/ppermute | solution.py:437
  29.7 4.2 %collective-permute-start.6 = (f32[256,128]{1,0:T(8,128)S(1)}, f32[256,128]{1,0:T(8,128)S(1)}, u32[]{:S(2)}, u32[]{:S(2)}) collective-permute-start(f32[256,128]{1,0:T(8,128)S(1)} %get-tuple-element.102), channel_id=1, source_target_pairs={{0,2},{1,3},{2,0},{3,1},{4,6},{5,7},{6,4},{7,5},{8,10},{9,11},{10,... | collective-permute-start | bytes 393224 | tf_op jit(solution)/shard_map/ppermute | solution.py:431
  30.7 4.1 %collective-permute-start.7 = (f32[256,128]{1,0:T(8,128)S(1)}, f32[256,128]{1,0:T(8,128)S(1)}, u32[]{:S(2)}, u32[]{:S(2)}) collective-permute-start(f32[256,128]{1,0:T(8,128)S(1)} %get-tuple-element.103), channel_id=1, source_target_pairs={{0,4},{1,5},{2,6},{3,7},{4,0},{5,1},{6,2},{7,3},{8,12},{9,13},{10,... | collective-permute-start | bytes 393224 | tf_op jit(solution)/shard_map/ppermute | solution.py:431
  31.2 6.4 %collective-permute-start.8 = (f32[256,128]{1,0:T(8,128)S(1)}, f32[256,128]{1,0:T(8,128)S(1)}, u32[]{:S(2)}, u32[]{:S(2)}) collective-permute-start(f32[256,128]{1,0:T(8,128)S(1)} %get-tuple-element.104), channel_id=1, source_target_pairs={{0,6},{1,7},{2,4},{3,5},{4,2},{5,3},{6,0},{7,1},{8,14},{9,15},{10,... | collective-permute-start | bytes 393224 | tf_op jit(solution)/shard_map/ppermute | solution.py:431
  41.0 5.8 %collective-permute-start.10 = (f32[272,128]{1,0:T(8,128)S(1)}, f32[272,128]{1,0:T(8,128)S(1)}, u32[]{:S(2)}, u32[]{:S(2)}) collective-permute-start(f32[272,128]{1,0:T(8,128)S(1)} %get-tuple-element.113), channel_id=1, source_target_pairs={{0,2},{1,3},{2,0},{3,1},{4,6},{5,7},{6,4},{7,5},{8,10},{9,11},{10,... | collective-permute-start | bytes 417800 | tf_op jit(solution)/shard_map/ppermute | solution.py:431
  41.0 5.7 %collective-permute-start.11 = (f32[272,128]{1,0:T(8,128)S(1)}, f32[272,128]{1,0:T(8,128)S(1)}, u32[]{:S(2)}, u32[]{:S(2)}) collective-permute-start(f32[272,128]{1,0:T(8,128)S(1)} %get-tuple-element.114), channel_id=1, source_target_pairs={{0,4},{1,5},{2,6},{3,7},{4,0},{5,1},{6,2},{7,3},{8,12},{9,13},{10,... | collective-permute-start | bytes 417800 | tf_op jit(solution)/shard_map/ppermute | solution.py:431
  42.4 6.0 %collective-permute-start.12 = (f32[272,128]{1,0:T(8,128)S(1)}, f32[272,128]{1,0:T(8,128)S(1)}, u32[]{:S(2)}, u32[]{:S(2)}) collective-permute-start(f32[272,128]{1,0:T(8,128)S(1)} %get-tuple-element.115), channel_id=1, source_target_pairs={{0,6},{1,7},{2,4},{3,5},{4,2},{5,3},{6,0},{7,1},{8,14},{9,15},{10,... | collective-permute-start | bytes 417800 | tf_op jit(solution)/shard_map/ppermute | solution.py:431
  49.0 19.5 %collective-permute-start.13 = (f32[384,1024]{1,0:T(8,128)S(1)}, f32[384,1024]{1,0:T(8,128)S(1)}, u32[]{:S(2)}, u32[]{:S(2)}) collective-permute-start(f32[384,1024]{1,0:T(8,128)S(1)} %get-tuple-element.127), channel_id=1, source_target_pairs={{0,1},{1,0},{2,3},{3,2},{4,5},{5,4},{6,7},{7,6},{8,9},{9,8},{10,11... | collective-permute-start | bytes 4718600 | tf_op jit(solution)/shard_map/ppermute | solution.py:427
  51.9 9.9 %collective-permute-start.15 = (f32[272,128]{1,0:T(8,128)S(1)}, f32[272,128]{1,0:T(8,128)S(1)}, u32[]{:S(2)}, u32[]{:S(2)}) collective-permute-start(f32[272,128]{1,0:T(8,128)S(1)} %get-tuple-element.126), channel_id=1, source_target_pairs={{0,16},{1,17},{2,18},{3,19},{4,20},{5,21},{6,22},{7,23},{8,24},{9,... | collective-permute-start | bytes 417800 | tf_op jit(solution)/shard_map/ppermute | solution.py:437
  54.8 7.6 %collective-permute-start.14 = (f32[272,128]{1,0:T(8,128)S(1)}, f32[272,128]{1,0:T(8,128)S(1)}, u32[]{:S(2)}, u32[]{:S(2)}) collective-permute-start(f32[272,128]{1,0:T(8,128)S(1)} %get-tuple-element.126), channel_id=1, source_target_pairs={{0,24},{1,25},{2,26},{3,27},{4,28},{5,29},{6,30},{7,31},{8,0},{9,1... | collective-permute-start | bytes 417800 | tf_op jit(solution)/shard_map/ppermute | solution.py:437
  63.2 8.4 %collective-permute-start.16 = (f32[256,128]{1,0:T(8,128)S(1)}, f32[256,128]{1,0:T(8,128)S(1)}, u32[]{:S(2)}, u32[]{:S(2)}) collective-permute-start(f32[256,128]{1,0:T(8,128)S(1)} %get-tuple-element.132), channel_id=1, source_target_pairs={{0,2},{1,3},{2,0},{3,1},{4,6},{5,7},{6,4},{7,5},{8,10},{9,11},{10,... | collective-permute-start | bytes 393224 | tf_op jit(solution)/shard_map/ppermute | solution.py:431
  63.9 7.7 %collective-permute-start.17 = (f32[256,128]{1,0:T(8,128)S(1)}, f32[256,128]{1,0:T(8,128)S(1)}, u32[]{:S(2)}, u32[]{:S(2)}) collective-permute-start(f32[256,128]{1,0:T(8,128)S(1)} %get-tuple-element.133), channel_id=1, source_target_pairs={{0,4},{1,5},{2,6},{3,7},{4,0},{5,1},{6,2},{7,3},{8,12},{9,13},{10,... | collective-permute-start | bytes 393224 | tf_op jit(solution)/shard_map/ppermute | solution.py:431
  64.8 6.8 %collective-permute-start.18 = (f32[256,128]{1,0:T(8,128)S(1)}, f32[256,128]{1,0:T(8,128)S(1)}, u32[]{:S(2)}, u32[]{:S(2)}) collective-permute-start(f32[256,128]{1,0:T(8,128)S(1)} %get-tuple-element.134), channel_id=1, source_target_pairs={{0,6},{1,7},{2,4},{3,5},{4,2},{5,3},{6,0},{7,1},{8,14},{9,15},{10,... | collective-permute-start | bytes 393224 | tf_op jit(solution)/shard_map/ppermute | solution.py:431
  65.9 5.7 %collective-permute-start.19 = (f32[8,128]{1,0:T(8,128)S(1)}, f32[8,128]{1,0:T(8,128)S(1)}, u32[]{:S(2)}, u32[]{:S(2)}) collective-permute-start(f32[8,128]{1,0:T(8,128)S(1)} %get-tuple-element.146.refs_2_), channel_id=1, source_target_pairs={{0,8},{1,9},{2,10},{3,11},{4,12},{5,13},{6,14},{7,15},{8,16},{9,17... | collective-permute-start | bytes 12296 | tf_op jit(solution)/shard_map/ppermute | solution.py:437
  72.4 3.7 %collective-permute-start.20 = (f32[1032,128]{1,0:T(8,128)S(1)}, f32[1032,128]{1,0:T(8,128)S(1)}, u32[]{:S(2)}, u32[]{:S(2)}) collective-permute-start(f32[1032,128]{1,0:T(8,128)S(1)} %get-tuple-element.147), channel_id=1, source_target_pairs={{0,1},{1,0},{2,3},{3,2},{4,5},{5,4},{6,7},{7,6},{8,9},{9,8},{10,11... | collective-permute-start | bytes 1585160 | tf_op jit(solution)/shard_map/ppermute | solution.py:427

commit v4 on v3

--- a/solution.py
+++ b/solution.py
@@ -255,35 +255,31 @@
 
 
 def finish_kernel(docs, key, value, key_part, value_part, state, *refs, half, other):
-    refs, (key_held, value_held, sems) = refs[:-3], refs[-3:]
+    refs, (key_held, value_held, gain_held, sems) = refs[:-4], refs[-4:]
+    copies = []
     if other:
         refs, gain_grad = refs[:-1], refs[-1]
         for head in range(half):
-            gain_grad[pl.ds(my_core() * half + head, 1), :] = refs[0][pl.ds(head, 1), :]
-            gain_grad[pl.ds((1 - my_core()) * half + head, 1), :] = state[pl.ds(half * 128 + head, 1), :]
+            gain_held[pl.ds(my_core() * half + head, 1), :] = refs[0][pl.ds(head, 1), :]
+            gain_held[pl.ds((1 - my_core()) * half + head, 1), :] = state[pl.ds(half * 128 + head, 1), :]
+        copies.append(pltpu.make_async_copy(gain_held, gain_grad, sems.at[2, 0]))
+        copies[-1].start()
     key_grad, value_grad = refs[-2:]
     leave = column(docs, False, F32)
     base = (1 - my_core() if other else my_core()) * half
-    copies = []
-    for heads in batches(half, 4):
-        results = []
+    for at, heads in enumerate(batches(half, 4)):
         for head in heads:
             cols, full = pl.ds(head * 128, 128), wide(base, head)
             g = state[cols, :].astype(BF16)
-            results.append(
-                (
-                    (key_part[:, cols] + leave * dot(value[:, full], g, 1, 1)).astype(BF16),
-                    (value_part[:, cols] + leave * dot(key[:, full], g, 1, 0)).astype(BF16),
-                )
-            )
-        for head, (key_sum, value_sum) in zip(heads, results):
-            cols, full = pl.ds(head * 128, 128), wide(base, head)
-            key_held[:, cols] = key_sum
-            value_held[:, cols] = value_sum
-            copies.append(pltpu.make_async_copy(key_held.at[:, cols], key_grad.at[:, full], sems.at[0, head]))
-            copies.append(pltpu.make_async_copy(value_held.at[:, cols], value_grad.at[:, full], sems.at[1, head]))
-            copies[-2].start()
-            copies[-1].start()
+            key_held[:, cols] = (key_part[:, cols] + leave * dot(value[:, full], g, 1, 1)).astype(BF16)
+            value_held[:, cols] = (value_part[:, cols] + leave * dot(key[:, full], g, 1, 0)).astype(BF16)
+        size = len(heads) * 128
+        held = pl.ds(heads[0] * 128, size)
+        full = pl.ds(pl.multiple_of((base + heads[0]) * 128, 128), size)
+        copies.append(pltpu.make_async_copy(key_held.at[:, held], key_grad.at[:, full], sems.at[0, at]))
+        copies.append(pltpu.make_async_copy(value_held.at[:, held], value_grad.at[:, full], sems.at[1, at]))
+        copies[-2].start()
+        copies[-1].start()
     for copy in copies:
         copy.wait()
 
@@ -481,12 +477,13 @@
             [shape(tokens, cols, BF16)] * 2 + [shape(heads, width, F32)] * len(sums),
             flops=2 * half * tokens * width * 2 * width,
             in_specs=[None] * (5 + len(sums)) + [any_place] * len(into),
-            out_specs=[any_place] * 2 + [None] * len(sums),
+            out_specs=[any_place] * (2 + len(sums)),
             aliases={7: 0, 8: 1} if into else None,
             scratch=[
                 pltpu.VMEM((tokens, rows), BF16),
                 pltpu.VMEM((tokens, rows), BF16),
-                pltpu.SemaphoreType.DMA((2, half)),
+                pltpu.VMEM((heads, width), F32),
+                pltpu.SemaphoreType.DMA((3, half)),
             ],
         )
 

time: 78.9 us -> 78.6 us (level)
  no operation moved by 1% of the time
where the time goes in v4:
time: 78.6 us; the launch traced here: 78.5 us
  starting transfers between devices  27.6 us (35%)
  waiting for transfers between devices  25.5 us (32%)
  Pallas kernels  23.7 us (30%)
  between operations  1.01 us (1%)
    pallas_call x13, Pallas kernels, call(): pl.pallas_call(kernel, out_shape=outs, grid_spec=pltpu.PrefetchScalarGrid...  22 us
    ppermute x5, waiting for transfers between devices, around(): return lax.ppermute(value, 'ctx', pairs)  15.7 us
    ppermute x12, starting transfers between devices, to_chips(): lax.ppermute(values[turn], 'ctx', [(i, i ^ 2 * turn) for i in range(shard...  11.8 us
    ppermute x12, waiting for transfers between devices, to_chips(): lax.ppermute(values[turn], 'ctx', [(i, i ^ 2 * turn) for i in range(shard...  9.45 us
    ppermute x5, starting transfers between devices, around(): return lax.ppermute(value, 'ctx', pairs)  9.35 us
    ppermute x4, starting transfers between devices, swap(): return lax.ppermute(value, 'ctx', [(i, i ^ 1) for i in range(shards)])  6.4 us
    pallas_call x1, Pallas kernels, local(): pl.pallas_call(functools.partial(first_kernel, half=half), out_shape=[pay...  1.77 us
  transfers between devices with their start and end apart: 21, of which 9 were waited for; matrix products, arithmetic and copies ran while one was open for 0% of the time, Pallas kernels for 18%

profile of v4, /device:TPU:1, one launch (start us, length us, event | category | flops | bytes accessed | tf_op | source)
XLA Modules:
  0.0 78.5 jit_solution(5404443288394680320)
XLA Ops:
  0.7 1.8 %shard_map.93 = (f32[1032,128]{1,0:T(8,128)S(1)}, bf16[256,1024]{1,0:T(8,128)(2,1)S(1)}, bf16[256,1024]{1,0:T(8,128)(2,1)S(1)}) custom-call(s32[1,2]{1,0:T(1,128)} %docs.14, bf16[256,2048]{1,0:T(8,128)(2,1)} %bitcast.7, bf16[256,2048]{1,0:T(8,128)(2,1)} %bitcast.13), custom_call_target="tpu_custom_call" | custom-call | flops 67108864 | bytes 2097152 | tf_op jit(solution)/shard_map/pallas_call | solution.py:493
  2.5 0.1 collective-permute-start
  2.6 0.7 copy-done.4
  3.2 0.9 %shard_map.94.own = f32[1032,128]{1,0:T(8,128)S(1)} custom-call(s32[1,2]{1,0:T(1,128)S(1)} %copy-done.4, bf16[256,1024]{1,0:T(8,128)(2,1)S(1)} %get-tuple-element.86.key, bf16[256,1024]{1,0:T(8,128)(2,1)S(1)} %get-tuple-element.87.value), custom_call_target="tpu_custom_call" | custom-call | flops 67108864 | bytes 1576960 | tf_op jit(solution)/shard_map/pallas_call | solution.py:390
  4.1 0.0 copy-start.5
  4.1 0.3 collective-permute-done.other
  4.4 0.6 shard_map.95
  5.1 2.4 %collective-permute-start.1 = (f32[264,128]{1,0:T(8,128)S(1)}, f32[264,128]{1,0:T(8,128)S(1)}, u32[]{:S(2)}, u32[]{:S(2)}) collective-permute-start(f32[264,128]{1,0:T(8,128)S(1)} %get-tuple-element.89), channel_id=1, source_target_pairs={{0,2},{1,3},{2,0},{3,1},{4,6},{5,7},{6,4},{7,5},{8,10},{9,11},{10,... | collective-permute-start | bytes 405512 | tf_op jit(solution)/shard_map/ppermute | solution.py:427
  7.5 1.2 %collective-permute-start.2 = (f32[264,128]{1,0:T(8,128)S(1)}, f32[264,128]{1,0:T(8,128)S(1)}, u32[]{:S(2)}, u32[]{:S(2)}) collective-permute-start(f32[264,128]{1,0:T(8,128)S(1)} %get-tuple-element.90), channel_id=1, source_target_pairs={{0,4},{1,5},{2,6},{3,7},{4,0},{5,1},{6,2},{7,3},{8,12},{9,13},{10,... | collective-permute-start | bytes 405512 | tf_op jit(solution)/shard_map/ppermute | solution.py:427
  8.8 0.0 collective-permute-start.3
  8.8 3.6 %shard_map.96 = (f32[256,1024]{1,0:T(8,128)S(1)}, f32[768,1024]{1,0:T(8,128)S(1)}) custom-call(s32[1,2]{1,0:T(1,128)S(1)} %copy-done.4, bf16[256,2048]{1,0:T(8,128)(2,1)S(1)} %bitcast.19, bf16[256,2048]{1,0:T(8,128)(2,1)S(1)} %bitcast.8, bf16[256,2048]{1,0:T(8,128)(2,1)S(1)} %bitcast.14, bf16[256,2048]{1,0:T(8,128)(2,1)S(1)} %bitcast.23), custom_call_target="tpu_custom_call" | custom-call | flops 536870912 | bytes 8388608 | tf_op jit(solution)/shard_map/pallas_call | solution.py:390
  12.4 0.0 collective-permute-done.2.c2
  12.4 2.5 %collective-permute-done.3.c3 = f32[264,128]{1,0:T(8,128)S(1)} collective-permute-done((f32[264,128]{1,0:T(8,128)S(1)}, f32[264,128]{1,0:T(8,128)S(1)}, u32[]{:S(2)}, u32[]{:S(2)}) %collective-permute-start.3) | collective-permute-done | bytes 135200 | tf_op jit(solution)/shard_map/ppermute | solution.py:427
  14.9 0.6 shard_map.97
  15.5 1.6 %collective-permute-start.9 = (f32[768,1024]{1,0:T(8,128)S(1)}, f32[768,1024]{1,0:T(8,128)S(1)}, u32[]{:S(2)}, u32[]{:S(2)}) collective-permute-start(f32[768,1024]{1,0:T(8,128)S(1)} %get-tuple-element.110), channel_id=1, source_target_pairs={{0,1},{1,0},{2,3},{3,2},{4,5},{5,4},{6,7},{7,6},{8,9},{9,8},{10,11... | collective-permute-start | bytes 9437192 | tf_op jit(solution)/shard_map/ppermute | solution.py:423
  17.1 2.3 %collective-permute-start.5 = (f32[264,128]{1,0:T(8,128)S(1)}, f32[264,128]{1,0:T(8,128)S(1)}, u32[]{:S(2)}, u32[]{:S(2)}) collective-permute-start(f32[264,128]{1,0:T(8,128)S(1)} %shard_map.97), channel_id=1, source_target_pairs={{0,16},{1,17},{2,18},{3,19},{4,20},{5,21},{6,22},{7,23},{8,24},{9,... | collective-permute-start | bytes 405512 | tf_op jit(solution)/shard_map/ppermute | solution.py:433
  19.4 1.3 %collective-permute-start.4 = (f32[264,128]{1,0:T(8,128)S(1)}, f32[264,128]{1,0:T(8,128)S(1)}, u32[]{:S(2)}, u32[]{:S(2)}) collective-permute-start(f32[264,128]{1,0:T(8,128)S(1)} %shard_map.97), channel_id=1, source_target_pairs={{0,8},{1,9},{2,10},{3,11},{4,12},{5,13},{6,14},{7,15},{8,16},{9,17... | collective-permute-start | bytes 405512 | tf_op jit(solution)/shard_map/ppermute | solution.py:433
  20.7 8.2 %collective-permute-done.5.refs_1_ = f32[264,128]{1,0:T(8,128)S(1)} collective-permute-done((f32[264,128]{1,0:T(8,128)S(1)}, f32[264,128]{1,0:T(8,128)S(1)}, u32[]{:S(2)}, u32[]{:S(2)}) %collective-permute-start.5) | collective-permute-done | bytes 135200 | tf_op jit(solution)/shard_map/ppermute | solution.py:433
  28.9 0.7 shard_map.98
  29.7 1.0 %collective-permute-start.6 = (f32[256,128]{1,0:T(8,128)S(1)}, f32[256,128]{1,0:T(8,128)S(1)}, u32[]{:S(2)}, u32[]{:S(2)}) collective-permute-start(f32[256,128]{1,0:T(8,128)S(1)} %get-tuple-element.102), channel_id=1, source_target_pairs={{0,2},{1,3},{2,0},{3,1},{4,6},{5,7},{6,4},{7,5},{8,10},{9,11},{10,... | collective-permute-start | bytes 393224 | tf_op jit(solution)/shard_map/ppermute | solution.py:427
  30.7 0.5 collective-permute-start.7
  31.2 1.2 %collective-permute-start.8 = (f32[256,128]{1,0:T(8,128)S(1)}, f32[256,128]{1,0:T(8,128)S(1)}, u32[]{:S(2)}, u32[]{:S(2)}) collective-permute-start(f32[256,128]{1,0:T(8,128)S(1)} %get-tuple-element.104), channel_id=1, source_target_pairs={{0,6},{1,7},{2,4},{3,5},{4,2},{5,3},{6,0},{7,1},{8,14},{9,15},{10,... | collective-permute-start | bytes 393224 | tf_op jit(solution)/shard_map/ppermute | solution.py:427
  32.4 1.5 %collective-permute-done.6.c1 = f32[256,128]{1,0:T(8,128)S(1)} collective-permute-done((f32[256,128]{1,0:T(8,128)S(1)}, f32[256,128]{1,0:T(8,128)S(1)}, u32[]{:S(2)}, u32[]{:S(2)}) %collective-permute-start.6) | collective-permute-done | bytes 131104 | tf_op jit(solution)/shard_map/ppermute | solution.py:427
  33.9 0.9 %collective-permute-done.7.c2 = f32[256,128]{1,0:T(8,128)S(1)} collective-permute-done((f32[256,128]{1,0:T(8,128)S(1)}, f32[256,128]{1,0:T(8,128)S(1)}, u32[]{:S(2)}, u32[]{:S(2)}) %collective-permute-start.7) | collective-permute-done | bytes 131104 | tf_op jit(solution)/shard_map/ppermute | solution.py:427
  34.8 2.9 %collective-permute-done.8.c3 = f32[256,128]{1,0:T(8,128)S(1)} collective-permute-done((f32[256,128]{1,0:T(8,128)S(1)}, f32[256,128]{1,0:T(8,128)S(1)}, u32[]{:S(2)}, u32[]{:S(2)}) %collective-permute-start.8) | collective-permute-done | bytes 131104 | tf_op jit(solution)/shard_map/ppermute | solution.py:427
  37.7 3.3 %shard_map.99 = (f32[272,128]{1,0:T(8,128)S(1)}, f32[272,128]{1,0:T(8,128)S(1)}, f32[272,128]{1,0:T(8,128)S(1)}, f32[272,128]{1,0:T(8,128)S(1)}, f32[1032,128]{1...) custom-call(s32[1,2]{1,0:T(1,128)S(1)} %copy-done.4, ...), custom_call_target="tpu_custom_call" | custom-call | flops 268435456 | bytes 11853824 | tf_op jit(solution)/shard_map/pallas_call | solution.py:390
  41.0 0.1 collective-permute-start.10
  41.0 1.4 %collective-permute-start.11 = (f32[272,128]{1,0:T(8,128)S(1)}, f32[272,128]{1,0:T(8,128)S(1)}, u32[]{:S(2)}, u32[]{:S(2)}) collective-permute-start(f32[272,128]{1,0:T(8,128)S(1)} %get-tuple-element.114), channel_id=1, source_target_pairs={{0,4},{1,5},{2,6},{3,7},{4,0},{5,1},{6,2},{7,3},{8,12},{9,13},{10,... | collective-permute-start | bytes 417800 | tf_op jit(solution)/shard_map/ppermute | solution.py:427
  42.4 1.2 %collective-permute-start.12 = (f32[272,128]{1,0:T(8,128)S(1)}, f32[272,128]{1,0:T(8,128)S(1)}, u32[]{:S(2)}, u32[]{:S(2)}) collective-permute-start(f32[272,128]{1,0:T(8,128)S(1)} %get-tuple-element.115), channel_id=1, source_target_pairs={{0,6},{1,7},{2,4},{3,5},{4,2},{5,3},{6,0},{7,1},{8,14},{9,15},{10,... | collective-permute-start | bytes 417800 | tf_op jit(solution)/shard_map/ppermute | solution.py:427
  43.7 3.1 %shard_map.100 = (bf16[256,2048]{1,0:T(8,128)(2,1)}, f32[256,1024]{1,0:T(8,128)S(1)}, f32[256,1024]{1,0:T(8,128)S(1)}) custom-call(s32[1,2]{1,0:T(1,128)S(1)} %copy-done.4, bf16[256,2048]{1,0:T(8,128)(2,1)S(1)} %bitcast.21, bf16[256,2048]{1,0:T(8,128)(2,1)S(1)} %bitcast.9, bf16[256,2048]{1,0:T(8,128)(2,1)S(1)} %bitcast.15, ...), custom_call_target="tpu_custom_call" | custom-call | flops 872415232 | bytes 7077888 | tf_op jit(solution)/shard_map/pallas_call | solution.py:390
  46.7 0.0 collective-permute-done.10.c1
  46.8 1.6 %collective-permute-done.12.c3 = f32[272,128]{1,0:T(8,128)S(1)} collective-permute-done((f32[272,128]{1,0:T(8,128)S(1)}, f32[272,128]{1,0:T(8,128)S(1)}, u32[]{:S(2)}, u32[]{:S(2)}) %collective-permute-start.12) | collective-permute-done | bytes 139296 | tf_op jit(solution)/shard_map/ppermute | solution.py:427
  48.4 0.6 shard_map.101
  49.0 2.9 %collective-permute-start.13 = (f32[384,1024]{1,0:T(8,128)S(1)}, f32[384,1024]{1,0:T(8,128)S(1)}, u32[]{:S(2)}, u32[]{:S(2)}) collective-permute-start(f32[384,1024]{1,0:T(8,128)S(1)} %get-tuple-element.127), channel_id=1, source_target_pairs={{0,1},{1,0},{2,3},{3,2},{4,5},{5,4},{6,7},{7,6},{8,9},{9,8},{10,11... | collective-permute-start | bytes 4718600 | tf_op jit(solution)/shard_map/ppermute | solution.py:423
  51.9 2.9 %collective-permute-start.15 = (f32[272,128]{1,0:T(8,128)S(1)}, f32[272,128]{1,0:T(8,128)S(1)}, u32[]{:S(2)}, u32[]{:S(2)}) collective-permute-start(f32[272,128]{1,0:T(8,128)S(1)} %get-tuple-element.126), channel_id=1, source_target_pairs={{0,16},{1,17},{2,18},{3,19},{4,20},{5,21},{6,22},{7,23},{8,24},{9,... | collective-permute-start | bytes 417800 | tf_op jit(solution)/shard_map/ppermute | solution.py:433
  54.8 0.2 collective-permute-start.14
  54.9 6.8 %collective-permute-done.15.refs_1_ = f32[272,128]{1,0:T(8,128)S(1)} collective-permute-done((f32[272,128]{1,0:T(8,128)S(1)}, f32[272,128]{1,0:T(8,128)S(1)}, u32[]{:S(2)}, u32[]{:S(2)}) %collective-permute-start.15) | collective-permute-done | bytes 139296 | tf_op jit(solution)/shard_map/ppermute | solution.py:433
  61.8 0.6 collective-permute-done.14.refs_0_
  62.4 0.7 shard_map.102
  63.2 0.7 collective-permute-start.16
  63.9 0.9 %collective-permute-start.17 = (f32[256,128]{1,0:T(8,128)S(1)}, f32[256,128]{1,0:T(8,128)S(1)}, u32[]{:S(2)}, u32[]{:S(2)}) collective-permute-start(f32[256,128]{1,0:T(8,128)S(1)} %get-tuple-element.133), channel_id=1, source_target_pairs={{0,4},{1,5},{2,6},{3,7},{4,0},{5,1},{6,2},{7,3},{8,12},{9,13},{10,... | collective-permute-start | bytes 393224 | tf_op jit(solution)/shard_map/ppermute | solution.py:427
  64.8 1.1 %collective-permute-start.18 = (f32[256,128]{1,0:T(8,128)S(1)}, f32[256,128]{1,0:T(8,128)S(1)}, u32[]{:S(2)}, u32[]{:S(2)}) collective-permute-start(f32[256,128]{1,0:T(8,128)S(1)} %get-tuple-element.134), channel_id=1, source_target_pairs={{0,6},{1,7},{2,4},{3,5},{4,2},{5,3},{6,0},{7,1},{8,14},{9,15},{10,... | collective-permute-start | bytes 393224 | tf_op jit(solution)/shard_map/ppermute | solution.py:427
  65.9 2.6 %collective-permute-start.19 = (f32[8,128]{1,0:T(8,128)S(1)}, f32[8,128]{1,0:T(8,128)S(1)}, u32[]{:S(2)}, u32[]{:S(2)}) collective-permute-start(f32[8,128]{1,0:T(8,128)S(1)} %get-tuple-element.146.refs_2_), channel_id=1, source_target_pairs={{0,8},{1,9},{2,10},{3,11},{4,12},{5,13},{6,14},{7,15},{8,16},{9,17... | collective-permute-start | bytes 12296 | tf_op jit(solution)/shard_map/ppermute | solution.py:433
  68.5 3.1 %shard_map.103 = (bf16[256,2048]{1,0:T(8,128)(2,1)}, f32[256,1024]{1,0:T(8,128)S(1)}, f32[256,1024]{1,0:T(8,128)S(1)}) custom-call(s32[1,2]{1,0:T(1,128)S(1)} %copy-done.4, bf16[256,2048]{1,0:T(8,128)(2,1)S(1)} %bitcast.22, bf16[256,2048]{1,0:T(8,128)(2,1)S(1)} %bitcast.10, bf16[256,2048]{1,0:T(8,128)(2,1)S(1)} %bitcast.16, ...), custom_call_target="tpu_custom_call", output_to_operand_aliasing={{0}: (5, {})} | custom-call | flops 872415232 | bytes 8912896 | tf_op jit(solution)/shard_map/pallas_call | solution.py:390
  71.6 0.7 shard_map.104
  72.4 1.8 %collective-permute-start.20 = (f32[1032,128]{1,0:T(8,128)S(1)}, f32[1032,128]{1,0:T(8,128)S(1)}, u32[]{:S(2)}, u32[]{:S(2)}) collective-permute-start(f32[1032,128]{1,0:T(8,128)S(1)} %get-tuple-element.147), channel_id=1, source_target_pairs={{0,1},{1,0},{2,3},{3,2},{4,5},{5,4},{6,7},{7,6},{8,9},{9,8},{10,11... | collective-permute-start | bytes 1585160 | tf_op jit(solution)/shard_map/ppermute | solution.py:423
  74.2 2.0 %shard_map.105 = (bf16[256,2048]{1,0:T(8,128)(2,1)}, bf16[256,2048]{1,0:T(8,128)(2,1)}) custom-call(s32[1,2]{1,0:T(1,128)S(1)} %copy-done.4, bf16[256,2048]{1,0:T(8,128)(2,1)S(1)} %bitcast.11, bf16[256,2048]{1,0:T(8,128)(2,1)S(1)} %bitcast.17, f32[256,1024]{1,0:T(8,128)S(1)} %get-tuple-element.120.key_part, f32[256,1024]{1,0:T(8,128)S(1)} %get-tuple-element.121.value_part, ...), custom_call_target="tpu_custom_call" | custom-call | flops 134217728 | bytes 6553600 | tf_op jit(solution)/shard_map/pallas_call | solution.py:390
  76.2 2.1 %shard_map.106 = (bf16[256,2048]{1,0:T(8,128)(2,1)}, bf16[256,2048]{1,0:T(8,128)(2,1)}, f32[16,128]{1,0:T(8,128)}) custom-call(s32[1,2]{1,0:T(1,128)S(1)} %copy-done.4, bf16[256,2048]{1,0:T(8,128)(2,1)S(1)} %bitcast.12, bf16[256,2048]{1,0:T(8,128)(2,1)S(1)} %bitcast.18, ...), custom_call_target="tpu_custom_call", output_to_operand_aliasing={{0}: (7, {}), {1}: (8, {})} | custom-call | flops 134217728 | bytes 8929280 | tf_op jit(solution)/shard_map/pallas_call | solution.py:390
  (20 shorter events, 0.0 us)
Async XLA Ops:
  0.6 8.2 %copy-start.1 = (bf16[1,256,2048]{2,1,0:T(8,128)(2,1)S(1)}, bf16[1,256,2048]{2,1,0:T(8,128)(2,1)}, u32[]{:S(2)}) copy-start(bf16[1,256,2048]{2,1,0:T(8,128)(2,1)} %param.8) | copy-start | bytes 3145732
  0.6 8.1 %copy-start = (bf16[1,256,2048]{2,1,0:T(8,128)(2,1)S(1)}, bf16[1,256,2048]{2,1,0:T(8,128)(2,1)}, u32[]{:S(2)}) copy-start(bf16[1,256,2048]{2,1,0:T(8,128)(2,1)} %param.7) | copy-start | bytes 3145732
  0.7 8.1 %copy-start.3 = (bf16[1,256,2048]{2,1,0:T(8,128)(2,1)S(1)}, bf16[1,256,2048]{2,1,0:T(8,128)(2,1)}, u32[]{:S(2)}) copy-start(bf16[1,256,2048]{2,1,0:T(8,128)(2,1)} %param.9) | copy-start | bytes 3145732
  0.7 8.1 %copy-start.2 = (bf16[1,256,2048]{2,1,0:T(8,128)(2,1)S(1)}, bf16[1,256,2048]{2,1,0:T(8,128)(2,1)}, u32[]{:S(2)}) copy-start(bf16[1,256,2048]{2,1,0:T(8,128)(2,1)} %param.6) | copy-start | bytes 3145732
  2.5 2.0 %collective-permute-start = (f32[1032,128]{1,0:T(8,128)S(1)}, f32[1032,128]{1,0:T(8,128)S(1)}, u32[]{:S(2)}, u32[]{:S(2)}) collective-permute-start(f32[1032,128]{1,0:T(8,128)S(1)} %get-tuple-element.81), channel_id=1, source_target_pairs={{0,1},{1,0},{2,3},{3,2},{4,5},{5,4},{6,7},{7,6},{8,9},{9,8},{10,11... | collective-permute-start | bytes 1585160 | tf_op jit(solution)/shard_map/ppermute | solution.py:423
  2.6 0.7 copy-start.4
  4.1 33.6 %copy-start.5 = (f32[16,128]{1,0:T(8,128)S(1)}, f32[16,128]{1,0:T(8,128)}, u32[]{:S(2)}) copy-start(f32[16,128]{1,0:T(8,128)} %gain.1) | copy-start | bytes 24580
  5.1 7.3 %collective-permute-start.1 = (f32[264,128]{1,0:T(8,128)S(1)}, f32[264,128]{1,0:T(8,128)S(1)}, u32[]{:S(2)}, u32[]{:S(2)}) collective-permute-start(f32[264,128]{1,0:T(8,128)S(1)} %get-tuple-element.89), channel_id=1, source_target_pairs={{0,2},{1,3},{2,0},{3,1},{4,6},{5,7},{6,4},{7,5},{8,10},{9,11},{10,... | collective-permute-start | bytes 405512 | tf_op jit(solution)/shard_map/ppermute | solution.py:427
  7.5 4.8 %collective-permute-start.2 = (f32[264,128]{1,0:T(8,128)S(1)}, f32[264,128]{1,0:T(8,128)S(1)}, u32[]{:S(2)}, u32[]{:S(2)}) collective-permute-start(f32[264,128]{1,0:T(8,128)S(1)} %get-tuple-element.90), channel_id=1, source_target_pairs={{0,4},{1,5},{2,6},{3,7},{4,0},{5,1},{6,2},{7,3},{8,12},{9,13},{10,... | collective-permute-start | bytes 405512 | tf_op jit(solution)/shard_map/ppermute | solution.py:427
  8.8 6.1 %collective-permute-start.3 = (f32[264,128]{1,0:T(8,128)S(1)}, f32[264,128]{1,0:T(8,128)S(1)}, u32[]{:S(2)}, u32[]{:S(2)}) collective-permute-start(f32[264,128]{1,0:T(8,128)S(1)} %get-tuple-element.91), channel_id=1, source_target_pairs={{0,6},{1,7},{2,4},{3,5},{4,2},{5,3},{6,0},{7,1},{8,14},{9,15},{10,... | collective-permute-start | bytes 405512 | tf_op jit(solution)/shard_map/ppermute | solution.py:427
  15.5 22.2 %collective-permute-start.9 = (f32[768,1024]{1,0:T(8,128)S(1)}, f32[768,1024]{1,0:T(8,128)S(1)}, u32[]{:S(2)}, u32[]{:S(2)}) collective-permute-start(f32[768,1024]{1,0:T(8,128)S(1)} %get-tuple-element.110), channel_id=1, source_target_pairs={{0,1},{1,0},{2,3},{3,2},{4,5},{5,4},{6,7},{7,6},{8,9},{9,8},{10,11... | collective-permute-start | bytes 9437192 | tf_op jit(solution)/shard_map/ppermute | solution.py:423
  17.1 11.9 %collective-permute-start.5 = (f32[264,128]{1,0:T(8,128)S(1)}, f32[264,128]{1,0:T(8,128)S(1)}, u32[]{:S(2)}, u32[]{:S(2)}) collective-permute-start(f32[264,128]{1,0:T(8,128)S(1)} %shard_map.97), channel_id=1, source_target_pairs={{0,16},{1,17},{2,18},{3,19},{4,20},{5,21},{6,22},{7,23},{8,24},{9,... | collective-permute-start | bytes 405512 | tf_op jit(solution)/shard_map/ppermute | solution.py:433
  19.4 9.5 %collective-permute-start.4 = (f32[264,128]{1,0:T(8,128)S(1)}, f32[264,128]{1,0:T(8,128)S(1)}, u32[]{:S(2)}, u32[]{:S(2)}) collective-permute-start(f32[264,128]{1,0:T(8,128)S(1)} %shard_map.97), channel_id=1, source_target_pairs={{0,8},{1,9},{2,10},{3,11},{4,12},{5,13},{6,14},{7,15},{8,16},{9,17... | collective-permute-start | bytes 405512 | tf_op jit(solution)/shard_map/ppermute | solution.py:433
  29.7 4.2 %collective-permute-start.6 = (f32[256,128]{1,0:T(8,128)S(1)}, f32[256,128]{1,0:T(8,128)S(1)}, u32[]{:S(2)}, u32[]{:S(2)}) collective-permute-start(f32[256,128]{1,0:T(8,128)S(1)} %get-tuple-element.102), channel_id=1, source_target_pairs={{0,2},{1,3},{2,0},{3,1},{4,6},{5,7},{6,4},{7,5},{8,10},{9,11},{10,... | collective-permute-start | bytes 393224 | tf_op jit(solution)/shard_map/ppermute | solution.py:427
  30.7 4.1 %collective-permute-start.7 = (f32[256,128]{1,0:T(8,128)S(1)}, f32[256,128]{1,0:T(8,128)S(1)}, u32[]{:S(2)}, u32[]{:S(2)}) collective-permute-start(f32[256,128]{1,0:T(8,128)S(1)} %get-tuple-element.103), channel_id=1, source_target_pairs={{0,4},{1,5},{2,6},{3,7},{4,0},{5,1},{6,2},{7,3},{8,12},{9,13},{10,... | collective-permute-start | bytes 393224 | tf_op jit(solution)/shard_map/ppermute | solution.py:427
  31.2 6.4 %collective-permute-start.8 = (f32[256,128]{1,0:T(8,128)S(1)}, f32[256,128]{1,0:T(8,128)S(1)}, u32[]{:S(2)}, u32[]{:S(2)}) collective-permute-start(f32[256,128]{1,0:T(8,128)S(1)} %get-tuple-element.104), channel_id=1, source_target_pairs={{0,6},{1,7},{2,4},{3,5},{4,2},{5,3},{6,0},{7,1},{8,14},{9,15},{10,... | collective-permute-start | bytes 393224 | tf_op jit(solution)/shard_map/ppermute | solution.py:427
  41.0 5.8 %collective-permute-start.10 = (f32[272,128]{1,0:T(8,128)S(1)}, f32[272,128]{1,0:T(8,128)S(1)}, u32[]{:S(2)}, u32[]{:S(2)}) collective-permute-start(f32[272,128]{1,0:T(8,128)S(1)} %get-tuple-element.113), channel_id=1, source_target_pairs={{0,2},{1,3},{2,0},{3,1},{4,6},{5,7},{6,4},{7,5},{8,10},{9,11},{10,... | collective-permute-start | bytes 417800 | tf_op jit(solution)/shard_map/ppermute | solution.py:427
  41.0 5.7 %collective-permute-start.11 = (f32[272,128]{1,0:T(8,128)S(1)}, f32[272,128]{1,0:T(8,128)S(1)}, u32[]{:S(2)}, u32[]{:S(2)}) collective-permute-start(f32[272,128]{1,0:T(8,128)S(1)} %get-tuple-element.114), channel_id=1, source_target_pairs={{0,4},{1,5},{2,6},{3,7},{4,0},{5,1},{6,2},{7,3},{8,12},{9,13},{10,... | collective-permute-start | bytes 417800 | tf_op jit(solution)/shard_map/ppermute | solution.py:427
  42.4 6.0 %collective-permute-start.12 = (f32[272,128]{1,0:T(8,128)S(1)}, f32[272,128]{1,0:T(8,128)S(1)}, u32[]{:S(2)}, u32[]{:S(2)}) collective-permute-start(f32[272,128]{1,0:T(8,128)S(1)} %get-tuple-element.115), channel_id=1, source_target_pairs={{0,6},{1,7},{2,4},{3,5},{4,2},{5,3},{6,0},{7,1},{8,14},{9,15},{10,... | collective-permute-start | bytes 417800 | tf_op jit(solution)/shard_map/ppermute | solution.py:427
  49.0 19.5 %collective-permute-start.13 = (f32[384,1024]{1,0:T(8,128)S(1)}, f32[384,1024]{1,0:T(8,128)S(1)}, u32[]{:S(2)}, u32[]{:S(2)}) collective-permute-start(f32[384,1024]{1,0:T(8,128)S(1)} %get-tuple-element.127), channel_id=1, source_target_pairs={{0,1},{1,0},{2,3},{3,2},{4,5},{5,4},{6,7},{7,6},{8,9},{9,8},{10,11... | collective-permute-start | bytes 4718600 | tf_op jit(solution)/shard_map/ppermute | solution.py:423
  51.9 9.9 %collective-permute-start.15 = (f32[272,128]{1,0:T(8,128)S(1)}, f32[272,128]{1,0:T(8,128)S(1)}, u32[]{:S(2)}, u32[]{:S(2)}) collective-permute-start(f32[272,128]{1,0:T(8,128)S(1)} %get-tuple-element.126), channel_id=1, source_target_pairs={{0,16},{1,17},{2,18},{3,19},{4,20},{5,21},{6,22},{7,23},{8,24},{9,... | collective-permute-start | bytes 417800 | tf_op jit(solution)/shard_map/ppermute | solution.py:433
  54.8 7.6 %collective-permute-start.14 = (f32[272,128]{1,0:T(8,128)S(1)}, f32[272,128]{1,0:T(8,128)S(1)}, u32[]{:S(2)}, u32[]{:S(2)}) collective-permute-start(f32[272,128]{1,0:T(8,128)S(1)} %get-tuple-element.126), channel_id=1, source_target_pairs={{0,24},{1,25},{2,26},{3,27},{4,28},{5,29},{6,30},{7,31},{8,0},{9,1... | collective-permute-start | bytes 417800 | tf_op jit(solution)/shard_map/ppermute | solution.py:433
  63.2 8.4 %collective-permute-start.16 = (f32[256,128]{1,0:T(8,128)S(1)}, f32[256,128]{1,0:T(8,128)S(1)}, u32[]{:S(2)}, u32[]{:S(2)}) collective-permute-start(f32[256,128]{1,0:T(8,128)S(1)} %get-tuple-element.132), channel_id=1, source_target_pairs={{0,2},{1,3},{2,0},{3,1},{4,6},{5,7},{6,4},{7,5},{8,10},{9,11},{10,... | collective-permute-start | bytes 393224 | tf_op jit(solution)/shard_map/ppermute | solution.py:427
  63.9 7.7 %collective-permute-start.17 = (f32[256,128]{1,0:T(8,128)S(1)}, f32[256,128]{1,0:T(8,128)S(1)}, u32[]{:S(2)}, u32[]{:S(2)}) collective-permute-start(f32[256,128]{1,0:T(8,128)S(1)} %get-tuple-element.133), channel_id=1, source_target_pairs={{0,4},{1,5},{2,6},{3,7},{4,0},{5,1},{6,2},{7,3},{8,12},{9,13},{10,... | collective-permute-start | bytes 393224 | tf_op jit(solution)/shard_map/ppermute | solution.py:427
  64.8 6.8 %collective-permute-start.18 = (f32[256,128]{1,0:T(8,128)S(1)}, f32[256,128]{1,0:T(8,128)S(1)}, u32[]{:S(2)}, u32[]{:S(2)}) collective-permute-start(f32[256,128]{1,0:T(8,128)S(1)} %get-tuple-element.134), channel_id=1, source_target_pairs={{0,6},{1,7},{2,4},{3,5},{4,2},{5,3},{6,0},{7,1},{8,14},{9,15},{10,... | collective-permute-start | bytes 393224 | tf_op jit(solution)/shard_map/ppermute | solution.py:427
  65.9 5.7 %collective-permute-start.19 = (f32[8,128]{1,0:T(8,128)S(1)}, f32[8,128]{1,0:T(8,128)S(1)}, u32[]{:S(2)}, u32[]{:S(2)}) collective-permute-start(f32[8,128]{1,0:T(8,128)S(1)} %get-tuple-element.146.refs_2_), channel_id=1, source_target_pairs={{0,8},{1,9},{2,10},{3,11},{4,12},{5,13},{6,14},{7,15},{8,16},{9,17... | collective-permute-start | bytes 12296 | tf_op jit(solution)/shard_map/ppermute | solution.py:433
  72.4 3.9 %collective-permute-start.20 = (f32[1032,128]{1,0:T(8,128)S(1)}, f32[1032,128]{1,0:T(8,128)S(1)}, u32[]{:S(2)}, u32[]{:S(2)}) collective-permute-start(f32[1032,128]{1,0:T(8,128)S(1)} %get-tuple-element.147), channel_id=1, source_target_pairs={{0,1},{1,0},{2,3},{3,2},{4,5},{5,4},{6,7},{7,6},{8,9},{9,8},{10,11... | collective-permute-start | bytes 1585160 | tf_op jit(solution)/shard_map/ppermute | solution.py:423

commit v5 on v4

--- a/solution.py
+++ b/solution.py
@@ -10,6 +10,7 @@
 BLK = 128
 EPSILON = 1e-06
 CHIPS = 4
+TURNS = (0, 3, 1, 2)
 GROUP = 2 * CHIPS
 IDS = 8
 FIRST, LAST = 0, 1
@@ -185,7 +186,7 @@
     for turn, chip in enumerate((c0, c1, c2, c3)):
         results = []
         for step in range(chunk):
-            head = lax.bitwise_xor(my_chip(), turn) * chunk + step
+            head = lax.bitwise_xor(my_chip(), TURNS[turn]) * chunk + step
             cols, full = wide(0, head), wide(base, head)
             coming = chip[pl.ds(step * 128, 128), :]
             state = (coming * keep_coming + other[cols, :] * keep_other).astype(BF16)
@@ -299,7 +300,7 @@
     own_weight = match(row(own, rows, LAST), last)
     other_weight = match(row(other, rows, LAST), last)
     for turn, out in enumerate(outs):
-        owner = lax.bitwise_xor(my_chip(), turn)
+        owner = lax.bitwise_xor(my_chip(), TURNS[turn])
         part = pl.ds(pl.multiple_of(owner * size, size), size)
         out[pl.ds(0, size), :] = own[part, :] * own_weight + other[part, :] * other_weight
         out[pl.ds(size, IDS), :] = jnp.zeros((IDS, 128), F32)
@@ -324,7 +325,7 @@
     chips = (c0, c1, c2, c3)
     backward = distances[0] < 0
     others, outs = refs[: len(distances)], refs[-CHIPS:]
-    place = [lax.bitwise_xor(my_chip(), turn) for turn in range(CHIPS)]
+    place = [lax.bitwise_xor(my_chip(), TURNS[turn]) for turn in range(CHIPS)]
     my_plane = lax.axis_index("ctx") // GROUP
     first = functools.reduce(jnp.minimum, [row(c, size, FIRST) for c in chips])
     coming = jnp.zeros((size, 128), F32)
@@ -369,7 +370,7 @@
         row(other, rows, LAST),
     )
     for turn, chip in enumerate((c0, c1, c2, c3)):
-        owner = lax.bitwise_xor(my_chip(), turn)
+        owner = lax.bitwise_xor(my_chip(), TURNS[turn])
         part = pl.ds(pl.multiple_of(owner * size, size), size)
         coming = chip[pl.ds(0, size), :]
         send[part, :] = coming * send_coming + own[part, :] * send_own
@@ -424,7 +425,7 @@
 
     def to_chips(values):
         return [values[0]] + [
-            lax.ppermute(values[turn], "ctx", [(i, i ^ (2 * turn)) for i in range(shards)])
+            lax.ppermute(values[turn], "ctx", [(i, i ^ (2 * TURNS[turn])) for i in range(shards)])
             for turn in (1, 2, 3)
         ]
 

time: 78.6 us -> 79.2 us (level)
  waiting for transfers between devices: 25.5 us -> 27.3 us
  starting transfers between devices: 27.6 us -> 26.3 us
    ppermute x12, waiting for transfers between devices: 9.45 us -> 11.3 us  [to_chips(): lax.ppermute(values[turn], 'ctx', [(i, i ^ 2 * TURNS[turn]) for i in rang...]
    ppermute x4, starting transfers between devices: 6.4 us -> 4.57 us  [swap(): return lax.ppermute(value, 'ctx', [(i, i ^ 1) for i in range(shards)])]
  transfers between devices with their start and end apart: 21 -> 21, of which waited for: 9 -> 11; matrix products, arithmetic and copies ran while one was open for 0% -> 0% of each run, Pallas kernels for 18% -> 18%
where the time goes in v5:
time: 79.2 us; the launch traced here: 79 us
  waiting for transfers between devices  27.3 us (34%)
  starting transfers between devices  26.3 us (33%)
  Pallas kernels  23.7 us (30%)
  between operations  0.98 us (1%)
    pallas_call x13, Pallas kernels, call(): pl.pallas_call(kernel, out_shape=outs, grid_spec=pltpu.PrefetchScalarGrid...  22 us
    ppermute x5, waiting for transfers between devices, around(): return lax.ppermute(value, 'ctx', pairs)  15.7 us
    ppermute x12, starting transfers between devices, to_chips(): lax.ppermute(values[turn], 'ctx', [(i, i ^ 2 * TURNS[turn]) for i in rang...  12.1 us
    ppermute x12, waiting for transfers between devices, to_chips(): lax.ppermute(values[turn], 'ctx', [(i, i ^ 2 * TURNS[turn]) for i in rang...  11.3 us
    ppermute x5, starting transfers between devices, around(): return lax.ppermute(value, 'ctx', pairs)  9.62 us
    ppermute x4, starting transfers between devices, swap(): return lax.ppermute(value, 'ctx', [(i, i ^ 1) for i in range(shards)])  4.57 us
    pallas_call x1, Pallas kernels, local(): pl.pallas_call(functools.partial(first_kernel, half=half), out_shape=[pay...  1.77 us
  transfers between devices with their start and end apart: 21, of which 11 were waited for; matrix products, arithmetic and copies ran while one was open for 0% of the time, Pallas kernels for 18%

profile of v5, /device:TPU:1, one launch (start us, length us, event | category | flops | bytes accessed | tf_op | source)
XLA Modules:
  0.0 79.0 jit_solution(52750429385816340)
XLA Ops:
  0.7 1.8 %shard_map.93 = (f32[1032,128]{1,0:T(8,128)S(1)}, bf16[256,1024]{1,0:T(8,128)(2,1)S(1)}, bf16[256,1024]{1,0:T(8,128)(2,1)S(1)}) custom-call(s32[1,2]{1,0:T(1,128)} %docs.14, bf16[256,2048]{1,0:T(8,128)(2,1)} %bitcast.7, bf16[256,2048]{1,0:T(8,128)(2,1)} %bitcast.13), custom_call_target="tpu_custom_call" | custom-call | flops 67108864 | bytes 2097152 | tf_op jit(solution)/shard_map/pallas_call | solution.py:494
  2.5 0.1 collective-permute-start
  2.6 0.7 copy-done.4
  3.2 0.9 %shard_map.94.own = f32[1032,128]{1,0:T(8,128)S(1)} custom-call(s32[1,2]{1,0:T(1,128)S(1)} %copy-done.4, bf16[256,1024]{1,0:T(8,128)(2,1)S(1)} %get-tuple-element.86.key, bf16[256,1024]{1,0:T(8,128)(2,1)S(1)} %get-tuple-element.87.value), custom_call_target="tpu_custom_call" | custom-call | flops 67108864 | bytes 1576960 | tf_op jit(solution)/shard_map/pallas_call | solution.py:391
  4.1 0.0 copy-start.5
  4.1 0.3 collective-permute-done.other
  4.4 0.6 shard_map.95
  5.1 3.4 %collective-permute-start.1 = (f32[264,128]{1,0:T(8,128)S(1)}, f32[264,128]{1,0:T(8,128)S(1)}, u32[]{:S(2)}, u32[]{:S(2)}) collective-permute-start(f32[264,128]{1,0:T(8,128)S(1)} %get-tuple-element.89), channel_id=1, source_target_pairs={{0,6},{1,7},{2,4},{3,5},{4,2},{5,3},{6,0},{7,1},{8,14},{9,15},{10,... | collective-permute-start | bytes 405512 | tf_op jit(solution)/shard_map/ppermute | solution.py:428
  8.5 0.3 collective-permute-start.2
  8.7 0.1 collective-permute-start.3
  8.9 3.6 %shard_map.96 = (f32[256,1024]{1,0:T(8,128)S(1)}, f32[768,1024]{1,0:T(8,128)S(1)}) custom-call(s32[1,2]{1,0:T(1,128)S(1)} %copy-done.4, bf16[256,2048]{1,0:T(8,128)(2,1)S(1)} %bitcast.19, bf16[256,2048]{1,0:T(8,128)(2,1)S(1)} %bitcast.8, bf16[256,2048]{1,0:T(8,128)(2,1)S(1)} %bitcast.14, bf16[256,2048]{1,0:T(8,128)(2,1)S(1)} %bitcast.23), custom_call_target="tpu_custom_call" | custom-call | flops 536870912 | bytes 8388608 | tf_op jit(solution)/shard_map/pallas_call | solution.py:391
  12.4 2.6 %collective-permute-done.2.c2 = f32[264,128]{1,0:T(8,128)S(1)} collective-permute-done((f32[264,128]{1,0:T(8,128)S(1)}, f32[264,128]{1,0:T(8,128)S(1)}, u32[]{:S(2)}, u32[]{:S(2)}) %collective-permute-start.2) | collective-permute-done | bytes 135200 | tf_op jit(solution)/shard_map/ppermute | solution.py:428
  15.0 0.2 collective-permute-done.3.c3
  15.2 0.6 shard_map.97
  15.8 1.0 %collective-permute-start.9 = (f32[768,1024]{1,0:T(8,128)S(1)}, f32[768,1024]{1,0:T(8,128)S(1)}, u32[]{:S(2)}, u32[]{:S(2)}) collective-permute-start(f32[768,1024]{1,0:T(8,128)S(1)} %get-tuple-element.110), channel_id=1, source_target_pairs={{0,1},{1,0},{2,3},{3,2},{4,5},{5,4},{6,7},{7,6},{8,9},{9,8},{10,11... | collective-permute-start | bytes 9437192 | tf_op jit(solution)/shard_map/ppermute | solution.py:424
  16.9 2.3 %collective-permute-start.5 = (f32[264,128]{1,0:T(8,128)S(1)}, f32[264,128]{1,0:T(8,128)S(1)}, u32[]{:S(2)}, u32[]{:S(2)}) collective-permute-start(f32[264,128]{1,0:T(8,128)S(1)} %shard_map.97), channel_id=1, source_target_pairs={{0,16},{1,17},{2,18},{3,19},{4,20},{5,21},{6,22},{7,23},{8,24},{9,... | collective-permute-start | bytes 405512 | tf_op jit(solution)/shard_map/ppermute | solution.py:434
  19.2 1.3 %collective-permute-start.4 = (f32[264,128]{1,0:T(8,128)S(1)}, f32[264,128]{1,0:T(8,128)S(1)}, u32[]{:S(2)}, u32[]{:S(2)}) collective-permute-start(f32[264,128]{1,0:T(8,128)S(1)} %shard_map.97), channel_id=1, source_target_pairs={{0,8},{1,9},{2,10},{3,11},{4,12},{5,13},{6,14},{7,15},{8,16},{9,17... | collective-permute-start | bytes 405512 | tf_op jit(solution)/shard_map/ppermute | solution.py:434
  20.5 8.2 %collective-permute-done.5.refs_1_ = f32[264,128]{1,0:T(8,128)S(1)} collective-permute-done((f32[264,128]{1,0:T(8,128)S(1)}, f32[264,128]{1,0:T(8,128)S(1)}, u32[]{:S(2)}, u32[]{:S(2)}) %collective-permute-start.5) | collective-permute-done | bytes 135200 | tf_op jit(solution)/shard_map/ppermute | solution.py:434
  28.7 0.7 shard_map.98
  29.5 2.1 %collective-permute-start.6 = (f32[256,128]{1,0:T(8,128)S(1)}, f32[256,128]{1,0:T(8,128)S(1)}, u32[]{:S(2)}, u32[]{:S(2)}) collective-permute-start(f32[256,128]{1,0:T(8,128)S(1)} %get-tuple-element.102), channel_id=1, source_target_pairs={{0,6},{1,7},{2,4},{3,5},{4,2},{5,3},{6,0},{7,1},{8,14},{9,15},{10,... | collective-permute-start | bytes 393224 | tf_op jit(solution)/shard_map/ppermute | solution.py:428
  31.6 0.3 collective-permute-start.7
  31.9 0.3 collective-permute-start.8
  32.2 2.4 %collective-permute-done.6.c1 = f32[256,128]{1,0:T(8,128)S(1)} collective-permute-done((f32[256,128]{1,0:T(8,128)S(1)}, f32[256,128]{1,0:T(8,128)S(1)}, u32[]{:S(2)}, u32[]{:S(2)}) %collective-permute-start.6) | collective-permute-done | bytes 131104 | tf_op jit(solution)/shard_map/ppermute | solution.py:428
  34.6 2.8 %collective-permute-done.7.c2 = f32[256,128]{1,0:T(8,128)S(1)} collective-permute-done((f32[256,128]{1,0:T(8,128)S(1)}, f32[256,128]{1,0:T(8,128)S(1)}, u32[]{:S(2)}, u32[]{:S(2)}) %collective-permute-start.7) | collective-permute-done | bytes 131104 | tf_op jit(solution)/shard_map/ppermute | solution.py:428
  37.4 0.4 collective-permute-done.8.c3
  37.8 3.3 %shard_map.99 = (f32[272,128]{1,0:T(8,128)S(1)}, f32[272,128]{1,0:T(8,128)S(1)}, f32[272,128]{1,0:T(8,128)S(1)}, f32[272,128]{1,0:T(8,128)S(1)}, f32[1032,128]{1...) custom-call(s32[1,2]{1,0:T(1,128)S(1)} %copy-done.4, ...), custom_call_target="tpu_custom_call" | custom-call | flops 268435456 | bytes 11853824 | tf_op jit(solution)/shard_map/pallas_call | solution.py:391
  41.0 2.6 %collective-permute-start.10 = (f32[272,128]{1,0:T(8,128)S(1)}, f32[272,128]{1,0:T(8,128)S(1)}, u32[]{:S(2)}, u32[]{:S(2)}) collective-permute-start(f32[272,128]{1,0:T(8,128)S(1)} %get-tuple-element.113), channel_id=1, source_target_pairs={{0,6},{1,7},{2,4},{3,5},{4,2},{5,3},{6,0},{7,1},{8,14},{9,15},{10,... | collective-permute-start | bytes 417800 | tf_op jit(solution)/shard_map/ppermute | solution.py:428
  43.6 0.3 collective-permute-start.11
  43.9 0.1 collective-permute-start.12
  44.0 3.1 %shard_map.100 = (bf16[256,2048]{1,0:T(8,128)(2,1)}, f32[256,1024]{1,0:T(8,128)S(1)}, f32[256,1024]{1,0:T(8,128)S(1)}) custom-call(s32[1,2]{1,0:T(1,128)S(1)} %copy-done.4, bf16[256,2048]{1,0:T(8,128)(2,1)S(1)} %bitcast.21, bf16[256,2048]{1,0:T(8,128)(2,1)S(1)} %bitcast.9, bf16[256,2048]{1,0:T(8,128)(2,1)S(1)} %bitcast.15, ...), custom_call_target="tpu_custom_call" | custom-call | flops 872415232 | bytes 7077888 | tf_op jit(solution)/shard_map/pallas_call | solution.py:391
  47.0 2.6 %collective-permute-done.11.c2 = f32[272,128]{1,0:T(8,128)S(1)} collective-permute-done((f32[272,128]{1,0:T(8,128)S(1)}, f32[272,128]{1,0:T(8,128)S(1)}, u32[]{:S(2)}, u32[]{:S(2)}) %collective-permute-start.11) | collective-permute-done | bytes 139296 | tf_op jit(solution)/shard_map/ppermute | solution.py:428
  49.6 0.4 collective-permute-done.12.c3
  50.0 0.6 shard_map.101
  50.6 1.6 %collective-permute-start.13 = (f32[384,1024]{1,0:T(8,128)S(1)}, f32[384,1024]{1,0:T(8,128)S(1)}, u32[]{:S(2)}, u32[]{:S(2)}) collective-permute-start(f32[384,1024]{1,0:T(8,128)S(1)} %get-tuple-element.127), channel_id=1, source_target_pairs={{0,1},{1,0},{2,3},{3,2},{4,5},{5,4},{6,7},{7,6},{8,9},{9,8},{10,11... | collective-permute-start | bytes 4718600 | tf_op jit(solution)/shard_map/ppermute | solution.py:424
  52.1 3.2 %collective-permute-start.15 = (f32[272,128]{1,0:T(8,128)S(1)}, f32[272,128]{1,0:T(8,128)S(1)}, u32[]{:S(2)}, u32[]{:S(2)}) collective-permute-start(f32[272,128]{1,0:T(8,128)S(1)} %get-tuple-element.126), channel_id=1, source_target_pairs={{0,16},{1,17},{2,18},{3,19},{4,20},{5,21},{6,22},{7,23},{8,24},{9,... | collective-permute-start | bytes 417800 | tf_op jit(solution)/shard_map/ppermute | solution.py:434
  55.3 0.2 collective-permute-start.14
  55.5 6.8 %collective-permute-done.15.refs_1_ = f32[272,128]{1,0:T(8,128)S(1)} collective-permute-done((f32[272,128]{1,0:T(8,128)S(1)}, f32[272,128]{1,0:T(8,128)S(1)}, u32[]{:S(2)}, u32[]{:S(2)}) %collective-permute-start.15) | collective-permute-done | bytes 139296 | tf_op jit(solution)/shard_map/ppermute | solution.py:434
  62.3 0.6 collective-permute-done.14.refs_0_
  63.0 0.7 shard_map.102
  63.7 2.1 %collective-permute-start.16 = (f32[256,128]{1,0:T(8,128)S(1)}, f32[256,128]{1,0:T(8,128)S(1)}, u32[]{:S(2)}, u32[]{:S(2)}) collective-permute-start(f32[256,128]{1,0:T(8,128)S(1)} %get-tuple-element.132), channel_id=1, source_target_pairs={{0,6},{1,7},{2,4},{3,5},{4,2},{5,3},{6,0},{7,1},{8,14},{9,15},{10,... | collective-permute-start | bytes 393224 | tf_op jit(solution)/shard_map/ppermute | solution.py:428
  65.8 0.3 collective-permute-start.17
  66.1 0.3 collective-permute-start.18
  66.4 2.6 %collective-permute-start.19 = (f32[8,128]{1,0:T(8,128)S(1)}, f32[8,128]{1,0:T(8,128)S(1)}, u32[]{:S(2)}, u32[]{:S(2)}) collective-permute-start(f32[8,128]{1,0:T(8,128)S(1)} %get-tuple-element.146.refs_2_), channel_id=1, source_target_pairs={{0,8},{1,9},{2,10},{3,11},{4,12},{5,13},{6,14},{7,15},{8,16},{9,17... | collective-permute-start | bytes 12296 | tf_op jit(solution)/shard_map/ppermute | solution.py:434
  69.1 3.1 %shard_map.103 = (bf16[256,2048]{1,0:T(8,128)(2,1)}, f32[256,1024]{1,0:T(8,128)S(1)}, f32[256,1024]{1,0:T(8,128)S(1)}) custom-call(s32[1,2]{1,0:T(1,128)S(1)} %copy-done.4, bf16[256,2048]{1,0:T(8,128)(2,1)S(1)} %bitcast.22, bf16[256,2048]{1,0:T(8,128)(2,1)S(1)} %bitcast.10, bf16[256,2048]{1,0:T(8,128)(2,1)S(1)} %bitcast.16, ...), custom_call_target="tpu_custom_call", output_to_operand_aliasing={{0}: (5, {})} | custom-call | flops 872415232 | bytes 8912896 | tf_op jit(solution)/shard_map/pallas_call | solution.py:391
  72.2 0.7 shard_map.104
  72.9 1.8 %collective-permute-start.20 = (f32[1032,128]{1,0:T(8,128)S(1)}, f32[1032,128]{1,0:T(8,128)S(1)}, u32[]{:S(2)}, u32[]{:S(2)}) collective-permute-start(f32[1032,128]{1,0:T(8,128)S(1)} %get-tuple-element.147), channel_id=1, source_target_pairs={{0,1},{1,0},{2,3},{3,2},{4,5},{5,4},{6,7},{7,6},{8,9},{9,8},{10,11... | collective-permute-start | bytes 1585160 | tf_op jit(solution)/shard_map/ppermute | solution.py:424
  74.7 2.0 %shard_map.105 = (bf16[256,2048]{1,0:T(8,128)(2,1)}, bf16[256,2048]{1,0:T(8,128)(2,1)}) custom-call(s32[1,2]{1,0:T(1,128)S(1)} %copy-done.4, bf16[256,2048]{1,0:T(8,128)(2,1)S(1)} %bitcast.11, bf16[256,2048]{1,0:T(8,128)(2,1)S(1)} %bitcast.17, f32[256,1024]{1,0:T(8,128)S(1)} %get-tuple-element.120.key_part, f32[256,1024]{1,0:T(8,128)S(1)} %get-tuple-element.121.value_part, ...), custom_call_target="tpu_custom_call" | custom-call | flops 134217728 | bytes 6553600 | tf_op jit(solution)/shard_map/pallas_call | solution.py:391
  76.8 2.1 %shard_map.106 = (bf16[256,2048]{1,0:T(8,128)(2,1)}, bf16[256,2048]{1,0:T(8,128)(2,1)}, f32[16,128]{1,0:T(8,128)}) custom-call(s32[1,2]{1,0:T(1,128)S(1)} %copy-done.4, bf16[256,2048]{1,0:T(8,128)(2,1)S(1)} %bitcast.12, bf16[256,2048]{1,0:T(8,128)(2,1)S(1)} %bitcast.18, ...), custom_call_target="tpu_custom_call", output_to_operand_aliasing={{0}: (7, {}), {1}: (8, {})} | custom-call | flops 134217728 | bytes 8929280 | tf_op jit(solution)/shard_map/pallas_call | solution.py:391
  (20 shorter events, 0.0 us)
Async XLA Ops:
  0.6 8.2 %copy-start.1 = (bf16[1,256,2048]{2,1,0:T(8,128)(2,1)S(1)}, bf16[1,256,2048]{2,1,0:T(8,128)(2,1)}, u32[]{:S(2)}) copy-start(bf16[1,256,2048]{2,1,0:T(8,128)(2,1)} %param.8) | copy-start | bytes 3145732
  0.6 8.2 %copy-start = (bf16[1,256,2048]{2,1,0:T(8,128)(2,1)S(1)}, bf16[1,256,2048]{2,1,0:T(8,128)(2,1)}, u32[]{:S(2)}) copy-start(bf16[1,256,2048]{2,1,0:T(8,128)(2,1)} %param.7) | copy-start | bytes 3145732
  0.7 8.2 %copy-start.3 = (bf16[1,256,2048]{2,1,0:T(8,128)(2,1)S(1)}, bf16[1,256,2048]{2,1,0:T(8,128)(2,1)}, u32[]{:S(2)}) copy-start(bf16[1,256,2048]{2,1,0:T(8,128)(2,1)} %param.9) | copy-start | bytes 3145732
  0.7 8.2 %copy-start.2 = (bf16[1,256,2048]{2,1,0:T(8,128)(2,1)S(1)}, bf16[1,256,2048]{2,1,0:T(8,128)(2,1)}, u32[]{:S(2)}) copy-start(bf16[1,256,2048]{2,1,0:T(8,128)(2,1)} %param.6) | copy-start | bytes 3145732
  2.5 2.0 %collective-permute-start = (f32[1032,128]{1,0:T(8,128)S(1)}, f32[1032,128]{1,0:T(8,128)S(1)}, u32[]{:S(2)}, u32[]{:S(2)}) collective-permute-start(f32[1032,128]{1,0:T(8,128)S(1)} %get-tuple-element.81), channel_id=1, source_target_pairs={{0,1},{1,0},{2,3},{3,2},{4,5},{5,4},{6,7},{7,6},{8,9},{9,8},{10,11... | collective-permute-start | bytes 1585160 | tf_op jit(solution)/shard_map/ppermute | solution.py:424
  2.6 0.7 copy-start.4
  4.1 33.6 %copy-start.5 = (f32[16,128]{1,0:T(8,128)S(1)}, f32[16,128]{1,0:T(8,128)}, u32[]{:S(2)}) copy-start(f32[16,128]{1,0:T(8,128)} %gain.1) | copy-start | bytes 24580
  5.1 7.3 %collective-permute-start.1 = (f32[264,128]{1,0:T(8,128)S(1)}, f32[264,128]{1,0:T(8,128)S(1)}, u32[]{:S(2)}, u32[]{:S(2)}) collective-permute-start(f32[264,128]{1,0:T(8,128)S(1)} %get-tuple-element.89), channel_id=1, source_target_pairs={{0,6},{1,7},{2,4},{3,5},{4,2},{5,3},{6,0},{7,1},{8,14},{9,15},{10,... | collective-permute-start | bytes 405512 | tf_op jit(solution)/shard_map/ppermute | solution.py:428
  8.5 6.6 %collective-permute-start.2 = (f32[264,128]{1,0:T(8,128)S(1)}, f32[264,128]{1,0:T(8,128)S(1)}, u32[]{:S(2)}, u32[]{:S(2)}) collective-permute-start(f32[264,128]{1,0:T(8,128)S(1)} %get-tuple-element.90), channel_id=1, source_target_pairs={{0,2},{1,3},{2,0},{3,1},{4,6},{5,7},{6,4},{7,5},{8,10},{9,11},{10,... | collective-permute-start | bytes 405512 | tf_op jit(solution)/shard_map/ppermute | solution.py:428
  8.7 6.5 %collective-permute-start.3 = (f32[264,128]{1,0:T(8,128)S(1)}, f32[264,128]{1,0:T(8,128)S(1)}, u32[]{:S(2)}, u32[]{:S(2)}) collective-permute-start(f32[264,128]{1,0:T(8,128)S(1)} %get-tuple-element.91), channel_id=1, source_target_pairs={{0,4},{1,5},{2,6},{3,7},{4,0},{5,1},{6,2},{7,3},{8,12},{9,13},{10,... | collective-permute-start | bytes 405512 | tf_op jit(solution)/shard_map/ppermute | solution.py:428
  15.8 21.9 %collective-permute-start.9 = (f32[768,1024]{1,0:T(8,128)S(1)}, f32[768,1024]{1,0:T(8,128)S(1)}, u32[]{:S(2)}, u32[]{:S(2)}) collective-permute-start(f32[768,1024]{1,0:T(8,128)S(1)} %get-tuple-element.110), channel_id=1, source_target_pairs={{0,1},{1,0},{2,3},{3,2},{4,5},{5,4},{6,7},{7,6},{8,9},{9,8},{10,11... | collective-permute-start | bytes 9437192 | tf_op jit(solution)/shard_map/ppermute | solution.py:424
  16.9 11.9 %collective-permute-start.5 = (f32[264,128]{1,0:T(8,128)S(1)}, f32[264,128]{1,0:T(8,128)S(1)}, u32[]{:S(2)}, u32[]{:S(2)}) collective-permute-start(f32[264,128]{1,0:T(8,128)S(1)} %shard_map.97), channel_id=1, source_target_pairs={{0,16},{1,17},{2,18},{3,19},{4,20},{5,21},{6,22},{7,23},{8,24},{9,... | collective-permute-start | bytes 405512 | tf_op jit(solution)/shard_map/ppermute | solution.py:434
  19.2 9.5 %collective-permute-start.4 = (f32[264,128]{1,0:T(8,128)S(1)}, f32[264,128]{1,0:T(8,128)S(1)}, u32[]{:S(2)}, u32[]{:S(2)}) collective-permute-start(f32[264,128]{1,0:T(8,128)S(1)} %shard_map.97), channel_id=1, source_target_pairs={{0,8},{1,9},{2,10},{3,11},{4,12},{5,13},{6,14},{7,15},{8,16},{9,17... | collective-permute-start | bytes 405512 | tf_op jit(solution)/shard_map/ppermute | solution.py:434
  29.5 5.1 %collective-permute-start.6 = (f32[256,128]{1,0:T(8,128)S(1)}, f32[256,128]{1,0:T(8,128)S(1)}, u32[]{:S(2)}, u32[]{:S(2)}) collective-permute-start(f32[256,128]{1,0:T(8,128)S(1)} %get-tuple-element.102), channel_id=1, source_target_pairs={{0,6},{1,7},{2,4},{3,5},{4,2},{5,3},{6,0},{7,1},{8,14},{9,15},{10,... | collective-permute-start | bytes 393224 | tf_op jit(solution)/shard_map/ppermute | solution.py:428
  31.6 5.8 %collective-permute-start.7 = (f32[256,128]{1,0:T(8,128)S(1)}, f32[256,128]{1,0:T(8,128)S(1)}, u32[]{:S(2)}, u32[]{:S(2)}) collective-permute-start(f32[256,128]{1,0:T(8,128)S(1)} %get-tuple-element.103), channel_id=1, source_target_pairs={{0,2},{1,3},{2,0},{3,1},{4,6},{5,7},{6,4},{7,5},{8,10},{9,11},{10,... | collective-permute-start | bytes 393224 | tf_op jit(solution)/shard_map/ppermute | solution.py:428
  31.9 5.9 %collective-permute-start.8 = (f32[256,128]{1,0:T(8,128)S(1)}, f32[256,128]{1,0:T(8,128)S(1)}, u32[]{:S(2)}, u32[]{:S(2)}) collective-permute-start(f32[256,128]{1,0:T(8,128)S(1)} %get-tuple-element.104), channel_id=1, source_target_pairs={{0,4},{1,5},{2,6},{3,7},{4,0},{5,1},{6,2},{7,3},{8,12},{9,13},{10,... | collective-permute-start | bytes 393224 | tf_op jit(solution)/shard_map/ppermute | solution.py:428
  41.0 6.0 %collective-permute-start.10 = (f32[272,128]{1,0:T(8,128)S(1)}, f32[272,128]{1,0:T(8,128)S(1)}, u32[]{:S(2)}, u32[]{:S(2)}) collective-permute-start(f32[272,128]{1,0:T(8,128)S(1)} %get-tuple-element.113), channel_id=1, source_target_pairs={{0,6},{1,7},{2,4},{3,5},{4,2},{5,3},{6,0},{7,1},{8,14},{9,15},{10,... | collective-permute-start | bytes 417800 | tf_op jit(solution)/shard_map/ppermute | solution.py:428
  43.6 6.0 %collective-permute-start.11 = (f32[272,128]{1,0:T(8,128)S(1)}, f32[272,128]{1,0:T(8,128)S(1)}, u32[]{:S(2)}, u32[]{:S(2)}) collective-permute-start(f32[272,128]{1,0:T(8,128)S(1)} %get-tuple-element.114), channel_id=1, source_target_pairs={{0,2},{1,3},{2,0},{3,1},{4,6},{5,7},{6,4},{7,5},{8,10},{9,11},{10,... | collective-permute-start | bytes 417800 | tf_op jit(solution)/shard_map/ppermute | solution.py:428
  43.9 6.1 %collective-permute-start.12 = (f32[272,128]{1,0:T(8,128)S(1)}, f32[272,128]{1,0:T(8,128)S(1)}, u32[]{:S(2)}, u32[]{:S(2)}) collective-permute-start(f32[272,128]{1,0:T(8,128)S(1)} %get-tuple-element.115), channel_id=1, source_target_pairs={{0,4},{1,5},{2,6},{3,7},{4,0},{5,1},{6,2},{7,3},{8,12},{9,13},{10,... | collective-permute-start | bytes 417800 | tf_op jit(solution)/shard_map/ppermute | solution.py:428
  50.6 18.5 %collective-permute-start.13 = (f32[384,1024]{1,0:T(8,128)S(1)}, f32[384,1024]{1,0:T(8,128)S(1)}, u32[]{:S(2)}, u32[]{:S(2)}) collective-permute-start(f32[384,1024]{1,0:T(8,128)S(1)} %get-tuple-element.127), channel_id=1, source_target_pairs={{0,1},{1,0},{2,3},{3,2},{4,5},{5,4},{6,7},{7,6},{8,9},{9,8},{10,11... | collective-permute-start | bytes 4718600 | tf_op jit(solution)/shard_map/ppermute | solution.py:424
  52.1 10.2 %collective-permute-start.15 = (f32[272,128]{1,0:T(8,128)S(1)}, f32[272,128]{1,0:T(8,128)S(1)}, u32[]{:S(2)}, u32[]{:S(2)}) collective-permute-start(f32[272,128]{1,0:T(8,128)S(1)} %get-tuple-element.126), channel_id=1, source_target_pairs={{0,16},{1,17},{2,18},{3,19},{4,20},{5,21},{6,22},{7,23},{8,24},{9,... | collective-permute-start | bytes 417800 | tf_op jit(solution)/shard_map/ppermute | solution.py:434
  55.3 7.6 %collective-permute-start.14 = (f32[272,128]{1,0:T(8,128)S(1)}, f32[272,128]{1,0:T(8,128)S(1)}, u32[]{:S(2)}, u32[]{:S(2)}) collective-permute-start(f32[272,128]{1,0:T(8,128)S(1)} %get-tuple-element.126), channel_id=1, source_target_pairs={{0,24},{1,25},{2,26},{3,27},{4,28},{5,29},{6,30},{7,31},{8,0},{9,1... | collective-permute-start | bytes 417800 | tf_op jit(solution)/shard_map/ppermute | solution.py:434
  63.7 8.4 %collective-permute-start.16 = (f32[256,128]{1,0:T(8,128)S(1)}, f32[256,128]{1,0:T(8,128)S(1)}, u32[]{:S(2)}, u32[]{:S(2)}) collective-permute-start(f32[256,128]{1,0:T(8,128)S(1)} %get-tuple-element.132), channel_id=1, source_target_pairs={{0,6},{1,7},{2,4},{3,5},{4,2},{5,3},{6,0},{7,1},{8,14},{9,15},{10,... | collective-permute-start | bytes 393224 | tf_op jit(solution)/shard_map/ppermute | solution.py:428
  65.8 6.3 %collective-permute-start.17 = (f32[256,128]{1,0:T(8,128)S(1)}, f32[256,128]{1,0:T(8,128)S(1)}, u32[]{:S(2)}, u32[]{:S(2)}) collective-permute-start(f32[256,128]{1,0:T(8,128)S(1)} %get-tuple-element.133), channel_id=1, source_target_pairs={{0,2},{1,3},{2,0},{3,1},{4,6},{5,7},{6,4},{7,5},{8,10},{9,11},{10,... | collective-permute-start | bytes 393224 | tf_op jit(solution)/shard_map/ppermute | solution.py:428
  66.1 6.0 %collective-permute-start.18 = (f32[256,128]{1,0:T(8,128)S(1)}, f32[256,128]{1,0:T(8,128)S(1)}, u32[]{:S(2)}, u32[]{:S(2)}) collective-permute-start(f32[256,128]{1,0:T(8,128)S(1)} %get-tuple-element.134), channel_id=1, source_target_pairs={{0,4},{1,5},{2,6},{3,7},{4,0},{5,1},{6,2},{7,3},{8,12},{9,13},{10,... | collective-permute-start | bytes 393224 | tf_op jit(solution)/shard_map/ppermute | solution.py:428
  66.4 5.7 %collective-permute-start.19 = (f32[8,128]{1,0:T(8,128)S(1)}, f32[8,128]{1,0:T(8,128)S(1)}, u32[]{:S(2)}, u32[]{:S(2)}) collective-permute-start(f32[8,128]{1,0:T(8,128)S(1)} %get-tuple-element.146.refs_2_), channel_id=1, source_target_pairs={{0,8},{1,9},{2,10},{3,11},{4,12},{5,13},{6,14},{7,15},{8,16},{9,17... | collective-permute-start | bytes 12296 | tf_op jit(solution)/shard_map/ppermute | solution.py:434
  72.9 3.9 %collective-permute-start.20 = (f32[1032,128]{1,0:T(8,128)S(1)}, f32[1032,128]{1,0:T(8,128)S(1)}, u32[]{:S(2)}, u32[]{:S(2)}) collective-permute-start(f32[1032,128]{1,0:T(8,128)S(1)} %get-tuple-element.147), channel_id=1, source_target_pairs={{0,1},{1,0},{2,3},{3,2},{4,5},{5,4},{6,7},{7,6},{8,9},{9,8},{10,11... | collective-permute-start | bytes 1585160 | tf_op jit(solution)/shard_map/ppermute | solution.py:424

commit v6 on v4

--- a/solution.py
+++ b/solution.py
@@ -445,7 +445,7 @@
         )
         distances = (-1, -2) if backward else (1, 2)
         others = [around(plane, distance) for distance in distances]
-        others = tie(others, beside_planes(plane))
+        others = tie(others, beside_planes(plane, others))
         sent = call(
             functools.partial(chain_kernel, size=size, distances=distances, planes=planes),
             doc_ids,
@@ -534,7 +534,7 @@
         )
         return kept["inside"]
 
-    def forward_message(plane):
+    def forward_message(plane, others):
         kept["message"] = swap(tie(kept["message"], plane))
         return []
 
@@ -553,8 +553,8 @@
         kept["first"] = within(False, [tie(attn, sent), state], None)
         return kept["first"]
 
-    def beside_planes(plane):
-        kept["reply"] = swap(tie(reply, plane))
+    def beside_planes(plane, others):
+        kept["reply"] = swap(tie(reply, others))
         return []
 
     def beside_down(sent, gain):

time: 78.6 us -> 76.8 us (0.977)
  starting transfers between devices: 27.6 us -> 26.6 us
  waiting for transfers between devices: 25.5 us -> 24.6 us
    ppermute x5, waiting for transfers between devices: 15.7 us -> 14.2 us  [around(): return lax.ppermute(value, 'ctx', pairs)]
where the time goes in v6:
time: 76.8 us; the launch traced here: 76.6 us
  starting transfers between devices  26.6 us (35%)
  waiting for transfers between devices  24.6 us (32%)
  Pallas kernels  23.7 us (31%)
  between operations  0.99 us (1%)
    pallas_call x13, Pallas kernels, call(): pl.pallas_call(kernel, out_shape=outs, grid_spec=pltpu.PrefetchScalarGrid...  22 us
    ppermute x5, waiting for transfers between devices, around(): return lax.ppermute(value, 'ctx', pairs)  14.2 us
    ppermute x12, starting transfers between devices, to_chips(): lax.ppermute(values[turn], 'ctx', [(i, i ^ 2 * turn) for i in range(shard...  11.8 us
    ppermute x12, waiting for transfers between devices, to_chips(): lax.ppermute(values[turn], 'ctx', [(i, i ^ 2 * turn) for i in range(shard...  10.1 us
    ppermute x5, starting transfers between devices, around(): return lax.ppermute(value, 'ctx', pairs)  9.11 us
    ppermute x4, starting transfers between devices, swap(): return lax.ppermute(value, 'ctx', [(i, i ^ 1) for i in range(shards)])  5.66 us
    pallas_call x1, Pallas kernels, local(): pl.pallas_call(functools.partial(first_kernel, half=half), out_shape=[pay...  1.77 us
  transfers between devices with their start and end apart: 21, of which 9 were waited for; matrix products, arithmetic and copies ran while one was open for 0% of the time, Pallas kernels for 18%

profile of v6, /device:TPU:1, one launch (start us, length us, event | category | flops | bytes accessed | tf_op | source)
XLA Modules:
  0.0 76.6 jit_solution(1869937139788299539)
XLA Ops:
  0.7 1.8 %shard_map.93 = (f32[1032,128]{1,0:T(8,128)S(1)}, bf16[256,1024]{1,0:T(8,128)(2,1)S(1)}, bf16[256,1024]{1,0:T(8,128)(2,1)S(1)}) custom-call(s32[1,2]{1,0:T(1,128)} %docs.14, bf16[256,2048]{1,0:T(8,128)(2,1)} %bitcast.7, bf16[256,2048]{1,0:T(8,128)(2,1)} %bitcast.13), custom_call_target="tpu_custom_call" | custom-call | flops 67108864 | bytes 2097152 | tf_op jit(solution)/shard_map/pallas_call | solution.py:493
  2.5 0.1 collective-permute-start
  2.6 0.7 copy-done.4
  3.2 0.9 %shard_map.94.own = f32[1032,128]{1,0:T(8,128)S(1)} custom-call(s32[1,2]{1,0:T(1,128)S(1)} %copy-done.4, bf16[256,1024]{1,0:T(8,128)(2,1)S(1)} %get-tuple-element.86.key, bf16[256,1024]{1,0:T(8,128)(2,1)S(1)} %get-tuple-element.87.value), custom_call_target="tpu_custom_call" | custom-call | flops 67108864 | bytes 1576960 | tf_op jit(solution)/shard_map/pallas_call | solution.py:390
  4.1 0.0 copy-start.5
  4.1 0.3 collective-permute-done.other
  4.4 0.6 shard_map.95
  5.1 2.4 %collective-permute-start.1 = (f32[264,128]{1,0:T(8,128)S(1)}, f32[264,128]{1,0:T(8,128)S(1)}, u32[]{:S(2)}, u32[]{:S(2)}) collective-permute-start(f32[264,128]{1,0:T(8,128)S(1)} %get-tuple-element.89), channel_id=1, source_target_pairs={{0,2},{1,3},{2,0},{3,1},{4,6},{5,7},{6,4},{7,5},{8,10},{9,11},{10,... | collective-permute-start | bytes 405512 | tf_op jit(solution)/shard_map/ppermute | solution.py:427
  7.5 1.2 %collective-permute-start.2 = (f32[264,128]{1,0:T(8,128)S(1)}, f32[264,128]{1,0:T(8,128)S(1)}, u32[]{:S(2)}, u32[]{:S(2)}) collective-permute-start(f32[264,128]{1,0:T(8,128)S(1)} %get-tuple-element.90), channel_id=1, source_target_pairs={{0,4},{1,5},{2,6},{3,7},{4,0},{5,1},{6,2},{7,3},{8,12},{9,13},{10,... | collective-permute-start | bytes 405512 | tf_op jit(solution)/shard_map/ppermute | solution.py:427
  8.8 0.0 collective-permute-start.3
  8.8 3.6 %shard_map.96 = (f32[256,1024]{1,0:T(8,128)S(1)}, f32[768,1024]{1,0:T(8,128)S(1)}) custom-call(s32[1,2]{1,0:T(1,128)S(1)} %copy-done.4, bf16[256,2048]{1,0:T(8,128)(2,1)S(1)} %bitcast.19, bf16[256,2048]{1,0:T(8,128)(2,1)S(1)} %bitcast.8, bf16[256,2048]{1,0:T(8,128)(2,1)S(1)} %bitcast.14, bf16[256,2048]{1,0:T(8,128)(2,1)S(1)} %bitcast.23), custom_call_target="tpu_custom_call" | custom-call | flops 536870912 | bytes 8388608 | tf_op jit(solution)/shard_map/pallas_call | solution.py:390
  12.4 0.0 collective-permute-done.2.c2
  12.4 2.5 %collective-permute-done.3.c3 = f32[264,128]{1,0:T(8,128)S(1)} collective-permute-done((f32[264,128]{1,0:T(8,128)S(1)}, f32[264,128]{1,0:T(8,128)S(1)}, u32[]{:S(2)}, u32[]{:S(2)}) %collective-permute-start.3) | collective-permute-done | bytes 135200 | tf_op jit(solution)/shard_map/ppermute | solution.py:427
  14.9 0.6 shard_map.97
  15.5 1.6 %collective-permute-start.9 = (f32[768,1024]{1,0:T(8,128)S(1)}, f32[768,1024]{1,0:T(8,128)S(1)}, u32[]{:S(2)}, u32[]{:S(2)}) collective-permute-start(f32[768,1024]{1,0:T(8,128)S(1)} %get-tuple-element.110), channel_id=1, source_target_pairs={{0,1},{1,0},{2,3},{3,2},{4,5},{5,4},{6,7},{7,6},{8,9},{9,8},{10,11... | collective-permute-start | bytes 9437192 | tf_op jit(solution)/shard_map/ppermute | solution.py:423
  17.1 2.3 %collective-permute-start.5 = (f32[264,128]{1,0:T(8,128)S(1)}, f32[264,128]{1,0:T(8,128)S(1)}, u32[]{:S(2)}, u32[]{:S(2)}) collective-permute-start(f32[264,128]{1,0:T(8,128)S(1)} %shard_map.97), channel_id=1, source_target_pairs={{0,16},{1,17},{2,18},{3,19},{4,20},{5,21},{6,22},{7,23},{8,24},{9,... | collective-permute-start | bytes 405512 | tf_op jit(solution)/shard_map/ppermute | solution.py:433
  19.4 1.3 %collective-permute-start.4 = (f32[264,128]{1,0:T(8,128)S(1)}, f32[264,128]{1,0:T(8,128)S(1)}, u32[]{:S(2)}, u32[]{:S(2)}) collective-permute-start(f32[264,128]{1,0:T(8,128)S(1)} %shard_map.97), channel_id=1, source_target_pairs={{0,8},{1,9},{2,10},{3,11},{4,12},{5,13},{6,14},{7,15},{8,16},{9,17... | collective-permute-start | bytes 405512 | tf_op jit(solution)/shard_map/ppermute | solution.py:433
  20.7 8.2 %collective-permute-done.5.refs_1_ = f32[264,128]{1,0:T(8,128)S(1)} collective-permute-done((f32[264,128]{1,0:T(8,128)S(1)}, f32[264,128]{1,0:T(8,128)S(1)}, u32[]{:S(2)}, u32[]{:S(2)}) %collective-permute-start.5) | collective-permute-done | bytes 135200 | tf_op jit(solution)/shard_map/ppermute | solution.py:433
  28.9 0.0 collective-permute-done.4.refs_0_
  28.9 0.7 shard_map.98
  29.7 1.0 %collective-permute-start.6 = (f32[256,128]{1,0:T(8,128)S(1)}, f32[256,128]{1,0:T(8,128)S(1)}, u32[]{:S(2)}, u32[]{:S(2)}) collective-permute-start(f32[256,128]{1,0:T(8,128)S(1)} %get-tuple-element.102), channel_id=1, source_target_pairs={{0,2},{1,3},{2,0},{3,1},{4,6},{5,7},{6,4},{7,5},{8,10},{9,11},{10,... | collective-permute-start | bytes 393224 | tf_op jit(solution)/shard_map/ppermute | solution.py:427
  30.7 0.5 collective-permute-start.7
  31.2 1.2 %collective-permute-start.8 = (f32[256,128]{1,0:T(8,128)S(1)}, f32[256,128]{1,0:T(8,128)S(1)}, u32[]{:S(2)}, u32[]{:S(2)}) collective-permute-start(f32[256,128]{1,0:T(8,128)S(1)} %get-tuple-element.104), channel_id=1, source_target_pairs={{0,6},{1,7},{2,4},{3,5},{4,2},{5,3},{6,0},{7,1},{8,14},{9,15},{10,... | collective-permute-start | bytes 393224 | tf_op jit(solution)/shard_map/ppermute | solution.py:427
  32.4 1.5 %collective-permute-done.6.c1 = f32[256,128]{1,0:T(8,128)S(1)} collective-permute-done((f32[256,128]{1,0:T(8,128)S(1)}, f32[256,128]{1,0:T(8,128)S(1)}, u32[]{:S(2)}, u32[]{:S(2)}) %collective-permute-start.6) | collective-permute-done | bytes 131104 | tf_op jit(solution)/shard_map/ppermute | solution.py:427
  33.9 0.9 %collective-permute-done.7.c2 = f32[256,128]{1,0:T(8,128)S(1)} collective-permute-done((f32[256,128]{1,0:T(8,128)S(1)}, f32[256,128]{1,0:T(8,128)S(1)}, u32[]{:S(2)}, u32[]{:S(2)}) %collective-permute-start.7) | collective-permute-done | bytes 131104 | tf_op jit(solution)/shard_map/ppermute | solution.py:427
  34.8 2.9 %collective-permute-done.8.c3 = f32[256,128]{1,0:T(8,128)S(1)} collective-permute-done((f32[256,128]{1,0:T(8,128)S(1)}, f32[256,128]{1,0:T(8,128)S(1)}, u32[]{:S(2)}, u32[]{:S(2)}) %collective-permute-start.8) | collective-permute-done | bytes 131104 | tf_op jit(solution)/shard_map/ppermute | solution.py:427
  37.7 3.3 %shard_map.99 = (f32[272,128]{1,0:T(8,128)S(1)}, f32[272,128]{1,0:T(8,128)S(1)}, f32[272,128]{1,0:T(8,128)S(1)}, f32[272,128]{1,0:T(8,128)S(1)}, f32[1032,128]{1...) custom-call(s32[1,2]{1,0:T(1,128)S(1)} %copy-done.4, ...), custom_call_target="tpu_custom_call" | custom-call | flops 268435456 | bytes 11853824 | tf_op jit(solution)/shard_map/pallas_call | solution.py:390
  41.0 0.1 collective-permute-start.10
  41.0 1.4 %collective-permute-start.11 = (f32[272,128]{1,0:T(8,128)S(1)}, f32[272,128]{1,0:T(8,128)S(1)}, u32[]{:S(2)}, u32[]{:S(2)}) collective-permute-start(f32[272,128]{1,0:T(8,128)S(1)} %get-tuple-element.114), channel_id=1, source_target_pairs={{0,4},{1,5},{2,6},{3,7},{4,0},{5,1},{6,2},{7,3},{8,12},{9,13},{10,... | collective-permute-start | bytes 417800 | tf_op jit(solution)/shard_map/ppermute | solution.py:427
  42.4 1.2 %collective-permute-start.12 = (f32[272,128]{1,0:T(8,128)S(1)}, f32[272,128]{1,0:T(8,128)S(1)}, u32[]{:S(2)}, u32[]{:S(2)}) collective-permute-start(f32[272,128]{1,0:T(8,128)S(1)} %get-tuple-element.115), channel_id=1, source_target_pairs={{0,6},{1,7},{2,4},{3,5},{4,2},{5,3},{6,0},{7,1},{8,14},{9,15},{10,... | collective-permute-start | bytes 417800 | tf_op jit(solution)/shard_map/ppermute | solution.py:427
  43.7 3.1 %shard_map.100 = (bf16[256,2048]{1,0:T(8,128)(2,1)}, f32[256,1024]{1,0:T(8,128)S(1)}, f32[256,1024]{1,0:T(8,128)S(1)}) custom-call(s32[1,2]{1,0:T(1,128)S(1)} %copy-done.4, bf16[256,2048]{1,0:T(8,128)(2,1)S(1)} %bitcast.21, bf16[256,2048]{1,0:T(8,128)(2,1)S(1)} %bitcast.9, bf16[256,2048]{1,0:T(8,128)(2,1)S(1)} %bitcast.15, ...), custom_call_target="tpu_custom_call" | custom-call | flops 872415232 | bytes 7077888 | tf_op jit(solution)/shard_map/pallas_call | solution.py:390
  46.8 1.6 %collective-permute-done.12.c3 = f32[272,128]{1,0:T(8,128)S(1)} collective-permute-done((f32[272,128]{1,0:T(8,128)S(1)}, f32[272,128]{1,0:T(8,128)S(1)}, u32[]{:S(2)}, u32[]{:S(2)}) %collective-permute-start.12) | collective-permute-done | bytes 139296 | tf_op jit(solution)/shard_map/ppermute | solution.py:427
  48.4 0.6 shard_map.101
  49.0 3.4 %collective-permute-start.14 = (f32[272,128]{1,0:T(8,128)S(1)}, f32[272,128]{1,0:T(8,128)S(1)}, u32[]{:S(2)}, u32[]{:S(2)}) collective-permute-start(f32[272,128]{1,0:T(8,128)S(1)} %get-tuple-element.126), channel_id=1, source_target_pairs={{0,16},{1,17},{2,18},{3,19},{4,20},{5,21},{6,22},{7,23},{8,24},{9,... | collective-permute-start | bytes 417800 | tf_op jit(solution)/shard_map/ppermute | solution.py:433
  52.4 0.2 collective-permute-start.13
  52.5 5.9 %collective-permute-done.14.refs_1_ = f32[272,128]{1,0:T(8,128)S(1)} collective-permute-done((f32[272,128]{1,0:T(8,128)S(1)}, f32[272,128]{1,0:T(8,128)S(1)}, u32[]{:S(2)}, u32[]{:S(2)}) %collective-permute-start.14) | collective-permute-done | bytes 139296 | tf_op jit(solution)/shard_map/ppermute | solution.py:433
  58.5 2.9 %collective-permute-start.15 = (f32[384,1024]{1,0:T(8,128)S(1)}, f32[384,1024]{1,0:T(8,128)S(1)}, u32[]{:S(2)}, u32[]{:S(2)}) collective-permute-start(f32[384,1024]{1,0:T(8,128)S(1)} %get-tuple-element.127), channel_id=1, source_target_pairs={{0,1},{1,0},{2,3},{3,2},{4,5},{5,4},{6,7},{7,6},{8,9},{9,8},{10,11... | collective-permute-start | bytes 4718600 | tf_op jit(solution)/shard_map/ppermute | solution.py:423
  61.3 0.7 shard_map.102
  62.1 0.7 collective-permute-start.16
  62.8 1.1 %collective-permute-start.17 = (f32[256,128]{1,0:T(8,128)S(1)}, f32[256,128]{1,0:T(8,128)S(1)}, u32[]{:S(2)}, u32[]{:S(2)}) collective-permute-start(f32[256,128]{1,0:T(8,128)S(1)} %get-tuple-element.133), channel_id=1, source_target_pairs={{0,4},{1,5},{2,6},{3,7},{4,0},{5,1},{6,2},{7,3},{8,12},{9,13},{10,... | collective-permute-start | bytes 393224 | tf_op jit(solution)/shard_map/ppermute | solution.py:427
  63.9 0.9 %collective-permute-start.18 = (f32[256,128]{1,0:T(8,128)S(1)}, f32[256,128]{1,0:T(8,128)S(1)}, u32[]{:S(2)}, u32[]{:S(2)}) collective-permute-start(f32[256,128]{1,0:T(8,128)S(1)} %get-tuple-element.134), channel_id=1, source_target_pairs={{0,6},{1,7},{2,4},{3,5},{4,2},{5,3},{6,0},{7,1},{8,14},{9,15},{10,... | collective-permute-start | bytes 393224 | tf_op jit(solution)/shard_map/ppermute | solution.py:427
  64.8 1.9 %collective-permute-start.19 = (f32[8,128]{1,0:T(8,128)S(1)}, f32[8,128]{1,0:T(8,128)S(1)}, u32[]{:S(2)}, u32[]{:S(2)}) collective-permute-start(f32[8,128]{1,0:T(8,128)S(1)} %get-tuple-element.146.refs_2_), channel_id=1, source_target_pairs={{0,8},{1,9},{2,10},{3,11},{4,12},{5,13},{6,14},{7,15},{8,16},{9,17... | collective-permute-start | bytes 12296 | tf_op jit(solution)/shard_map/ppermute | solution.py:433
  66.7 3.1 %shard_map.103 = (bf16[256,2048]{1,0:T(8,128)(2,1)}, f32[256,1024]{1,0:T(8,128)S(1)}, f32[256,1024]{1,0:T(8,128)S(1)}) custom-call(s32[1,2]{1,0:T(1,128)S(1)} %copy-done.4, bf16[256,2048]{1,0:T(8,128)(2,1)S(1)} %bitcast.22, bf16[256,2048]{1,0:T(8,128)(2,1)S(1)} %bitcast.10, bf16[256,2048]{1,0:T(8,128)(2,1)S(1)} %bitcast.16, ...), custom_call_target="tpu_custom_call", output_to_operand_aliasing={{0}: (5, {})} | custom-call | flops 872415232 | bytes 8912896 | tf_op jit(solution)/shard_map/pallas_call | solution.py:390
  69.8 0.7 collective-permute-done.18.c3
  70.5 0.7 shard_map.104
  71.2 1.1 %collective-permute-start.20 = (f32[1032,128]{1,0:T(8,128)S(1)}, f32[1032,128]{1,0:T(8,128)S(1)}, u32[]{:S(2)}, u32[]{:S(2)}) collective-permute-start(f32[1032,128]{1,0:T(8,128)S(1)} %get-tuple-element.147), channel_id=1, source_target_pairs={{0,1},{1,0},{2,3},{3,2},{4,5},{5,4},{6,7},{7,6},{8,9},{9,8},{10,11... | collective-permute-start | bytes 1585160 | tf_op jit(solution)/shard_map/ppermute | solution.py:423
  72.3 2.0 %shard_map.105 = (bf16[256,2048]{1,0:T(8,128)(2,1)}, bf16[256,2048]{1,0:T(8,128)(2,1)}) custom-call(s32[1,2]{1,0:T(1,128)S(1)} %copy-done.4, bf16[256,2048]{1,0:T(8,128)(2,1)S(1)} %bitcast.11, bf16[256,2048]{1,0:T(8,128)(2,1)S(1)} %bitcast.17, f32[256,1024]{1,0:T(8,128)S(1)} %get-tuple-element.120.key_part, f32[256,1024]{1,0:T(8,128)S(1)} %get-tuple-element.121.value_part, ...), custom_call_target="tpu_custom_call" | custom-call | flops 134217728 | bytes 6553600 | tf_op jit(solution)/shard_map/pallas_call | solution.py:390
  74.4 2.1 %shard_map.106 = (bf16[256,2048]{1,0:T(8,128)(2,1)}, bf16[256,2048]{1,0:T(8,128)(2,1)}, f32[16,128]{1,0:T(8,128)}) custom-call(s32[1,2]{1,0:T(1,128)S(1)} %copy-done.4, bf16[256,2048]{1,0:T(8,128)(2,1)S(1)} %bitcast.12, bf16[256,2048]{1,0:T(8,128)(2,1)S(1)} %bitcast.18, ...), custom_call_target="tpu_custom_call", output_to_operand_aliasing={{0}: (7, {}), {1}: (8, {})} | custom-call | flops 134217728 | bytes 8929280 | tf_op jit(solution)/shard_map/pallas_call | solution.py:390
  (20 shorter events, 0.0 us)
Async XLA Ops:
  0.6 8.2 %copy-start.1 = (bf16[1,256,2048]{2,1,0:T(8,128)(2,1)S(1)}, bf16[1,256,2048]{2,1,0:T(8,128)(2,1)}, u32[]{:S(2)}) copy-start(bf16[1,256,2048]{2,1,0:T(8,128)(2,1)} %param.8) | copy-start | bytes 3145732
  0.6 8.1 %copy-start = (bf16[1,256,2048]{2,1,0:T(8,128)(2,1)S(1)}, bf16[1,256,2048]{2,1,0:T(8,128)(2,1)}, u32[]{:S(2)}) copy-start(bf16[1,256,2048]{2,1,0:T(8,128)(2,1)} %param.7) | copy-start | bytes 3145732
  0.7 8.1 %copy-start.3 = (bf16[1,256,2048]{2,1,0:T(8,128)(2,1)S(1)}, bf16[1,256,2048]{2,1,0:T(8,128)(2,1)}, u32[]{:S(2)}) copy-start(bf16[1,256,2048]{2,1,0:T(8,128)(2,1)} %param.9) | copy-start | bytes 3145732
  0.7 8.1 %copy-start.2 = (bf16[1,256,2048]{2,1,0:T(8,128)(2,1)S(1)}, bf16[1,256,2048]{2,1,0:T(8,128)(2,1)}, u32[]{:S(2)}) copy-start(bf16[1,256,2048]{2,1,0:T(8,128)(2,1)} %param.6) | copy-start | bytes 3145732
  2.5 2.0 %collective-permute-start = (f32[1032,128]{1,0:T(8,128)S(1)}, f32[1032,128]{1,0:T(8,128)S(1)}, u32[]{:S(2)}, u32[]{:S(2)}) collective-permute-start(f32[1032,128]{1,0:T(8,128)S(1)} %get-tuple-element.81), channel_id=1, source_target_pairs={{0,1},{1,0},{2,3},{3,2},{4,5},{5,4},{6,7},{7,6},{8,9},{9,8},{10,11... | collective-permute-start | bytes 1585160 | tf_op jit(solution)/shard_map/ppermute | solution.py:423
  2.6 0.7 copy-start.4
  4.1 33.6 %copy-start.5 = (f32[16,128]{1,0:T(8,128)S(1)}, f32[16,128]{1,0:T(8,128)}, u32[]{:S(2)}) copy-start(f32[16,128]{1,0:T(8,128)} %gain.1) | copy-start | bytes 24580
  5.1 7.3 %collective-permute-start.1 = (f32[264,128]{1,0:T(8,128)S(1)}, f32[264,128]{1,0:T(8,128)S(1)}, u32[]{:S(2)}, u32[]{:S(2)}) collective-permute-start(f32[264,128]{1,0:T(8,128)S(1)} %get-tuple-element.89), channel_id=1, source_target_pairs={{0,2},{1,3},{2,0},{3,1},{4,6},{5,7},{6,4},{7,5},{8,10},{9,11},{10,... | collective-permute-start | bytes 405512 | tf_op jit(solution)/shard_map/ppermute | solution.py:427
  7.5 4.8 %collective-permute-start.2 = (f32[264,128]{1,0:T(8,128)S(1)}, f32[264,128]{1,0:T(8,128)S(1)}, u32[]{:S(2)}, u32[]{:S(2)}) collective-permute-start(f32[264,128]{1,0:T(8,128)S(1)} %get-tuple-element.90), channel_id=1, source_target_pairs={{0,4},{1,5},{2,6},{3,7},{4,0},{5,1},{6,2},{7,3},{8,12},{9,13},{10,... | collective-permute-start | bytes 405512 | tf_op jit(solution)/shard_map/ppermute | solution.py:427
  8.8 6.1 %collective-permute-start.3 = (f32[264,128]{1,0:T(8,128)S(1)}, f32[264,128]{1,0:T(8,128)S(1)}, u32[]{:S(2)}, u32[]{:S(2)}) collective-permute-start(f32[264,128]{1,0:T(8,128)S(1)} %get-tuple-element.91), channel_id=1, source_target_pairs={{0,6},{1,7},{2,4},{3,5},{4,2},{5,3},{6,0},{7,1},{8,14},{9,15},{10,... | collective-permute-start | bytes 405512 | tf_op jit(solution)/shard_map/ppermute | solution.py:427
  15.5 22.2 %collective-permute-start.9 = (f32[768,1024]{1,0:T(8,128)S(1)}, f32[768,1024]{1,0:T(8,128)S(1)}, u32[]{:S(2)}, u32[]{:S(2)}) collective-permute-start(f32[768,1024]{1,0:T(8,128)S(1)} %get-tuple-element.110), channel_id=1, source_target_pairs={{0,1},{1,0},{2,3},{3,2},{4,5},{5,4},{6,7},{7,6},{8,9},{9,8},{10,11... | collective-permute-start | bytes 9437192 | tf_op jit(solution)/shard_map/ppermute | solution.py:423
  17.1 11.9 %collective-permute-start.5 = (f32[264,128]{1,0:T(8,128)S(1)}, f32[264,128]{1,0:T(8,128)S(1)}, u32[]{:S(2)}, u32[]{:S(2)}) collective-permute-start(f32[264,128]{1,0:T(8,128)S(1)} %shard_map.97), channel_id=1, source_target_pairs={{0,16},{1,17},{2,18},{3,19},{4,20},{5,21},{6,22},{7,23},{8,24},{9,... | collective-permute-start | bytes 405512 | tf_op jit(solution)/shard_map/ppermute | solution.py:433
  19.4 9.5 %collective-permute-start.4 = (f32[264,128]{1,0:T(8,128)S(1)}, f32[264,128]{1,0:T(8,128)S(1)}, u32[]{:S(2)}, u32[]{:S(2)}) collective-permute-start(f32[264,128]{1,0:T(8,128)S(1)} %shard_map.97), channel_id=1, source_target_pairs={{0,8},{1,9},{2,10},{3,11},{4,12},{5,13},{6,14},{7,15},{8,16},{9,17... | collective-permute-start | bytes 405512 | tf_op jit(solution)/shard_map/ppermute | solution.py:433
  29.7 4.2 %collective-permute-start.6 = (f32[256,128]{1,0:T(8,128)S(1)}, f32[256,128]{1,0:T(8,128)S(1)}, u32[]{:S(2)}, u32[]{:S(2)}) collective-permute-start(f32[256,128]{1,0:T(8,128)S(1)} %get-tuple-element.102), channel_id=1, source_target_pairs={{0,2},{1,3},{2,0},{3,1},{4,6},{5,7},{6,4},{7,5},{8,10},{9,11},{10,... | collective-permute-start | bytes 393224 | tf_op jit(solution)/shard_map/ppermute | solution.py:427
  30.7 4.1 %collective-permute-start.7 = (f32[256,128]{1,0:T(8,128)S(1)}, f32[256,128]{1,0:T(8,128)S(1)}, u32[]{:S(2)}, u32[]{:S(2)}) collective-permute-start(f32[256,128]{1,0:T(8,128)S(1)} %get-tuple-element.103), channel_id=1, source_target_pairs={{0,4},{1,5},{2,6},{3,7},{4,0},{5,1},{6,2},{7,3},{8,12},{9,13},{10,... | collective-permute-start | bytes 393224 | tf_op jit(solution)/shard_map/ppermute | solution.py:427
  31.2 6.4 %collective-permute-start.8 = (f32[256,128]{1,0:T(8,128)S(1)}, f32[256,128]{1,0:T(8,128)S(1)}, u32[]{:S(2)}, u32[]{:S(2)}) collective-permute-start(f32[256,128]{1,0:T(8,128)S(1)} %get-tuple-element.104), channel_id=1, source_target_pairs={{0,6},{1,7},{2,4},{3,5},{4,2},{5,3},{6,0},{7,1},{8,14},{9,15},{10,... | collective-permute-start | bytes 393224 | tf_op jit(solution)/shard_map/ppermute | solution.py:427
  41.0 5.8 %collective-permute-start.10 = (f32[272,128]{1,0:T(8,128)S(1)}, f32[272,128]{1,0:T(8,128)S(1)}, u32[]{:S(2)}, u32[]{:S(2)}) collective-permute-start(f32[272,128]{1,0:T(8,128)S(1)} %get-tuple-element.113), channel_id=1, source_target_pairs={{0,2},{1,3},{2,0},{3,1},{4,6},{5,7},{6,4},{7,5},{8,10},{9,11},{10,... | collective-permute-start | bytes 417800 | tf_op jit(solution)/shard_map/ppermute | solution.py:427
  41.0 5.7 %collective-permute-start.11 = (f32[272,128]{1,0:T(8,128)S(1)}, f32[272,128]{1,0:T(8,128)S(1)}, u32[]{:S(2)}, u32[]{:S(2)}) collective-permute-start(f32[272,128]{1,0:T(8,128)S(1)} %get-tuple-element.114), channel_id=1, source_target_pairs={{0,4},{1,5},{2,6},{3,7},{4,0},{5,1},{6,2},{7,3},{8,12},{9,13},{10,... | collective-permute-start | bytes 417800 | tf_op jit(solution)/shard_map/ppermute | solution.py:427
  42.4 6.0 %collective-permute-start.12 = (f32[272,128]{1,0:T(8,128)S(1)}, f32[272,128]{1,0:T(8,128)S(1)}, u32[]{:S(2)}, u32[]{:S(2)}) collective-permute-start(f32[272,128]{1,0:T(8,128)S(1)} %get-tuple-element.115), channel_id=1, source_target_pairs={{0,6},{1,7},{2,4},{3,5},{4,2},{5,3},{6,0},{7,1},{8,14},{9,15},{10,... | collective-permute-start | bytes 417800 | tf_op jit(solution)/shard_map/ppermute | solution.py:427
  49.0 9.5 %collective-permute-start.14 = (f32[272,128]{1,0:T(8,128)S(1)}, f32[272,128]{1,0:T(8,128)S(1)}, u32[]{:S(2)}, u32[]{:S(2)}) collective-permute-start(f32[272,128]{1,0:T(8,128)S(1)} %get-tuple-element.126), channel_id=1, source_target_pairs={{0,16},{1,17},{2,18},{3,19},{4,20},{5,21},{6,22},{7,23},{8,24},{9,... | collective-permute-start | bytes 417800 | tf_op jit(solution)/shard_map/ppermute | solution.py:433
  52.4 6.1 %collective-permute-start.13 = (f32[272,128]{1,0:T(8,128)S(1)}, f32[272,128]{1,0:T(8,128)S(1)}, u32[]{:S(2)}, u32[]{:S(2)}) collective-permute-start(f32[272,128]{1,0:T(8,128)S(1)} %get-tuple-element.126), channel_id=1, source_target_pairs={{0,24},{1,25},{2,26},{3,27},{4,28},{5,29},{6,30},{7,31},{8,0},{9,1... | collective-permute-start | bytes 417800 | tf_op jit(solution)/shard_map/ppermute | solution.py:433
  58.5 8.3 %collective-permute-start.15 = (f32[384,1024]{1,0:T(8,128)S(1)}, f32[384,1024]{1,0:T(8,128)S(1)}, u32[]{:S(2)}, u32[]{:S(2)}) collective-permute-start(f32[384,1024]{1,0:T(8,128)S(1)} %get-tuple-element.127), channel_id=1, source_target_pairs={{0,1},{1,0},{2,3},{3,2},{4,5},{5,4},{6,7},{7,6},{8,9},{9,8},{10,11... | collective-permute-start | bytes 4718600 | tf_op jit(solution)/shard_map/ppermute | solution.py:423
  62.1 7.7 %collective-permute-start.16 = (f32[256,128]{1,0:T(8,128)S(1)}, f32[256,128]{1,0:T(8,128)S(1)}, u32[]{:S(2)}, u32[]{:S(2)}) collective-permute-start(f32[256,128]{1,0:T(8,128)S(1)} %get-tuple-element.132), channel_id=1, source_target_pairs={{0,2},{1,3},{2,0},{3,1},{4,6},{5,7},{6,4},{7,5},{8,10},{9,11},{10,... | collective-permute-start | bytes 393224 | tf_op jit(solution)/shard_map/ppermute | solution.py:427
  62.8 7.0 %collective-permute-start.17 = (f32[256,128]{1,0:T(8,128)S(1)}, f32[256,128]{1,0:T(8,128)S(1)}, u32[]{:S(2)}, u32[]{:S(2)}) collective-permute-start(f32[256,128]{1,0:T(8,128)S(1)} %get-tuple-element.133), channel_id=1, source_target_pairs={{0,4},{1,5},{2,6},{3,7},{4,0},{5,1},{6,2},{7,3},{8,12},{9,13},{10,... | collective-permute-start | bytes 393224 | tf_op jit(solution)/shard_map/ppermute | solution.py:427
  63.9 6.6 %collective-permute-start.18 = (f32[256,128]{1,0:T(8,128)S(1)}, f32[256,128]{1,0:T(8,128)S(1)}, u32[]{:S(2)}, u32[]{:S(2)}) collective-permute-start(f32[256,128]{1,0:T(8,128)S(1)} %get-tuple-element.134), channel_id=1, source_target_pairs={{0,6},{1,7},{2,4},{3,5},{4,2},{5,3},{6,0},{7,1},{8,14},{9,15},{10,... | collective-permute-start | bytes 393224 | tf_op jit(solution)/shard_map/ppermute | solution.py:427
  64.8 5.7 %collective-permute-start.19 = (f32[8,128]{1,0:T(8,128)S(1)}, f32[8,128]{1,0:T(8,128)S(1)}, u32[]{:S(2)}, u32[]{:S(2)}) collective-permute-start(f32[8,128]{1,0:T(8,128)S(1)} %get-tuple-element.146.refs_2_), channel_id=1, source_target_pairs={{0,8},{1,9},{2,10},{3,11},{4,12},{5,13},{6,14},{7,15},{8,16},{9,17... | collective-permute-start | bytes 12296 | tf_op jit(solution)/shard_map/ppermute | solution.py:433
  71.2 3.1 %collective-permute-start.20 = (f32[1032,128]{1,0:T(8,128)S(1)}, f32[1032,128]{1,0:T(8,128)S(1)}, u32[]{:S(2)}, u32[]{:S(2)}) collective-permute-start(f32[1032,128]{1,0:T(8,128)S(1)} %get-tuple-element.147), channel_id=1, source_target_pairs={{0,1},{1,0},{2,3},{3,2},{4,5},{5,4},{6,7},{7,6},{8,9},{9,8},{10,11... | collective-permute-start | bytes 1585160 | tf_op jit(solution)/shard_map/ppermute | solution.py:423
